TPU v7x, 32 devices: a whole 2x2x4 slice. The times are simulated.
32 devices in a mesh: shape: 2 (over x), query: 16 (over z, y, core).
Axes of the slice: x: 2, y: 2, z: 4, core: 2. Of those that a mesh axis runs over, the one named last changes fastest.
Arguments:
- latents: bfloat16 [512, 1024], P(('shape', 'query')), parts along dimension 0, may hold values from -6 to 6
- gain_self: float32 [1024], replicated, may hold values from 1.5 to 4, as said below
- w_qkv: bfloat16 [3, 1024, 1024], P(None, 'query'), may hold values from -0.1875 to 0.1875
- w_out: bfloat16 [1024, 1024], P('query'), may hold values from -0.1875 to 0.1875
- gain_cross: float32 [1024], replicated, may hold values from 1.5 to 4, as said below
- w_kv: bfloat16 [2, 1024, 1024], replicated, may hold values from -0.1875 to 0.1875
- w_embed: bfloat16 [51, 1024], replicated, may hold values from -0.875 to 0.875
- gain_point: float32 [1024], replicated, may hold values from 1.5 to 4, as said below
- w_query: bfloat16 [1024, 1024], replicated, may hold values from -0.1875 to 0.1875
- w_back: bfloat16 [1024, 1024], replicated, may hold values from -0.1875 to 0.1875
- gain_head: float32 [1024], replicated, may hold values from 0.5 to 1.5
- w_hidden: bfloat16 [1024, 1024], replicated, may hold values from -0.1875 to 0.1875
- w_sdf: bfloat16 [1024], replicated, may hold values from -0.1875 to 0.1875
Outputs:
- decoded: bfloat16 [512, 1024], P(('shape', 'query')), parts along dimension 0
- sdf: float32 [32768], P(('shape', 'query')), parts along dimension 0
There are 2 independent parts, one for each index of `shape`. A program takes and returns all parts, laid end to end along the dimension named above; an argument that names none is the same for every part. Nothing has to cross between parts.
Inputs may be any that keep to these rules, and one draw needn't show every extreme that they name: `gain_self`: per-channel norm gains. `gain_cross`: per-channel norm gains. `gain_point`: per-channel norm gains.
All inputs are finite; a program needn't handle non-finite values.
Results may differ from a plain program's by a relative error of at most 0.023.
The roundings to bfloat16 on the way count: a program that leaves them out, or rounds other values in their place, can miss the bound.
Values may be sent and summed in bfloat16 or wider, within the bound.
No kernel may reach another device: no remote copies, remote signals or barrier semaphores. Data moves between devices by JAX's collectives and lax.ppermute only.
A program may use at most 128 MiB of HBM per device.

v0:
```python
import math

import jax
import jax.numpy as jnp
from jax import lax
from jax.sharding import PartitionSpec as P

HEADS = 16
FREQS = 8
GRID = 512
PTS_DEV = 1024


def norm_rows(values, gain):
    center = jnp.mean(values, axis=-1, keepdims=True)
    centred = values - center
    spread = jnp.mean(centred * centred, axis=-1, keepdims=True)
    return centred * lax.rsqrt(spread + 1e-05) * gain


def attend(queries, keys, values):
    row_count, features = queries.shape
    key_count = keys.shape[0]
    head_dim = features // HEADS
    group_count = HEADS // 4
    head_queries = queries.reshape(row_count, group_count, 4, head_dim).transpose(1, 0, 2, 3)
    head_keys = keys.reshape(key_count, group_count, 4, head_dim).transpose(1, 0, 2, 3)
    head_values = values.reshape(key_count, group_count, 4, head_dim).transpose(1, 0, 2, 3)
    scaling = 1.0 / math.sqrt(head_dim)

    def per_group(block):
        group_query, group_keys, group_values = block
        scores = (
            jnp.einsum("rge,nge->grn", group_query, group_keys, preferred_element_type=jnp.float32)
            * scaling
        )
        highest = jnp.max(scores, axis=-1, keepdims=True)
        powers = jnp.exp(scores - highest)
        total = jnp.sum(powers, axis=-1, keepdims=True)
        weights = (powers / total).astype(jnp.bfloat16)
        blended = jnp.einsum(
            "grn,nge->rge", weights, group_values, preferred_element_type=jnp.float32
        )
        return blended.astype(jnp.bfloat16)

    result = lax.map(per_group, (head_queries, head_keys, head_values))
    return result.transpose(1, 0, 2, 3).reshape(row_count, features)


def point_features(numbers):
    cell_i = numbers // (GRID * GRID)
    cell_j = numbers // GRID % GRID
    cell_k = numbers % GRID
    cells = jnp.stack([cell_i, cell_j, cell_k], axis=1).astype(jnp.float32)
    coords = (2.0 * cells + 1.0) / GRID - 1.0
    freqs = 2.0 ** jnp.arange(FREQS, dtype=jnp.float32) * math.pi
    angles = (coords[:, :, None] * freqs[None, None, :]).reshape(numbers.shape[0], 3 * FREQS)
    return jnp.concatenate([coords, jnp.sin(angles), jnp.cos(angles)], axis=1).astype(jnp.bfloat16)


def shards(
    latents,
    gain_self,
    w_qkv,
    w_out,
    gain_cross,
    w_kv,
    w_embed,
    gain_point,
    w_query,
    w_back,
    gain_head,
    w_hidden,
    w_sdf,
):
    inputs = latents.astype(jnp.float32)
    normed = norm_rows(inputs, gain_self).astype(jnp.bfloat16)
    columns = normed
    qkv = jnp.einsum(
        "rd,sdc->src",
        columns,
        lax.all_gather(w_qkv, "query", axis=1, tiled=True),
        preferred_element_type=jnp.float32,
    ).astype(jnp.bfloat16)
    self_keys, self_values = (
        lax.all_gather(qkv[1], "query", axis=0, tiled=True),
        lax.all_gather(qkv[2], "query", axis=0, tiled=True),
    )
    attended = attend(qkv[0], self_keys, self_values)
    columns = attended
    update = jnp.dot(
        columns,
        lax.all_gather(w_out, "query", axis=0, tiled=True),
        preferred_element_type=jnp.float32,
    )
    decoded = (inputs + update).astype(jnp.bfloat16)
    normed_two = norm_rows(decoded.astype(jnp.float32), gain_cross).astype(jnp.bfloat16)
    stacked = jnp.einsum(
        "rd,sdc->src",
        lax.all_gather(normed_two, "query", axis=0, tiled=True),
        w_kv,
        preferred_element_type=jnp.float32,
    ).astype(jnp.bfloat16)
    cross_keys, cross_values = (stacked[0], stacked[1])
    numbers = lax.axis_index("query") * PTS_DEV + jnp.arange(PTS_DEV, dtype=jnp.int32)
    features = point_features(numbers)
    embedded = jnp.dot(features, w_embed, preferred_element_type=jnp.float32)
    point_normed = norm_rows(embedded, gain_point).astype(jnp.bfloat16)
    point_query = jnp.dot(point_normed, w_query, preferred_element_type=jnp.float32).astype(
        jnp.bfloat16
    )
    crossed = attend(point_query, cross_keys, cross_values)
    joined = embedded + jnp.dot(crossed, w_back, preferred_element_type=jnp.float32)
    head_in = norm_rows(joined, gain_head).astype(jnp.bfloat16)
    hidden = jax.nn.gelu(jnp.dot(head_in, w_hidden, preferred_element_type=jnp.float32)).astype(
        jnp.bfloat16
    )
    sdf = jnp.dot(hidden, w_sdf, preferred_element_type=jnp.float32)
    return (decoded, sdf)


def solution(mesh):
    return jax.shard_map(
        shards,
        mesh=mesh,
        in_specs=(
            P(("shape", "query"), None),
            P(),
            P(None, "query", None),
            P("query", None),
            P(),
            P(),
            P(),
            P(),
            P(),
            P(),
            P(),
            P(),
            P(),
        ),
        out_specs=(P(("shape", "query"), None), P(("shape", "query"))),
        check_vma=False,
    )
```

profile of v0, /device:TPU:0, one launch (start us, length us, event | category | flops | bytes accessed | tf_op | source)
XLA Modules:
  0.0 205.0 jit_solution(11181423388560623638)
XLA Ops:
  7.2 0.0 copy-start
  7.2 0.0 all-gather.5.cloned.1.call-start
  7.2 0.7 all-gather.5.cloned.1.call-update
  7.9 0.0 all-gather.7.cloned.1.call-start
  8.0 0.7 all-gather.7.cloned.1.call-update
  8.7 0.1 and_select_fusion
  8.8 0.1 mul.155
  8.9 0.9 convert_reduce_fusion
  9.8 0.9 fusion.95
  10.7 0.7 reshape.253
  11.4 0.4 fusion.89
  11.9 0.0 copy-start.7
  11.9 0.0 copy-start.8
  11.9 1.8 fusion.128
  13.7 0.5 multiply_reduce_fusion.2
  14.2 1.5 copy-done.1
  15.7 0.0 copy-done.8
  15.8 4.0 %fusion.76 = bf16[1024,1024]{0,1:T(8,128)(2,1)} fusion(bf16[1024,1024]{1,0:T(8,128)(2,1)S(1)} %copy-done.7, f32[1024,1024]{0,1:T(8,128)S(1)} %get-tuple-element.92, f32[1024]{0:T(1024)S(1)} %copy-done.8, f32[1024]{0:T(1024)S(1)} %add_rsqrt_fusion.1, f32[1024]{0:T(1024)S(1)} %broadcast_multiply_fusion.1), kind=kOutput, calls=%fused_computation.65 | convolution fusion | flops 2152726528 | bytes 8400896 | tf_op jit(solution)/shard_map/dot_general | solution.py:109
  19.8 55.1 %all-gather.5.cloned.1.call-done = bf16[3,1024,1024]{2,1,0:T(8,128)(2,1)} async-done(((bf16[3,64,1024]{2,1,0:T(8,128)(2,1)}), bf16[3,1024,1024]{2,1,0:T(8,128)(2,1)}) %all-gather.5.cloned.1.call-update) | async-done | bytes 6291472 | tf_op jit(solution)/shard_map/all_gather | solution.py:82
  74.9 3.8 %fusion.78 = bf16[3,16,1024]{2,1,0:T(8,128)(2,1)S(1)} fusion(bf16[3,1024,1024]{2,1,0:T(8,128)(2,1)} %all-gather.5.cloned.1.call-done, bf16[16,1024]{1,0:T(8,128)(2,1)S(1)} %copy-done.3, f32[1024]{0:T(1024)S(1)} %copy-done.5, f32[16]{0:T(128)S(1)} %add_rsqrt_fusion.3, f32[16]{0:T(128)S(1)} %broadcast_multiply_fusion.3), kind=kOutput, calls=%fused_computation.69 | convolution fusion | flops 100794368 | bytes 6426752 | tf_op jit(solution)/shard_map/rd,sdc->src/dot_general | solution.py:79
  78.7 21.0 %all-gather = bf16[1,256,1024]{2,1,0:T(8,128)(2,1)S(1)} all-gather(bf16[1,16,1024]{2,1,0:T(8,128)(2,1)S(1)} %get-tuple-element.86), channel_id=2, replica_groups=mesh['shape'=2,'query'=16] {'query'}, dimensions={1}, use_global_device_ids=true | all-gather | bytes 557056 | tf_op jit(solution)/shard_map/all_gather | solution.py:87
  99.7 1.0 copy.22
  100.7 20.4 %all-gather.1 = bf16[1,256,1024]{2,1,0:T(8,128)(2,1)S(1)} all-gather(bf16[1,16,1024]{2,1,0:T(8,128)(2,1)S(1)} %get-tuple-element.84), channel_id=3, replica_groups=mesh['shape'=2,'query'=16] {'query'}, dimensions={1}, use_global_device_ids=true | all-gather | bytes 557056 | tf_op jit(solution)/shard_map/all_gather | solution.py:86
  121.1 0.2 copy.24
  121.3 0.1 reshape_squeeze.9
  121.4 6.3 %while.20 = (s32[]{:T(128)}, bf16[4,16,4,64]{3,1,2,0:T(8,128)(2,1)S(1)}, bf16[4,256,4,64]{1,3,2,0:T(8,128)(2,1)}, bf16[4,16,4,64]{3,1,2,0:T(8,128)(2,1)S(1)}, bf16[4,256,4,64]{1,3,2,0:T(8,128)(2,1)S(1)}, /*index=5*/s32[]{:T(128)}) while((s32[]{:T(128)}, bf16[4,16,4,64]{3,1,2,0:T(8,128)(2,1)S(1)}, bf16[4,256,4,64]{1,3,2,0:T(8,128)(2,1)}, ...), condition=%wide.region_5.6_spmd, body=%wide.region_2.5_spmd.sunk | while | flops 6410816 | bytes 447813 | solution.py:46
  121.5 0.3 fusion.158
  121.8 1.3 fusion.159
  123.0 0.3 fusion.158
  123.3 1.3 fusion.159
  124.6 0.3 fusion.158
  124.9 1.3 fusion.159
  126.2 0.3 fusion.158
  126.5 1.3 fusion.159
  127.8 0.1 reshape.244
  127.9 0.0 all-gather.7.cloned.1.call-done
  127.9 2.1 %convert_reduce_fusion.1 = (f32[16]{0:T(128)S(1)}, bf16[16,1024]{1,0:T(8,128)(2,1)S(1)}) fusion(bf16[16,1024]{1,0:T(8,128)(2,1)S(1)} %reshape.244, bf16[1024,1024]{1,0:T(8,128)(2,1)} %all-gather.7.cloned.1.call-done, bf16[16,1024]{1,0:T(8,128)(2,1)S(1)} %copy-done.3), kind=kOutput, calls=%fused_computation.87 | convolution fusion | flops 33636336 | bytes 2195520 | tf_op jit(solution)/shard_map/dot_general | solution.py:91
  130.0 0.0 copy-start.4
  130.0 0.2 fusion.98
  130.2 0.0 copy-done.6
  130.2 0.1 fusion.100
  130.3 19.7 %all_gather.19 = bf16[256,1024]{1,0:T(8,128)(2,1)S(1)} all-gather(bf16[16,1024]{1,0:T(8,128)(2,1)S(1)} %fusion.100), channel_id=1, replica_groups=mesh['shape'=2,'query'=16] {'query'}, dimensions={0}, use_global_device_ids=true | all-gather | bytes 557056 | tf_op jit(solution)/shard_map/all_gather | solution.py:100
  150.0 3.5 %fusion.77 = bf16[2,256,1024]{2,1,0:T(8,128)(2,1)S(1)} fusion(bf16[2,1024,1024]{2,1,0:T(8,128)(2,1)} %param.22, bf16[256,1024]{1,0:T(8,128)(2,1)S(1)} %all_gather.19), kind=kOutput, calls=%fused_computation.67 | convolution fusion | flops 1074266112 | bytes 5767168 | tf_op jit(solution)/shard_map/rd,sdc->src/dot_general | solution.py:98
  153.5 0.1 fusion.126
  153.5 1.0 copy.26
  154.5 0.2 copy.27
  154.8 28.6 %while.21 = (s32[]{:T(128)}, bf16[4,1024,4,64]{1,3,2,0:T(8,128)(2,1)}, bf16[4,256,4,64]{1,3,2,0:T(8,128)(2,1)}, bf16[4,1024,4,64]{1,3,2,0:T(8,128)(2,1)}, bf16[4,256,4,64]{1,3,2,0:T(8,128)(2,1)S(1)}, /*index=5*/s32[]{:T(128)}) while((s32[]{:T(128)}, bf16[4,1024,4,64]{1,3,2,0:T(8,128)(2,1)}, bf16[4,256,4,64]{1,3,2,0:T(8,128)(2,1)}, ...), condition=%wide.region_13.14_spmd, body=%wide.region_10.13_spmd.sunk | while | flops 274989312 | bytes 18122820 | solution.py:46
  154.8 1.8 fusion.163
  156.6 3.1 %fusion.164 = (f32[4,1024]{1,0:T(4,128)S(1)}, f32[4,1024,256]{1,2,0:T(8,128)S(1)}) fusion(f32[4,1024,256]{1,2,0:T(8,128)S(1)} %fusion.163), kind=kOutput, calls=%fused_computation.139.clone.1 | output fusion | flops 4194559 | bytes 8404992 | tf_op jit(solution)/shard_map/while/body/eval_jaxpr/sub | solution.py:38
  159.7 2.2 %fusion.165 = bf16[4,1024,4,64]{1,3,2,0:T(8,128)(2,1)} fusion(bf16[4,1024,4,64]{1,3,2,0:T(8,128)(2,1)} %get-tuple-element.188, s32[]{:T(128)} %get-tuple-element.187, f32[4,1024,256]{1,2,0:T(8,128)S(1)} %get-tuple-element.161, f32[4,1024]{1,0:T(4,128)S(1)} %get-tuple-element.162, bf16[4,256,4,64]{1,3,2,0:T(8,128)(2,1)} %get-tuple-element.195), kind=kOutput, calls=%fused_computation.31.clone.1 | convolution fusion | flops 136577024 | bytes 4867072 | tf_op jit(solution)/shard_map/while/body/eval_jaxpr/grn,nge->rge/dot_general | solution.py:41
  161.9 1.8 fusion.163
  163.7 3.1 %fusion.164 = (f32[4,1024]{1,0:T(4,128)S(1)}, f32[4,1024,256]{1,2,0:T(8,128)S(1)}) fusion(f32[4,1024,256]{1,2,0:T(8,128)S(1)} %fusion.163), kind=kOutput, calls=%fused_computation.139.clone.1 | output fusion | flops 4194559 | bytes 8404992 | tf_op jit(solution)/shard_map/while/body/eval_jaxpr/sub | solution.py:38
  166.8 2.2 %fusion.165 = bf16[4,1024,4,64]{1,3,2,0:T(8,128)(2,1)} fusion(bf16[4,1024,4,64]{1,3,2,0:T(8,128)(2,1)} %get-tuple-element.188, s32[]{:T(128)} %get-tuple-element.187, f32[4,1024,256]{1,2,0:T(8,128)S(1)} %get-tuple-element.161, f32[4,1024]{1,0:T(4,128)S(1)} %get-tuple-element.162, bf16[4,256,4,64]{1,3,2,0:T(8,128)(2,1)} %get-tuple-element.195), kind=kOutput, calls=%fused_computation.31.clone.1 | convolution fusion | flops 136577024 | bytes 4867072 | tf_op jit(solution)/shard_map/while/body/eval_jaxpr/grn,nge->rge/dot_general | solution.py:41
  169.1 1.8 fusion.163
  170.9 3.1 %fusion.164 = (f32[4,1024]{1,0:T(4,128)S(1)}, f32[4,1024,256]{1,2,0:T(8,128)S(1)}) fusion(f32[4,1024,256]{1,2,0:T(8,128)S(1)} %fusion.163), kind=kOutput, calls=%fused_computation.139.clone.1 | output fusion | flops 4194559 | bytes 8404992 | tf_op jit(solution)/shard_map/while/body/eval_jaxpr/sub | solution.py:38
  174.0 2.2 %fusion.165 = bf16[4,1024,4,64]{1,3,2,0:T(8,128)(2,1)} fusion(bf16[4,1024,4,64]{1,3,2,0:T(8,128)(2,1)} %get-tuple-element.188, s32[]{:T(128)} %get-tuple-element.187, f32[4,1024,256]{1,2,0:T(8,128)S(1)} %get-tuple-element.161, f32[4,1024]{1,0:T(4,128)S(1)} %get-tuple-element.162, bf16[4,256,4,64]{1,3,2,0:T(8,128)(2,1)} %get-tuple-element.195), kind=kOutput, calls=%fused_computation.31.clone.1 | convolution fusion | flops 136577024 | bytes 4867072 | tf_op jit(solution)/shard_map/while/body/eval_jaxpr/grn,nge->rge/dot_general | solution.py:41
  176.2 1.8 fusion.163
  178.0 3.1 %fusion.164 = (f32[4,1024]{1,0:T(4,128)S(1)}, f32[4,1024,256]{1,2,0:T(8,128)S(1)}) fusion(f32[4,1024,256]{1,2,0:T(8,128)S(1)} %fusion.163), kind=kOutput, calls=%fused_computation.139.clone.1 | output fusion | flops 4194559 | bytes 8404992 | tf_op jit(solution)/shard_map/while/body/eval_jaxpr/sub | solution.py:38
  181.1 2.2 %fusion.165 = bf16[4,1024,4,64]{1,3,2,0:T(8,128)(2,1)} fusion(bf16[4,1024,4,64]{1,3,2,0:T(8,128)(2,1)} %get-tuple-element.188, s32[]{:T(128)} %get-tuple-element.187, f32[4,1024,256]{1,2,0:T(8,128)S(1)} %get-tuple-element.161, f32[4,1024]{1,0:T(4,128)S(1)} %get-tuple-element.162, bf16[4,256,4,64]{1,3,2,0:T(8,128)(2,1)} %get-tuple-element.195), kind=kOutput, calls=%fused_computation.31.clone.1 | convolution fusion | flops 136577024 | bytes 4867072 | tf_op jit(solution)/shard_map/while/body/eval_jaxpr/grn,nge->rge/dot_general | solution.py:41
  183.3 5.2 %fusion.129 = (f32[1024]{0:T(1024)S(1)}, f32[1024,1024]{0,1:T(8,128)S(1)}) fusion(f32[1024,1024]{0,1:T(8,128)} %copy-done.1, bf16[1024,1024]{0,1:T(8,128)(2,1)} %bitcast.28, bf16[1024,1024]{1,0:T(8,128)(2,1)S(1)} %copy-done), kind=kOutput, calls=%fused_computation.143 | convolution fusion | flops 2149579776 | bytes 12587008 | tf_op jit(solution)/shard_map/dot_general | solution.py:113
  188.6 0.0 copy-start.9
  188.6 1.9 copy-done.2
  190.5 0.5 multiply_reduce_fusion.1
  191.0 7.2 %fusion.74 = f32[1,1024]{1,0:T(1,128)} fusion(bf16[1024,1]{0,1:T(2,128)(2,1)S(1)} %reshape.253, bf16[1024,1024]{1,0:T(8,128)(2,1)} %param.28, f32[1024,1024]{0,1:T(8,128)} %copy-done.2, f32[1024]{0:T(1024)S(1)} %copy-done.9, f32[1024]{0:T(1024)S(1)} %add_rsqrt_fusion, f32[1024]{0:T(1024)S(1)} %broadcast_multiply_fusion), kind=kOutput, calls=%fused_computation.63 | convolution fusion | flops 2163212288 | bytes 6309888 | tf_op jit(solution)/shard_map/dot_general | solution.py:118
  (28 shorter events, 0.2 us)
Async XLA Ops:
  7.2 176.2 %copy-start = (bf16[1024,1024]{1,0:T(8,128)(2,1)S(1)}, bf16[1024,1024]{1,0:T(8,128)(2,1)}, u32[]{:S(2)}) copy-start(bf16[1024,1024]{1,0:T(8,128)(2,1)} %param.26) | copy-start | bytes 6291460
  7.2 67.7 %all-gather.5.cloned.1.call-start = ((), (), s32[]{:S(2)}) async-start(), calls=%async_computation | async-start | bytes 6684672 | tf_op jit(solution)/shard_map/all_gather | solution.py:82
  7.9 120.0 %all-gather.7.cloned.1.call-start = ((), (), s32[]{:S(2)}) async-start(), calls=%async_computation.1 | async-start | bytes 2228224 | tf_op jit(solution)/shard_map/all_gather | solution.py:93
  11.9 3.9 %copy-start.7 = (bf16[1024,1024]{1,0:T(8,128)(2,1)S(1)}, bf16[1024,1024]{1,0:T(8,128)(2,1)}, u32[]{:S(2)}) copy-start(bf16[1024,1024]{1,0:T(8,128)(2,1)} %param.25) | copy-start | bytes 6291460
  11.9 3.9 %copy-start.8 = (f32[1024]{0:T(1024)S(1)}, f32[1024]{0:T(1024)}, u32[]{:S(2)}) copy-start(f32[1024]{0:T(1024)} %param.24) | copy-start | bytes 12292
  13.7 2.0 copy-start.1
  15.8 59.1 %copy-start.3 = (bf16[16,1024]{1,0:T(8,128)(2,1)S(1)}, bf16[16,1024]{1,0:T(8,128)(2,1)}, u32[]{:S(2)}) copy-start(bf16[16,1024]{1,0:T(8,128)(2,1)} %param.17) | copy-start | bytes 98308
  15.8 59.1 %copy-start.5 = (f32[1024]{0:T(1024)S(1)}, f32[1024]{0:T(1024)}, u32[]{:S(2)}) copy-start(f32[1024]{0:T(1024)} %param.18) | copy-start | bytes 12292
  99.7 30.6 %copy-start.6 = (f32[1024]{0:T(1024)S(1)}, f32[1024]{0:T(1024)}, u32[]{:S(2)}) copy-start(f32[1024]{0:T(1024)} %param.21) | copy-start | bytes 12292
  130.0 23.5 %copy-start.4 = (bf16[16,1024]{1,0:T(8,128)(2,1)}, bf16[16,1024]{1,0:T(8,128)(2,1)S(1)}, u32[]{:S(2)}) copy-start(bf16[16,1024]{1,0:T(8,128)(2,1)S(1)} %get-tuple-element.90) | copy-start | bytes 98308
  188.6 1.9 copy-start.2
  188.6 2.4 %copy-start.9 = (f32[1024]{0:T(1024)S(1)}, f32[1024]{0:T(1024)}, u32[]{:S(2)}) copy-start(f32[1024]{0:T(1024)} %param.27) | copy-start | bytes 12292
Sparse Core Ops, SparseCore 0:
  10.2 64.6 all-gather.4
  77.1 42.7 all-gather.6
where the time goes:
time: 206 us; the launch traced here: 205 us
  blocking collectives  61.1 us (30%)
  waiting for transfers between devices  56.5 us (27%)
  matrix products  49.7 us (24%)
  other arithmetic  16.2 us (8%)
  between operations  14.3 us (7%)
  local copies, waits for them, and re-layouts  6.99 us (3%)
    all_gather x1, waiting for transfers between devices, shards(): lax.all_gather(w_qkv, 'query', axis=1, tiled=True)  55.1 us
    all_gather x1, blocking collectives, shards(): lax.all_gather(qkv[2], 'query', axis=0, tiled=True)  21 us
    all_gather x1, blocking collectives, shards(): lax.all_gather(qkv[1], 'query', axis=0, tiled=True)  20.4 us
    all_gather x1, blocking collectives, shards(): lax.all_gather(normed_two, 'query', axis=0, tiled=True)  19.7 us
    dot_general x8, matrix products, per_group(): jnp.einsum('grn,nge->rge', weights, group_values, preferred_element_type=...  13.9 us
    sub x4, other arithmetic, per_group(): powers = jnp.exp(scores - highest)  12.5 us
    dot_general x1, matrix products, shards(): sdf = jnp.dot(hidden, w_sdf, preferred_element_type=jnp.float32)  7.18 us
    dot_general x4, matrix products, per_group(): jnp.einsum('rge,nge->grn', group_query, group_keys, preferred_element_typ...  7.12 us
  transfers between devices with their start and end apart: 2, of which 1 were waited for; matrix products, arithmetic and copies ran while one was open for 10% of the time, Pallas kernels for 0%

commit v1 on v0

v1 whole, which is shorter than its diff:
```python
import functools
import math

import jax
import jax.numpy as jnp
from jax import lax
from jax.experimental import pallas as pl
from jax.experimental.pallas import tpu as pltpu
from jax.sharding import PartitionSpec as P

HEADS = 16
FREQS = 8
GRID = 512
HEAD_DIM = 64
SCALE = 1.0 / math.sqrt(HEAD_DIM)
POINT_BLOCK = 256
VMEM_LIMIT = 40 * 1024 * 1024
FEATURE_ROWS = 64


def norm_rows(values, gain):
    center = jnp.mean(values, axis=-1, keepdims=True)
    centred = values - center
    spread = jnp.mean(centred * centred, axis=-1, keepdims=True)
    return centred * lax.rsqrt(spread + 1e-05) * gain


def attend(queries, keys, values):
    row_count, features = queries.shape
    key_count = keys.shape[0]
    head_dim = features // HEADS
    group_count = HEADS // 4
    head_queries = queries.reshape(row_count, group_count, 4, head_dim).transpose(1, 0, 2, 3)
    head_keys = keys.reshape(key_count, group_count, 4, head_dim).transpose(1, 0, 2, 3)
    head_values = values.reshape(key_count, group_count, 4, head_dim).transpose(1, 0, 2, 3)
    scaling = 1.0 / math.sqrt(head_dim)

    def per_group(block):
        group_query, group_keys, group_values = block
        scores = (
            jnp.einsum("rge,nge->grn", group_query, group_keys, preferred_element_type=jnp.float32)
            * scaling
        )
        highest = jnp.max(scores, axis=-1, keepdims=True)
        powers = jnp.exp(scores - highest)
        total = jnp.sum(powers, axis=-1, keepdims=True)
        weights = (powers / total).astype(jnp.bfloat16)
        blended = jnp.einsum(
            "grn,nge->rge", weights, group_values, preferred_element_type=jnp.float32
        )
        return blended.astype(jnp.bfloat16)

    result = lax.map(per_group, (head_queries, head_keys, head_values))
    return result.transpose(1, 0, 2, 3).reshape(row_count, features)


def feature_rows(numbers):
    cell_i = numbers // (GRID * GRID)
    cell_j = numbers // GRID % GRID
    cell_k = numbers % GRID
    cells = jnp.stack([cell_i, cell_j, cell_k], axis=0).astype(jnp.float32)
    coords = (2.0 * cells + 1.0) / GRID - 1.0
    freqs = 2.0 ** jnp.arange(FREQS, dtype=jnp.float32) * math.pi
    angles = (coords[:, None, :] * freqs[None, :, None]).reshape(3 * FREQS, numbers.shape[0])
    return jnp.concatenate([coords, jnp.sin(angles), jnp.cos(angles)], axis=0).astype(jnp.bfloat16)


def any_slice(
    latents, gain_self, w_qkv, w_out, gain_cross, w_kv, w_embed, gain_point, w_query, w_back,
    gain_head, w_hidden, w_sdf, *, points,
):
    inputs = latents.astype(jnp.float32)
    normed = norm_rows(inputs, gain_self).astype(jnp.bfloat16)
    qkv = jnp.einsum(
        "rd,sdc->src",
        normed,
        lax.all_gather(w_qkv, "query", axis=1, tiled=True),
        preferred_element_type=jnp.float32,
    ).astype(jnp.bfloat16)
    self_keys, self_values = (
        lax.all_gather(qkv[1], "query", axis=0, tiled=True),
        lax.all_gather(qkv[2], "query", axis=0, tiled=True),
    )
    attended = attend(qkv[0], self_keys, self_values)
    update = jnp.dot(
        attended,
        lax.all_gather(w_out, "query", axis=0, tiled=True),
        preferred_element_type=jnp.float32,
    )
    decoded = (inputs + update).astype(jnp.bfloat16)
    normed_two = norm_rows(decoded.astype(jnp.float32), gain_cross).astype(jnp.bfloat16)
    stacked = jnp.einsum(
        "rd,sdc->src",
        lax.all_gather(normed_two, "query", axis=0, tiled=True),
        w_kv,
        preferred_element_type=jnp.float32,
    ).astype(jnp.bfloat16)
    numbers = lax.axis_index("query") * points + jnp.arange(points, dtype=jnp.int32)
    features = feature_rows(numbers).T
    embedded = jnp.dot(features, w_embed, preferred_element_type=jnp.float32)
    point_normed = norm_rows(embedded, gain_point).astype(jnp.bfloat16)
    point_query = jnp.dot(point_normed, w_query, preferred_element_type=jnp.float32).astype(
        jnp.bfloat16
    )
    crossed = attend(point_query, stacked[0], stacked[1])
    joined = embedded + jnp.dot(crossed, w_back, preferred_element_type=jnp.float32)
    head_in = norm_rows(joined, gain_head).astype(jnp.bfloat16)
    hidden = jax.nn.gelu(jnp.dot(head_in, w_hidden, preferred_element_type=jnp.float32)).astype(
        jnp.bfloat16
    )
    sdf = jnp.dot(hidden, w_sdf, preferred_element_type=jnp.float32)
    return (decoded, sdf)


def dot_nn(left, right):
    return lax.dot_general(left, right, (((1,), (0,)), ((), ())), preferred_element_type=jnp.float32)


def dot_nt(left, right):
    return lax.dot_general(left, right, (((1,), (1,)), ((), ())), preferred_element_type=jnp.float32)


def dot_tn(left, right):
    return lax.dot_general(left, right, (((0,), (0,)), ((), ())), preferred_element_type=jnp.float32)


def pack_kernel(w_ref, latents_ref, out_ref):
    rows = w_ref.shape[1]
    for target in range(HEADS):
        low = target * HEAD_DIM
        first = 512 * (target % 2)
        beside = [
            latents_ref[:, first + 256 + 64 * part : first + 320 + 64 * part] for part in range(4)
        ]
        pieces = [w_ref[s, :, low : low + HEAD_DIM] for s in range(3)]
        pieces.append(jnp.concatenate(beside, axis=0))
        out_ref[target, :rows, :] = jnp.concatenate(pieces, axis=1)
        out_ref[target, rows:, :] = latents_ref[:, first : first + 256]


def pack(w_qkv, latents):
    rows = w_qkv.shape[1]
    return pl.pallas_call(
        pack_kernel,
        out_shape=jax.ShapeDtypeStruct((HEADS, rows + 16, 256), jnp.bfloat16),
        name="pack",
    )(w_qkv, latents)


def unpack_kernel(received_ref, half_ref):
    rows = half_ref.shape[0]
    parts = [received_ref[:, 64:80, :].reshape(rows, 256)]
    for part in range(4):
        parts.append(received_ref[:, 16 * part : 16 * part + 16, 192:256].reshape(rows, 64))
    half_ref[...] = jnp.concatenate(parts, axis=1)


def unpack(received):
    rows = received.shape[0] * 16
    return pl.pallas_call(
        unpack_kernel,
        out_shape=jax.ShapeDtypeStruct((rows, 512), jnp.bfloat16),
        name="unpack",
    )(received)


def point_kernel(features_ref, w_embed_ref, gain_ref, w_query_ref, out_ref):
    embedded = dot_tn(features_ref[...], w_embed_ref[...])
    normed = norm_rows(embedded, gain_ref[...]).astype(jnp.bfloat16)
    out_ref[...] = dot_nn(normed, w_query_ref[...]).astype(jnp.bfloat16)


def point_queries(features, w_embed, gain, w_query):
    points = features.shape[1]
    width = w_query.shape[1]
    return pl.pallas_call(
        point_kernel,
        grid=(points // POINT_BLOCK,),
        in_specs=[
            pl.BlockSpec((FEATURE_ROWS, POINT_BLOCK), lambda i: (0, i)),
            pl.BlockSpec((FEATURE_ROWS, width), lambda i: (0, 0)),
            pl.BlockSpec((1, width), lambda i: (0, 0)),
            pl.BlockSpec((width, width), lambda i: (0, 0)),
        ],
        out_specs=pl.BlockSpec((POINT_BLOCK, width), lambda i: (i, 0)),
        out_shape=jax.ShapeDtypeStruct((points, width), jnp.bfloat16),
        cost_estimate=pl.CostEstimate(
            flops=2 * points * width * (width + FEATURE_ROWS),
            bytes_accessed=4 * width * width,
            transcendentals=0,
        ),
        name="point_queries",
    )(features, w_embed, gain, w_query)


def self_kernel(core_ref, received_ref, own_ref, other_ref, gain_ref, attended_ref, latents_ref):
    sources = received_ref.shape[0]
    first = core_ref[0] == 0
    own, other = own_ref[...], other_ref[...]
    latents = jnp.concatenate(
        [jnp.where(first, own, other), jnp.where(first, other, own)], axis=1
    )
    latents_ref[...] = latents
    normed = norm_rows(latents.astype(jnp.float32), gain_ref[...]).astype(jnp.bfloat16)
    weights = received_ref[:, :64, :].reshape(sources * 64, 256)
    qkv = dot_nn(normed, weights).astype(jnp.bfloat16)
    queries, keys = qkv[:, :64], qkv[:, 64:128]
    values = qkv[:, 128:192]
    scores = dot_nt(keys, queries) * SCALE
    powers = jnp.exp(scores - jnp.max(scores, axis=0, keepdims=True))
    shares = (powers / jnp.sum(powers, axis=0, keepdims=True)).astype(jnp.bfloat16)
    attended_ref[...] = dot_tn(values, shares).astype(jnp.bfloat16)


def self_attention(core, received, own, other, gain):
    rows = received.shape[0] * 16
    vmem = pl.BlockSpec(memory_space=pltpu.VMEM)
    return pl.pallas_call(
        self_kernel,
        in_specs=[pl.BlockSpec(memory_space=pltpu.SMEM)] + [vmem] * 4,
        out_shape=(
            jax.ShapeDtypeStruct((HEAD_DIM, rows), jnp.bfloat16),
            jax.ShapeDtypeStruct((rows, gain.shape[1]), jnp.bfloat16),
        ),
        name="self_attention",
    )(core, received, own, other, gain)


def tail_kernel(
    first_ref, near_ref, far_ref, out_near_ref, out_far_ref, latents_ref, gain_cross_ref, w_kv_ref,
    queries_ref, features_ref, w_back_ref, w_embed_ref, gain_head_ref, w_hidden_ref, w_sdf_ref,
    decoded_ref, sdf_ref, all_decoded, key_pairs, value_rows, crossed,
):
    width = latents_ref.shape[1]
    update = dot_tn(near_ref[...], out_near_ref[...]) + dot_tn(far_ref[...], out_far_ref[...])
    decoded = (latents_ref[...].astype(jnp.float32) + update).astype(jnp.bfloat16)
    all_decoded[...] = decoded
    decoded_ref[...] = all_decoded[pl.ds(pl.multiple_of(first_ref[0], 16), 16), :]
    normed = norm_rows(decoded.astype(jnp.float32), gain_cross_ref[...]).astype(jnp.bfloat16)
    keys = dot_nn(normed, w_kv_ref[0]).astype(jnp.bfloat16) * SCALE
    key_count = keys.shape[0]
    lane = lax.broadcasted_iota(jnp.int32, (key_count, 128), 1)
    for pair in range(HEADS // 2):
        both = keys[:, 128 * pair : 128 * pair + 128]
        zero = jnp.zeros_like(both)
        key_pairs[pair, :key_count, :] = jnp.where(lane < HEAD_DIM, both, zero)
        key_pairs[pair, key_count:, :] = jnp.where(lane < HEAD_DIM, zero, both)
    values = dot_nn(normed, w_kv_ref[1]).T.astype(jnp.bfloat16)
    for head in range(HEADS):
        value_rows[head, :HEAD_DIM, :] = values[HEAD_DIM * head : HEAD_DIM * head + HEAD_DIM, :]
        value_rows[head, HEAD_DIM:, :] = jnp.ones((16, key_count), jnp.bfloat16)

    for pair in range(HEADS // 2):
        scores = dot_nt(key_pairs[pair], queries_ref[:, 128 * pair : 128 * pair + 128])
        for half in range(2):
            head = 2 * pair + half
            own = scores[half * key_count : half * key_count + key_count, :]
            powers = jnp.exp(own - jnp.max(own, axis=0, keepdims=True)).astype(jnp.bfloat16)
            blended = dot_nn(value_rows[head], powers)
            crossed[HEAD_DIM * head : HEAD_DIM * head + HEAD_DIM, :] = (
                blended[:HEAD_DIM, :] / blended[HEAD_DIM : HEAD_DIM + 1, :]
            ).astype(jnp.bfloat16)

    joined = dot_nn(w_back_ref[...], crossed[...]) + dot_nn(w_embed_ref[...], features_ref[...])
    centred = joined - jnp.sum(joined, axis=0, keepdims=True) * (1.0 / width)
    spread = jnp.sum(centred * centred, axis=0, keepdims=True) * (1.0 / width)
    gain = jnp.concatenate([gain_head_ref[...]] * (joined.shape[1] // 128), axis=1)
    head_in = (centred * lax.rsqrt(spread + 1e-05) * gain).astype(jnp.bfloat16)
    hidden = jax.nn.gelu(dot_nn(w_hidden_ref[...], head_in)).astype(jnp.bfloat16)
    sdf_ref[...] = dot_nn(w_sdf_ref[...], hidden)[:1, :]


def tail(
    first, near, far, out_near, out_far, latents, gain_cross, w_kv, queries, features, w_back,
    w_embed, gain_head, w_hidden, w_sdf,
):
    points, width = queries.shape
    keys = latents.shape[0]
    vmem = pl.BlockSpec(memory_space=pltpu.VMEM)
    return pl.pallas_call(
        tail_kernel,
        in_specs=[pl.BlockSpec(memory_space=pltpu.SMEM)] + [vmem] * 14,
        out_specs=(vmem, vmem),
        out_shape=(
            jax.ShapeDtypeStruct((16, width), jnp.bfloat16),
            jax.ShapeDtypeStruct((1, points), jnp.float32),
        ),
        scratch_shapes=[
            pltpu.VMEM((keys, width), jnp.bfloat16),
            pltpu.VMEM((HEADS // 2, 2 * keys, 128), jnp.bfloat16),
            pltpu.VMEM((HEADS, HEAD_DIM + 16, keys), jnp.bfloat16),
            pltpu.VMEM((width, points), jnp.bfloat16),
        ],
        compiler_params=pltpu.CompilerParams(vmem_limit_bytes=VMEM_LIMIT),
        name="tail",
    )(
        first, near, far, out_near, out_far, latents, gain_cross, w_kv, queries, features, w_back,
        w_embed, gain_head, w_hidden, w_sdf,
    )


def swap(values, bit, count):
    return lax.ppermute(values, "query", [(i, i ^ bit) for i in range(count)])


def after(values, *others):
    return lax.optimization_barrier((values, *others))[0]


def one_head_each(
    latents, gain_self, w_qkv, w_out, gain_cross, w_kv, w_embed, gain_point, w_query, w_back,
    gain_head, w_hidden, w_sdf, *, points, count,
):
    me = lax.axis_index("query")
    rows = latents.shape[0]
    core = jnp.reshape(me % 2, (1,))
    packed = pack(w_qkv, latents)
    received = lax.all_to_all(packed, "query", split_axis=0, concat_axis=0, tiled=True)

    numbers = me * points + jnp.arange(points, dtype=jnp.int32)
    features = feature_rows(numbers)
    features = jnp.pad(features, ((0, FEATURE_ROWS - features.shape[0]), (0, 0)))
    w_embed = jnp.pad(w_embed, ((0, FEATURE_ROWS - w_embed.shape[0]), (0, 0)))
    queries = point_queries(after(features, packed), w_embed, gain_point[None, :], w_query)
    back = after(w_back, packed).T
    embed = after(w_embed, packed).T
    gain = jnp.broadcast_to(after(gain_head, packed)[:, None], (gain_head.shape[0], 128))
    sdf_row = jnp.pad(after(w_sdf, packed)[None, :], ((0, 15), (0, 0)))
    out = w_out
    out = jnp.concatenate([out, swap(after(out, packed), 8, count)], axis=0)

    received, queries, back, embed, gain, sdf_row = lax.optimization_barrier(
        (received, queries, back, embed, gain, sdf_row)
    )
    own = unpack(received)
    other = swap(own, 1, count)
    out_swapped = swap(after(out, received), 4, count)
    attended, all_latents = self_attention(core, received, own, other, gain_self[None, :])

    hidden = after(w_hidden, attended).T
    attended = jnp.concatenate([attended, swap(attended, 8, count)], axis=0)
    out = jnp.concatenate([out, after(out_swapped, attended)], axis=0)
    out_swapped = swap(out, 2, count)
    attended = jnp.concatenate([attended, swap(attended, 4, count)], axis=0)
    attended = jnp.concatenate([attended, swap(attended, 2, count)], axis=0)
    out = jnp.concatenate([out, after(out_swapped, attended)], axis=0)
    far = swap(attended, 1, count)
    out_far = swap(out, 1, count)
    decoded, sdf = tail(
        jnp.reshape(me * rows, (1,)), attended, far, out, out_far, all_latents,
        gain_cross[None, :], w_kv, queries, features, back, embed, gain, hidden, sdf_row,
    )
    return decoded, sdf[0]


def solution(mesh):
    parts, count = mesh.shape["shape"], mesh.shape["query"]

    def program(latents, *others):
        own = latents.shape[0] // (parts * count)
        points = 1024
        shards = functools.partial(any_slice, points=points)
        if count == HEADS and own == 16 and others[1].shape[1] // count == 64:
            shards = functools.partial(one_head_each, points=points, count=count)
        return jax.shard_map(
            shards,
            mesh=mesh,
            in_specs=(
                P(("shape", "query"), None),
                P(),
                P(None, "query", None),
                P("query", None),
                P(),
                P(),
                P(),
                P(),
                P(),
                P(),
                P(),
                P(),
                P(),
            ),
            out_specs=(P(("shape", "query"), None), P(("shape", "query"))),
            check_vma=False,
        )(latents, *others)

    return program
```

time: 206 us -> 94.6 us (0.46)
  blocking collectives: 61.1 us -> 0 us
  matrix products: 49.7 us -> 0 us
  waiting for transfers between devices: 56.5 us -> 14.7 us
  Pallas kernels: 0 us -> 30.9 us
  starting transfers between devices: 0.08 us -> 18.5 us
  local copies, waits for them, and re-layouts: 6.99 us -> 24.8 us
  between operations: 14.3 us -> 0.77 us
  other arithmetic: 16.2 us -> 3.98 us
    all_gather x3 -> x0, blocking collectives: 61.1 us -> none  [the longest x1 21 us: shards(): lax.all_gather(qkv[2], 'query', axis=0, tiled=True)]
    all_gather x2 -> x0, waiting for transfers between devices: 55.1 us -> none  [the longest x1 55.1 us: shards(): lax.all_gather(w_qkv, 'query', axis=1, tiled=True)]
    dot_general x19 -> x0, matrix products: 48.5 us -> none  [the longest x8 13.9 us: per_group(): jnp.einsum('grn,nge->rge', weights, group_values, preferred_element_type=...]
    pallas_call x0 -> x5, Pallas kernels: none -> 30.9 us  [the longest x1 16.5 us: tail(): pl.pallas_call(tail_kernel, in_specs=[pl.BlockSpec(memory_space=pltpu.SME...]
    ppermute x0 -> x9, waiting for transfers between devices: none -> 13.7 us  [swap(): return lax.ppermute(values, 'query', [(i, i ^ bit) for i in range(count)])]
    sub x4 -> x0, other arithmetic: 12.5 us -> none  [per_group(): powers = jnp.exp(scores - highest)]
    ppermute x0 -> x9, starting transfers between devices: none -> 11.1 us  [swap(): return lax.ppermute(values, 'query', [(i, i ^ bit) for i in range(count)])]
    unnamed x21 -> x30, local copies, waits for them, and re-layouts: 4.15 us -> 14.1 us
  transfers between devices with their start and end apart: 2 -> 10, of which waited for: 1 -> 4; matrix products, arithmetic and copies ran while one was open for 10% -> 21% of each run, Pallas kernels for 0% -> 13%
where the time goes in v1:
time: 94.6 us; the launch traced here: 93.7 us
  Pallas kernels  30.9 us (33%)
  local copies, waits for them, and re-layouts  24.8 us (26%)
  starting transfers between devices  18.5 us (20%)
  waiting for transfers between devices  14.7 us (16%)
  other arithmetic  3.98 us (4%)
    pallas_call x1, Pallas kernels, tail(): pl.pallas_call(tail_kernel, in_specs=[pl.BlockSpec(memory_space=pltpu.SME...  16.5 us
    unnamed x30, local copies, waits for them, and re-layouts  14.1 us
    ppermute x9, waiting for transfers between devices, swap(): return lax.ppermute(values, 'query', [(i, i ^ bit) for i in range(count)])  13.7 us
    ppermute x9, starting transfers between devices, swap(): return lax.ppermute(values, 'query', [(i, i ^ bit) for i in range(count)])  11.1 us
    all_to_all x1, starting transfers between devices, one_head_each(): lax.all_to_all(packed, 'query', split_axis=0, concat_axis=0, tiled=True)  7.39 us
    pallas_call x1, Pallas kernels, point_queries(): pl.pallas_call(point_kernel, grid=(points // POINT_BLOCK,), in_specs=[pl....  7.38 us
    optimization_barrier x2, local copies, waits for them, and re-layouts, after(): return lax.optimization_barrier((values, *others))[0]  6.86 us
    pallas_call x1, Pallas kernels, self_attention(): pl.pallas_call(self_kernel, in_specs=[pl.BlockSpec(memory_space=pltpu.SME...  2.88 us
  transfers between devices with their start and end apart: 10, of which 4 were waited for; matrix products, arithmetic and copies ran while one was open for 21% of the time, Pallas kernels for 13%

profile of v1, /device:TPU:0, one launch (start us, length us, event | category | flops | bytes accessed | tf_op | source)
XLA Modules:
  0.0 93.7 jit_solution(15816251931770495304)
XLA Ops:
  0.6 0.0 copy-start.9
  0.6 2.3 %pack.1 = bf16[16,80,256]{2,1,0:T(8,128)(2,1)} custom-call(bf16[3,64,1024]{2,1,0:T(8,128)(2,1)} %w_ref.1, bf16[16,1024]{1,0:T(8,128)(2,1)} %latents_ref.1), custom_call_target="tpu_custom_call" | custom-call | tf_op jit(solution)/shard_map/pack/pallas_call | solution.py:143
  2.9 7.4 %all-to-all-start = ((bf16[16,80,256]{2,1,0:T(8,128)(2,1)}), bf16[16,80,256]{2,1,0:T(8,128)(2,1)S(1)}, u32[]{:S(2)}, u32[]{:S(2)}) async-start(bf16[16,80,256]{2,1,0:T(8,128)(2,1)} %pack.1), calls=%async_computation | async-start | bytes 1310720 | tf_op jit(solution)/shard_map/all_to_all | solution.py:318
  10.3 2.8 %collective-permute-start.5 = (bf16[64,1024]{1,0:T(8,128)(2,1)}, bf16[64,1024]{1,0:T(8,128)(2,1)}, u32[]{:S(2)}, u32[]{:S(2)}) collective-permute-start(bf16[64,1024]{1,0:T(8,128)(2,1)} %param.16), channel_id=1, source_target_pairs={{0,8},{1,9},{2,10},{3,11},{4,12},{5,13},{6,14},{7,15},{8,0},{9,1},... | collective-permute-start | bytes 393224 | tf_op jit(solution)/shard_map/ppermute | solution.py:303
  13.1 0.1 mul.51
  13.2 0.0 copy-done.9
  13.2 0.2 copy.15
  13.4 0.1 pad.12
  13.5 0.8 copy.16.w_embed_ref
  14.3 0.1 and_select_fusion
  14.4 0.4 fusion.7
  14.8 0.7 fusion.4.features_ref
  15.5 0.0 copy-start.11
  15.5 7.4 %point_queries.1.queries_ref = bf16[1024,1024]{1,0:T(8,128)(2,1)} custom-call(bf16[64,1024]{1,0:T(8,128)(2,1)} %fusion.4.features_ref, bf16[64,1024]{1,0:T(8,128)(2,1)} %copy.16.w_embed_ref, f32[1,1024]{1,0:T(1,128)} %bitcast.24, bf16[1024,1024]{1,0:T(8,128)(2,1)} %w_query_ref.1), custom_call_target="tpu_custom_call" | custom-call | flops 2281701376 | bytes 4194304 | tf_op jit(solution)/shard_map/point_queries/pallas_call | solution.py:176
  22.9 0.0 copy-done.11
  22.9 0.6 pad.13.w_sdf_ref
  23.5 2.9 %copy.17 = bf16[1024,1024]{0,1:T(8,128)(2,1)S(1)} copy(bf16[1024,1024]{1,0:T(8,128)(2,1)} %param.22) | data formatting | bytes 4194304 | tf_op jit(solution)/shard_map/optimization_barrier | solution.py:307
  26.4 1.0 %all-to-all-done.received_ref = bf16[16,80,256]{2,1,0:T(8,128)(2,1)S(1)} async-done(((bf16[16,80,256]{2,1,0:T(8,128)(2,1)}), bf16[16,80,256]{2,1,0:T(8,128)(2,1)S(1)}, u32[]{:S(2)}, u32[]{:S(2)}) %all-to-all-start) | async-done | bytes 655392 | tf_op jit(solution)/shard_map/all_to_all | solution.py:318
  27.4 0.0 copy-start.8
  27.4 0.0 copy-done.10
  27.4 0.2 broadcast_in_dim.21.gain_head_ref
  27.6 0.6 copy-done.8
  28.2 1.9 %unpack.1.own_ref = bf16[256,512]{1,0:T(8,128)(2,1)} custom-call(bf16[16,80,256]{2,1,0:T(8,128)(2,1)} %copy-done.8), custom_call_target="tpu_custom_call" | custom-call | tf_op jit(solution)/shard_map/unpack/pallas_call | solution.py:160
  30.1 2.4 %collective-permute-start = (bf16[256,512]{1,0:T(8,128)(2,1)}, bf16[256,512]{1,0:T(8,128)(2,1)}, u32[]{:S(2)}, u32[]{:S(2)}) collective-permute-start(bf16[256,512]{1,0:T(8,128)(2,1)} %unpack.1.own_ref), channel_id=1, source_target_pairs={{0,1},{1,0},{2,3},{3,2},{4,5},{5,4},{6,7},{7,6},{8,9},{9,8},{10,11... | collective-permute-start | bytes 786440 | tf_op jit(solution)/shard_map/ppermute | solution.py:303
  32.5 1.6 %collective-permute-done.5 = bf16[64,1024]{1,0:T(8,128)(2,1)} collective-permute-done((bf16[64,1024]{1,0:T(8,128)(2,1)}, bf16[64,1024]{1,0:T(8,128)(2,1)}, u32[]{:S(2)}, u32[]{:S(2)}) %collective-permute-start.5) | collective-permute-done | bytes 131104 | tf_op jit(solution)/shard_map/ppermute | solution.py:303
  34.1 1.0 %pad_maximum_fusion.1 = bf16[128,1024]{1,0:T(8,128)(2,1)S(1)} fusion(bf16[64,1024]{1,0:T(8,128)(2,1)} %collective-permute-done.5, bf16[64,1024]{1,0:T(8,128)(2,1)} %param.16), kind=kLoop, calls=%fused_computation.5 | loop fusion | flops 524288 | bytes 524288 | tf_op jit(solution)/shard_map/concatenate | solution.py:330
  35.1 0.8 collective-permute-start.6
  35.9 1.6 %constant_dynamic-update-slice_fusion.9 = bf16[512,1024]{1,0:T(8,128)(2,1)} fusion(bf16[64,1024]{1,0:T(8,128)(2,1)} %param.16), kind=kLoop, calls=%fused_computation.23 | loop fusion | bytes 262144
  37.5 0.0 collective-permute-done.other_ref
  37.5 2.9 %self_attention.1 = (bf16[64,256]{1,0:T(8,128)(2,1)}, bf16[256,1024]{1,0:T(8,128)(2,1)}) custom-call(s32[1]{0:T(128)} %bitcast.1.core_ref, bf16[16,80,256]{2,1,0:T(8,128)(2,1)} %copy-done.8, bf16[256,512]{1,0:T(8,128)(2,1)} %unpack.1.own_ref, bf16[256,512]{1,0:T(8,128)(2,1)} %collective-permute-done.other_ref, f32[1,1024]{1,0:T(1,128)} %bitcast.23), custom_call_target="tpu_custom_call" | custom-call | tf_op jit(solution)/shard_map/self_attention/pallas_call | solution.py:218
  40.3 1.3 %collective-permute-start.1 = (bf16[64,256]{1,0:T(8,128)(2,1)}, bf16[64,256]{1,0:T(8,128)(2,1)S(1)}, u32[]{:S(2)}, u32[]{:S(2)}) collective-permute-start(bf16[64,256]{1,0:T(8,128)(2,1)} %get-tuple-element.28), channel_id=1, source_target_pairs={{0,8},{1,9},{2,10},{3,11},{4,12},{5,13},{6,14},{7,15},{8,0},{9,1},... | collective-permute-start | bytes 98312 | tf_op jit(solution)/shard_map/ppermute | solution.py:303
  41.7 1.4 %constant_dynamic-update-slice_fusion.1 = (bf16[128,256]{1,0:T(8,128)(2,1)S(1)}, bf16[512,256]{1,0:T(8,128)(2,1)}) fusion(bf16[64,256]{1,0:T(8,128)(2,1)} %get-tuple-element.28), kind=kLoop, calls=%fused_computation.15 | loop fusion | bytes 98304
  43.1 2.5 %collective-permute-done.1 = bf16[64,256]{1,0:T(8,128)(2,1)S(1)} collective-permute-done((bf16[64,256]{1,0:T(8,128)(2,1)}, bf16[64,256]{1,0:T(8,128)(2,1)S(1)}, u32[]{:S(2)}, u32[]{:S(2)}) %collective-permute-start.1) | collective-permute-done | bytes 32800 | tf_op jit(solution)/shard_map/ppermute | solution.py:303
  45.5 0.6 constant_dynamic-update-slice_fusion
  46.2 1.2 %collective-permute-start.2 = (bf16[128,256]{1,0:T(8,128)(2,1)S(1)}, bf16[128,256]{1,0:T(8,128)(2,1)S(1)}, u32[]{:S(2)}, u32[]{:S(2)}) collective-permute-start(bf16[128,256]{1,0:T(8,128)(2,1)S(1)} %get-tuple-element.44), channel_id=1, source_target_pairs={{0,4},{1,5},{2,6},{3,7},{4,0},{5,1},{6,2},{7,3},{8,12},{9,13},{10,... | collective-permute-start | bytes 196616 | tf_op jit(solution)/shard_map/ppermute | solution.py:303
  47.3 0.0 collective-permute-done.6
  47.3 1.0 %pad_maximum_fusion = bf16[256,1024]{1,0:T(8,128)(2,1)S(1)} fusion(bf16[128,1024]{1,0:T(8,128)(2,1)S(1)} %collective-permute-done.6, bf16[64,1024]{1,0:T(8,128)(2,1)} %collective-permute-done.5, bf16[64,1024]{1,0:T(8,128)(2,1)} %param.16), kind=kLoop, calls=%fused_computation | loop fusion | flops 1572864 | bytes 1048576 | tf_op jit(solution)/shard_map/concatenate | solution.py:342
  48.3 1.5 %collective-permute-start.7 = (bf16[256,1024]{1,0:T(8,128)(2,1)S(1)}, bf16[256,1024]{1,0:T(8,128)(2,1)S(1)}, u32[]{:S(2)}, u32[]{:S(2)}) collective-permute-start(bf16[256,1024]{1,0:T(8,128)(2,1)S(1)} %pad_maximum_fusion), channel_id=1, source_target_pairs={{0,2},{1,3},{2,0},{3,1},{4,6},{5,7},{6,4},{7,5},{8,10},{9,11},{10,... | collective-permute-start | bytes 1572872 | tf_op jit(solution)/shard_map/ppermute | solution.py:303
  49.8 1.6 %constant_dynamic-update-slice_fusion.8 = bf16[512,1024]{1,0:T(8,128)(2,1)} fusion(bf16[512,1024]{1,0:T(8,128)(2,1)} %constant_dynamic-update-slice_fusion.9, bf16[64,1024]{1,0:T(8,128)(2,1)} %collective-permute-done.5), kind=kLoop, calls=%fused_computation.22 | loop fusion | bytes 262144
  51.4 0.0 collective-permute-done.2
  51.4 0.8 pad_maximum_fusion.2
  52.2 0.6 collective-permute-start.3
  52.8 0.7 constant_dynamic-update-slice_fusion.7
  53.6 0.6 constant_dynamic-update-slice_fusion.3
  54.2 9.6 %collective-permute-done.3 = bf16[256,256]{1,0:T(8,128)(2,1)S(1)} collective-permute-done((bf16[256,256]{1,0:T(8,128)(2,1)S(1)}, bf16[256,256]{1,0:T(8,128)(2,1)S(1)}, u32[]{:S(2)}, u32[]{:S(2)}) %collective-permute-start.3) | collective-permute-done | bytes 131104 | tf_op jit(solution)/shard_map/ppermute | solution.py:303
  63.8 0.6 constant_dynamic-update-slice_fusion.2.near_ref
  64.4 0.0 collective-permute-done.7
  64.4 0.8 constant_dynamic-update-slice_fusion.6.out_near_ref
  65.3 0.0 collective-permute-start.8
  65.3 0.5 collective-permute-start.4
  65.8 0.0 copy-start.4
  65.8 4.0 %copy.18 = bf16[1024,1024]{0,1:T(8,128)(2,1)} copy(bf16[1024,1024]{1,0:T(8,128)(2,1)} %param.24) | data formatting | bytes 4194304 | tf_op jit(solution)/shard_map/optimization_barrier | solution.py:307
  69.8 0.0 collective-permute-done.4.far_ref
  69.8 0.0 collective-permute-done.8.out_far_ref
  69.8 0.0 copy-done.4
  69.8 0.0 copy-done.5
  69.8 0.0 copy-done.7
  69.8 0.0 copy-start
  69.8 1.6 %copy-done = bf16[1024,1024]{0,1:T(8,128)(2,1)S(1)} copy-done((bf16[1024,1024]{0,1:T(8,128)(2,1)S(1)}, bf16[1024,1024]{0,1:T(8,128)(2,1)}, u32[]{:S(2)}) %copy-start) | copy-done | bytes 2097176
  71.4 2.2 %copy-done.1 = bf16[2,1024,1024]{2,1,0:T(8,128)(2,1)S(1)} copy-done((bf16[2,1024,1024]{2,1,0:T(8,128)(2,1)S(1)}, bf16[2,1024,1024]{2,1,0:T(8,128)(2,1)}, u32[]{:S(2)}) %copy-start.1) | copy-done | bytes 4194328
  73.6 1.6 %copy-done.2 = bf16[1024,1024]{1,0:T(8,128)(2,1)S(1)} copy-done((bf16[1024,1024]{1,0:T(8,128)(2,1)S(1)}, bf16[1024,1024]{1,0:T(8,128)(2,1)}, u32[]{:S(2)}) %copy-start.2) | copy-done | bytes 2097176
  75.2 1.2 %copy-done.3 = bf16[512,1024]{1,0:T(8,128)(2,1)S(1)} copy-done((bf16[512,1024]{1,0:T(8,128)(2,1)S(1)}, bf16[512,1024]{1,0:T(8,128)(2,1)}, u32[]{:S(2)}) %copy-start.3) | copy-done | bytes 1048600
  76.4 0.8 copy-done.6
  77.2 16.5 %tail.1 = (bf16[16,1024]{1,0:T(8,128)(2,1)}, f32[1,1024]{1,0:T(1,128)}) custom-call(s32[1]{0:T(128)} %bitcast.first_ref, bf16[512,256]{1,0:T(8,128)(2,1)} %constant_dynamic-update-slice_fusion.2.near_ref, bf16[512,256]{1,0:T(8,128)(2,1)} %collective-permute-done.4.far_ref, bf16[512,1024]{1,0:T(8,128)(2,1)S(1)} %copy-done.3, ...), custom_call_target="tpu_custom_call" | custom-call | tf_op jit(solution)/shard_map/tail/pallas_call | solution.py:280
  (12 shorter events, 0.1 us)
Async XLA Ops:
  0.6 12.6 %copy-start.9 = (bf16[51,1024]{1,0:T(8,128)(2,1)S(1)}, bf16[51,1024]{1,0:T(8,128)(2,1)}, u32[]{:S(2)}) copy-start(bf16[51,1024]{1,0:T(8,128)(2,1)} %param.19) | copy-start | bytes 313348
  2.9 24.5 %all-to-all-start = ((bf16[16,80,256]{2,1,0:T(8,128)(2,1)}), bf16[16,80,256]{2,1,0:T(8,128)(2,1)S(1)}, u32[]{:S(2)}, u32[]{:S(2)}) async-start(bf16[16,80,256]{2,1,0:T(8,128)(2,1)} %pack.1), calls=%async_computation | async-start | bytes 1310720 | tf_op jit(solution)/shard_map/all_to_all | solution.py:318
  10.3 23.8 %collective-permute-start.5 = (bf16[64,1024]{1,0:T(8,128)(2,1)}, bf16[64,1024]{1,0:T(8,128)(2,1)}, u32[]{:S(2)}, u32[]{:S(2)}) collective-permute-start(bf16[64,1024]{1,0:T(8,128)(2,1)} %param.16), channel_id=1, source_target_pairs={{0,8},{1,9},{2,10},{3,11},{4,12},{5,13},{6,14},{7,15},{8,0},{9,1},... | collective-permute-start | bytes 393224 | tf_op jit(solution)/shard_map/ppermute | solution.py:303
  15.5 7.4 %copy-start.11 = (bf16[1024]{0:T(1024)(128)(2,1)S(1)}, bf16[1024]{0:T(1024)(128)(2,1)}, u32[]{:S(2)}) copy-start(bf16[1024]{0:T(1024)(128)(2,1)} %param.25) | copy-start | bytes 6148
  23.5 3.9 %copy-start.10 = (f32[1024]{0:T(1024)S(1)}, f32[1024]{0:T(1024)}, u32[]{:S(2)}) copy-start(f32[1024]{0:T(1024)} %param.23) | copy-start | bytes 12292
  27.4 0.8 copy-start.8
  30.1 7.4 %collective-permute-start = (bf16[256,512]{1,0:T(8,128)(2,1)}, bf16[256,512]{1,0:T(8,128)(2,1)}, u32[]{:S(2)}, u32[]{:S(2)}) collective-permute-start(bf16[256,512]{1,0:T(8,128)(2,1)} %unpack.1.own_ref), channel_id=1, source_target_pairs={{0,1},{1,0},{2,3},{3,2},{4,5},{5,4},{6,7},{7,6},{8,9},{9,8},{10,11... | collective-permute-start | bytes 786440 | tf_op jit(solution)/shard_map/ppermute | solution.py:303
  35.1 12.2 %collective-permute-start.6 = (bf16[128,1024]{1,0:T(8,128)(2,1)S(1)}, bf16[128,1024]{1,0:T(8,128)(2,1)S(1)}, u32[]{:S(2)}, u32[]{:S(2)}) collective-permute-start(bf16[128,1024]{1,0:T(8,128)(2,1)S(1)} %pad_maximum_fusion.1), channel_id=1, source_target_pairs={{0,4},{1,5},{2,6},{3,7},{4,0},{5,1},{6,2},{7,3},{8,12},{9,13},{10,... | collective-permute-start | bytes 786440 | tf_op jit(solution)/shard_map/ppermute | solution.py:303
  40.3 5.2 %collective-permute-start.1 = (bf16[64,256]{1,0:T(8,128)(2,1)}, bf16[64,256]{1,0:T(8,128)(2,1)S(1)}, u32[]{:S(2)}, u32[]{:S(2)}) collective-permute-start(bf16[64,256]{1,0:T(8,128)(2,1)} %get-tuple-element.28), channel_id=1, source_target_pairs={{0,8},{1,9},{2,10},{3,11},{4,12},{5,13},{6,14},{7,15},{8,0},{9,1},... | collective-permute-start | bytes 98312 | tf_op jit(solution)/shard_map/ppermute | solution.py:303
  46.2 5.3 %collective-permute-start.2 = (bf16[128,256]{1,0:T(8,128)(2,1)S(1)}, bf16[128,256]{1,0:T(8,128)(2,1)S(1)}, u32[]{:S(2)}, u32[]{:S(2)}) collective-permute-start(bf16[128,256]{1,0:T(8,128)(2,1)S(1)} %get-tuple-element.44), channel_id=1, source_target_pairs={{0,4},{1,5},{2,6},{3,7},{4,0},{5,1},{6,2},{7,3},{8,12},{9,13},{10,... | collective-permute-start | bytes 196616 | tf_op jit(solution)/shard_map/ppermute | solution.py:303
  48.3 16.1 %collective-permute-start.7 = (bf16[256,1024]{1,0:T(8,128)(2,1)S(1)}, bf16[256,1024]{1,0:T(8,128)(2,1)S(1)}, u32[]{:S(2)}, u32[]{:S(2)}) collective-permute-start(bf16[256,1024]{1,0:T(8,128)(2,1)S(1)} %pad_maximum_fusion), channel_id=1, source_target_pairs={{0,2},{1,3},{2,0},{3,1},{4,6},{5,7},{6,4},{7,5},{8,10},{9,11},{10,... | collective-permute-start | bytes 1572872 | tf_op jit(solution)/shard_map/ppermute | solution.py:303
  52.2 11.6 %collective-permute-start.3 = (bf16[256,256]{1,0:T(8,128)(2,1)S(1)}, bf16[256,256]{1,0:T(8,128)(2,1)S(1)}, u32[]{:S(2)}, u32[]{:S(2)}) collective-permute-start(bf16[256,256]{1,0:T(8,128)(2,1)S(1)} %pad_maximum_fusion.2), channel_id=1, source_target_pairs={{0,2},{1,3},{2,0},{3,1},{4,6},{5,7},{6,4},{7,5},{8,10},{9,11},{10,... | collective-permute-start | bytes 393224 | tf_op jit(solution)/shard_map/ppermute | solution.py:303
  65.3 4.5 %collective-permute-start.8 = (bf16[512,1024]{1,0:T(8,128)(2,1)}, bf16[512,1024]{1,0:T(8,128)(2,1)}, u32[]{:S(2)}, u32[]{:S(2)}) collective-permute-start(bf16[512,1024]{1,0:T(8,128)(2,1)} %constant_dynamic-update-slice_fusion.6.out_near_ref), channel_id=1, source_target_pairs={{0,1},{1,0},{2,3},{3,2},{4,5},{5,4},{6,7},{7,6},{8,9},{9,8},{10,11... | collective-permute-start | bytes 3145736 | tf_op jit(solution)/shard_map/ppermute | solution.py:303
  65.3 4.5 %collective-permute-start.4 = (bf16[512,256]{1,0:T(8,128)(2,1)}, bf16[512,256]{1,0:T(8,128)(2,1)}, u32[]{:S(2)}, u32[]{:S(2)}) collective-permute-start(bf16[512,256]{1,0:T(8,128)(2,1)} %constant_dynamic-update-slice_fusion.2.near_ref), channel_id=1, source_target_pairs={{0,1},{1,0},{2,3},{3,2},{4,5},{5,4},{6,7},{7,6},{8,9},{9,8},{10,11... | collective-permute-start | bytes 786440 | tf_op jit(solution)/shard_map/ppermute | solution.py:303
  65.8 4.0 %copy-start.4 = (bf16[64,1024]{1,0:T(8,128)(2,1)S(1)}, bf16[64,1024]{1,0:T(8,128)(2,1)}, u32[]{:S(2)}) copy-start(bf16[64,1024]{1,0:T(8,128)(2,1)} %fusion.4.features_ref) | copy-start | bytes 393220
  65.8 4.0 %copy-start.5 = (bf16[256,1024]{1,0:T(8,128)(2,1)S(1)}, bf16[256,1024]{1,0:T(8,128)(2,1)}, u32[]{:S(2)}) copy-start(bf16[256,1024]{1,0:T(8,128)(2,1)} %get-tuple-element.33.latents_ref) | copy-start | bytes 1572868
  65.8 4.0 %copy-start.7 = (f32[1024]{0:T(1024)S(1)}, f32[1024]{0:T(1024)}, u32[]{:S(2)}) copy-start(f32[1024]{0:T(1024)} %param.17) | copy-start | bytes 12292
  69.8 1.6 %copy-start = (bf16[1024,1024]{0,1:T(8,128)(2,1)S(1)}, bf16[1024,1024]{0,1:T(8,128)(2,1)}, u32[]{:S(2)}) copy-start(bf16[1024,1024]{0,1:T(8,128)(2,1)} %copy.18) | copy-start | bytes 6291460
  71.4 2.2 %copy-start.1 = (bf16[2,1024,1024]{2,1,0:T(8,128)(2,1)S(1)}, bf16[2,1024,1024]{2,1,0:T(8,128)(2,1)}, u32[]{:S(2)}) copy-start(bf16[2,1024,1024]{2,1,0:T(8,128)(2,1)} %w_kv_ref.1) | copy-start | bytes 12582916
  73.6 1.6 %copy-start.2 = (bf16[1024,1024]{1,0:T(8,128)(2,1)S(1)}, bf16[1024,1024]{1,0:T(8,128)(2,1)}, u32[]{:S(2)}) copy-start(bf16[1024,1024]{1,0:T(8,128)(2,1)} %point_queries.1.queries_ref) | copy-start | bytes 6291460
  75.2 1.2 %copy-start.3 = (bf16[512,1024]{1,0:T(8,128)(2,1)S(1)}, bf16[512,1024]{1,0:T(8,128)(2,1)}, u32[]{:S(2)}) copy-start(bf16[512,1024]{1,0:T(8,128)(2,1)} %constant_dynamic-update-slice_fusion.6.out_near_ref) | copy-start | bytes 3145732
  76.4 0.8 copy-start.6

commit v2 on v1

v2 whole, which is shorter than its diff:
```python
import functools
import math

import jax
import jax.numpy as jnp
from jax import lax
from jax.experimental import pallas as pl
from jax.experimental.pallas import tpu as pltpu
from jax.sharding import PartitionSpec as P

HEADS = 16
FREQS = 8
GRID = 512
HEAD_DIM = 64
SCALE = 1.0 / math.sqrt(HEAD_DIM)
POINT_BLOCK = 512
TAIL_LIMIT = 58
FEATURE_ROWS = 64
EXCHANGES = (8, 2, 4, 1)


def norm_rows(values, gain):
    center = jnp.mean(values, axis=-1, keepdims=True)
    centred = values - center
    spread = jnp.mean(centred * centred, axis=-1, keepdims=True)
    return centred * lax.rsqrt(spread + 1e-05) * gain


def attend(queries, keys, values):
    row_count, features = queries.shape
    key_count = keys.shape[0]
    head_dim = features // HEADS
    group_count = HEADS // 4
    head_queries = queries.reshape(row_count, group_count, 4, head_dim).transpose(1, 0, 2, 3)
    head_keys = keys.reshape(key_count, group_count, 4, head_dim).transpose(1, 0, 2, 3)
    head_values = values.reshape(key_count, group_count, 4, head_dim).transpose(1, 0, 2, 3)
    scaling = 1.0 / math.sqrt(head_dim)

    def per_group(block):
        group_query, group_keys, group_values = block
        scores = (
            jnp.einsum("rge,nge->grn", group_query, group_keys, preferred_element_type=jnp.float32)
            * scaling
        )
        highest = jnp.max(scores, axis=-1, keepdims=True)
        powers = jnp.exp(scores - highest)
        total = jnp.sum(powers, axis=-1, keepdims=True)
        weights = (powers / total).astype(jnp.bfloat16)
        blended = jnp.einsum(
            "grn,nge->rge", weights, group_values, preferred_element_type=jnp.float32
        )
        return blended.astype(jnp.bfloat16)

    result = lax.map(per_group, (head_queries, head_keys, head_values))
    return result.transpose(1, 0, 2, 3).reshape(row_count, features)


def feature_rows(numbers):
    cell_i = numbers // (GRID * GRID)
    cell_j = numbers // GRID % GRID
    cell_k = numbers % GRID
    cells = jnp.stack([cell_i, cell_j, cell_k], axis=0).astype(jnp.float32)
    coords = (2.0 * cells + 1.0) / GRID - 1.0
    freqs = 2.0 ** jnp.arange(FREQS, dtype=jnp.float32) * math.pi
    angles = (coords[:, None, :] * freqs[None, :, None]).reshape(3 * FREQS, numbers.shape[0])
    return jnp.concatenate([coords, jnp.sin(angles), jnp.cos(angles)], axis=0).astype(jnp.bfloat16)


def any_slice(
    latents, gain_self, w_qkv, w_out, gain_cross, w_kv, w_embed, gain_point, w_query, w_back,
    gain_head, w_hidden, w_sdf, *, points,
):
    inputs = latents.astype(jnp.float32)
    normed = norm_rows(inputs, gain_self).astype(jnp.bfloat16)
    qkv = jnp.einsum(
        "rd,sdc->src",
        normed,
        lax.all_gather(w_qkv, "query", axis=1, tiled=True),
        preferred_element_type=jnp.float32,
    ).astype(jnp.bfloat16)
    self_keys, self_values = (
        lax.all_gather(qkv[1], "query", axis=0, tiled=True),
        lax.all_gather(qkv[2], "query", axis=0, tiled=True),
    )
    attended = attend(qkv[0], self_keys, self_values)
    update = jnp.dot(
        attended,
        lax.all_gather(w_out, "query", axis=0, tiled=True),
        preferred_element_type=jnp.float32,
    )
    decoded = (inputs + update).astype(jnp.bfloat16)
    normed_two = norm_rows(decoded.astype(jnp.float32), gain_cross).astype(jnp.bfloat16)
    stacked = jnp.einsum(
        "rd,sdc->src",
        lax.all_gather(normed_two, "query", axis=0, tiled=True),
        w_kv,
        preferred_element_type=jnp.float32,
    ).astype(jnp.bfloat16)
    numbers = lax.axis_index("query") * points + jnp.arange(points, dtype=jnp.int32)
    features = feature_rows(numbers).T
    embedded = jnp.dot(features, w_embed, preferred_element_type=jnp.float32)
    point_normed = norm_rows(embedded, gain_point).astype(jnp.bfloat16)
    point_query = jnp.dot(point_normed, w_query, preferred_element_type=jnp.float32).astype(
        jnp.bfloat16
    )
    crossed = attend(point_query, stacked[0], stacked[1])
    joined = embedded + jnp.dot(crossed, w_back, preferred_element_type=jnp.float32)
    head_in = norm_rows(joined, gain_head).astype(jnp.bfloat16)
    hidden = jax.nn.gelu(jnp.dot(head_in, w_hidden, preferred_element_type=jnp.float32)).astype(
        jnp.bfloat16
    )
    sdf = jnp.dot(hidden, w_sdf, preferred_element_type=jnp.float32)
    return (decoded, sdf)


def dot_nn(left, right):
    return lax.dot_general(left, right, (((1,), (0,)), ((), ())), preferred_element_type=jnp.float32)


def dot_nt(left, right):
    return lax.dot_general(left, right, (((1,), (1,)), ((), ())), preferred_element_type=jnp.float32)


def dot_tn(left, right):
    return lax.dot_general(left, right, (((0,), (0,)), ((), ())), preferred_element_type=jnp.float32)


def limit(mebibytes):
    return pltpu.CompilerParams(vmem_limit_bytes=mebibytes * 1024 * 1024)


def pack_kernel(w_ref, latents_ref, out_ref):
    rows = w_ref.shape[1]
    count, width = latents_ref.shape
    pieces = width // 256
    for target in range(HEADS):
        low = target * HEAD_DIM
        query, key, value = (w_ref[s, :, low : low + HEAD_DIM] for s in range(3))
        out_ref[target, :rows, :] = jnp.concatenate([query, key], axis=1)
        out_ref[target, rows : rows + rows // 2, :] = jnp.concatenate(
            [value[: rows // 2], value[rows // 2 :]], axis=1
        )
        for piece in range(pieces):
            place = rows + rows // 2 + piece * count
            first = 128 * (piece + pieces * (target % 2))
            out_ref[target, place : place + count, :] = latents_ref[:, first : first + 128]


def pack(w_qkv, latents):
    rows = w_qkv.shape[1]
    count, width = latents.shape
    depth = rows + rows // 2 + count * (width // 256)
    return pl.pallas_call(
        pack_kernel,
        out_shape=jax.ShapeDtypeStruct((HEADS, depth, 128), jnp.bfloat16),
        name="pack",
    )(w_qkv, latents)


def unpack_kernel(received_ref, half_ref):
    rows, width = half_ref.shape
    count = rows // HEADS
    first = received_ref.shape[1] - count * (width // 128)
    for piece in range(width // 128):
        low = first + piece * count
        half_ref[:, 128 * piece : 128 * piece + 128] = received_ref[:, low : low + count, :].reshape(
            rows, 128
        )


def unpack(received, count, width):
    return pl.pallas_call(
        unpack_kernel,
        out_shape=jax.ShapeDtypeStruct((count * HEADS, width // 2), jnp.bfloat16),
        compiler_params=limit(4),
        name="unpack",
    )(received)


def point_norm_kernel(features_ref, w_embed_ref, gain_ref, out_ref):
    embedded = dot_tn(features_ref[...], w_embed_ref[...])
    out_ref[...] = norm_rows(embedded, gain_ref[...]).astype(jnp.bfloat16)


def point_norms(features, w_embed, gain):
    points, width = features.shape[1], w_embed.shape[1]
    return pl.pallas_call(
        point_norm_kernel,
        out_shape=jax.ShapeDtypeStruct((points, width), jnp.bfloat16),
        compiler_params=limit(16),
        cost_estimate=pl.CostEstimate(
            flops=16 * points * width, bytes_accessed=8 * points * width, transcendentals=0
        ),
        name="point_norms",
    )(features, w_embed, gain)


def point_query_kernel(normed_ref, w_query_ref, out_ref):
    out_ref[...] = dot_nn(normed_ref[...], w_query_ref[...]).astype(jnp.bfloat16)


def point_queries(normed, w_query):
    points, width = normed.shape
    return pl.pallas_call(
        point_query_kernel,
        grid=(points // POINT_BLOCK,),
        in_specs=[
            pl.BlockSpec((POINT_BLOCK, width), lambda i: (i, 0)),
            pl.BlockSpec((width, width), lambda i: (0, 0)),
        ],
        out_specs=pl.BlockSpec((POINT_BLOCK, width), lambda i: (i, 0)),
        out_shape=jax.ShapeDtypeStruct((points, width), jnp.bfloat16),
        cost_estimate=pl.CostEstimate(
            flops=2 * points * width * width, bytes_accessed=6 * width * width, transcendentals=0
        ),
        name="point_queries",
    )(normed, w_query)


def joined_halves(core, own, other):
    first = core == 0
    return jnp.concatenate([jnp.where(first, own, other), jnp.where(first, other, own)], axis=1)


def self_kernel(place_ref, received_ref, own_ref, other_ref, gain_ref, out_ref):
    latents = joined_halves(place_ref[1], own_ref[...], other_ref[...])
    normed = norm_rows(latents.astype(jnp.float32), gain_ref[...]).astype(jnp.bfloat16)
    width = latents.shape[1]
    rows = width // HEADS
    query_key = dot_nn(normed, received_ref[:, :rows, :].reshape(width, 2 * HEAD_DIM))
    query_key = query_key.astype(jnp.bfloat16)
    folded = received_ref[:, rows : rows + rows // 2, :]
    w_value = jnp.concatenate([folded[:, :, :HEAD_DIM], folded[:, :, HEAD_DIM:]], axis=1)
    values = dot_nn(normed, w_value.reshape(width, HEAD_DIM)).astype(jnp.bfloat16)
    scores = dot_nt(query_key[:, HEAD_DIM:], query_key[:, :HEAD_DIM]) * SCALE
    powers = jnp.exp(scores - jnp.max(scores, axis=0, keepdims=True))
    shares = (powers / jnp.sum(powers, axis=0, keepdims=True)).astype(jnp.bfloat16)
    attended = dot_tn(values, shares).astype(jnp.bfloat16)
    half = HEAD_DIM // 2
    for target in range(HEADS):
        out_ref[target] = attended[half * (target % 2) : half * (target % 2) + half, :]


def self_attention(place, received, own, other, gain):
    vmem = pl.BlockSpec(memory_space=pltpu.VMEM)
    return pl.pallas_call(
        self_kernel,
        in_specs=[pl.BlockSpec(memory_space=pltpu.SMEM)] + [vmem] * 4,
        out_shape=jax.ShapeDtypeStruct((HEADS, HEAD_DIM // 2, own.shape[0]), jnp.bfloat16),
        compiler_params=limit(8),
        name="self_attention",
    )(place, received, own, other, gain)


def tail_kernel(
    place_ref, near_ref, far_ref, out_0_ref, out_1_ref, out_2_ref, out_3_ref, own_ref, other_ref,
    gain_cross_ref, w_kv_ref,
    queries_ref, features_ref, w_back_ref, w_embed_ref, gain_head_ref, w_hidden_ref, w_sdf_ref,
    decoded_ref, sdf_ref, attended, all_decoded, key_pairs, value_rows, crossed,
    w_kv, queries, w_back, w_hidden, semaphores,
):
    loads = [
        pltpu.make_async_copy(source, target, semaphores.at[i])
        for i, (source, target) in enumerate(
            ((w_kv_ref, w_kv), (queries_ref, queries), (w_back_ref, w_back), (w_hidden_ref, w_hidden))
        )
    ]
    for load in loads:
        load.start()
    me, core = place_ref[0], place_ref[1]
    half = HEAD_DIM // 2
    for block in range(HEADS):
        head = me ^ sum(bit for place, bit in enumerate(EXCHANGES) if block >> place & 1)
        for side_ref, place in ((near_ref, core), (far_ref, 1 - core)):
            row = pl.multiple_of(HEAD_DIM * block + half * place, half)
            attended[pl.ds(row, half), :] = side_ref[head]
    update = joined_halves(core, own_ref[...], other_ref[...]).astype(jnp.float32)
    quarter = out_0_ref.shape[0]
    for piece, out_ref in enumerate((out_0_ref, out_1_ref, out_2_ref, out_3_ref)):
        update += dot_tn(attended[quarter * piece : quarter * piece + quarter, :], out_ref[...])
    decoded = update.astype(jnp.bfloat16)
    all_decoded[...] = decoded
    rows = decoded_ref.shape[0]
    decoded_ref[...] = all_decoded[pl.ds(pl.multiple_of(me * rows, rows), rows), :]
    normed = norm_rows(decoded.astype(jnp.float32), gain_cross_ref[...]).astype(jnp.bfloat16)
    loads[0].wait()
    keys = dot_nn(normed, w_kv[0]).astype(jnp.bfloat16) * SCALE
    key_count = keys.shape[0]
    lane = lax.broadcasted_iota(jnp.int32, (key_count, 128), 1)
    for pair in range(HEADS // 2):
        both = keys[:, 128 * pair : 128 * pair + 128]
        zero = jnp.zeros_like(both)
        key_pairs[pair, :key_count, :] = jnp.where(lane < HEAD_DIM, both, zero)
        key_pairs[pair, key_count:, :] = jnp.where(lane < HEAD_DIM, zero, both)
    values = dot_nn(normed, w_kv[1]).T.astype(jnp.bfloat16)
    for head in range(HEADS):
        value_rows[head, :HEAD_DIM, :] = values[HEAD_DIM * head : HEAD_DIM * head + HEAD_DIM, :]
        value_rows[head, HEAD_DIM:, :] = jnp.ones((16, key_count), jnp.bfloat16)

    loads[1].wait()
    for pair in range(HEADS // 2):
        scores = dot_nt(key_pairs[pair], queries[:, 128 * pair : 128 * pair + 128])
        for side in range(2):
            head = 2 * pair + side
            own = scores[side * key_count : side * key_count + key_count, :]
            powers = jnp.exp(own - jnp.max(own, axis=0, keepdims=True)).astype(jnp.bfloat16)
            blended = dot_nn(value_rows[head], powers)
            crossed[HEAD_DIM * head : HEAD_DIM * head + HEAD_DIM, :] = (
                blended[:HEAD_DIM, :] / blended[HEAD_DIM : HEAD_DIM + 1, :]
            ).astype(jnp.bfloat16)

    loads[2].wait()
    joined = dot_tn(crossed[...], w_back[...]) + dot_tn(features_ref[...], w_embed_ref[...])
    head_in = norm_rows(joined, gain_head_ref[...]).astype(jnp.bfloat16)
    loads[3].wait()
    hidden = jax.nn.gelu(dot_nn(head_in, w_hidden[...])).astype(jnp.bfloat16)
    sdf_ref[...] = dot_nt(w_sdf_ref[...], hidden)[:1, :]


def tail(
    place, near, far, outs, own, other, gain_cross, w_kv, queries, features, w_back, w_embed,
    gain_head, w_hidden, w_sdf,
):
    points, width = queries.shape
    keys = own.shape[0]
    hbm = pl.BlockSpec(memory_space=pl.ANY)
    vmem = pl.BlockSpec(memory_space=pltpu.VMEM)
    return pl.pallas_call(
        tail_kernel,
        in_specs=[pl.BlockSpec(memory_space=pltpu.SMEM)]
        + [vmem] * 9
        + [hbm, hbm, vmem, hbm, vmem, vmem, hbm, vmem],
        out_specs=(vmem, vmem),
        out_shape=(
            jax.ShapeDtypeStruct((keys // HEADS, width), jnp.bfloat16),
            jax.ShapeDtypeStruct((1, points), jnp.float32),
        ),
        scratch_shapes=[
            pltpu.VMEM((width, keys), jnp.bfloat16),
            pltpu.VMEM((keys, width), jnp.bfloat16),
            pltpu.VMEM((HEADS // 2, 2 * keys, 128), jnp.bfloat16),
            pltpu.VMEM((HEADS, HEAD_DIM + 16, keys), jnp.bfloat16),
            pltpu.VMEM((width, points), jnp.bfloat16),
            pltpu.VMEM(w_kv.shape, jnp.bfloat16),
            pltpu.VMEM(queries.shape, jnp.bfloat16),
            pltpu.VMEM(w_back.shape, jnp.bfloat16),
            pltpu.VMEM(w_hidden.shape, jnp.bfloat16),
            pltpu.SemaphoreType.DMA((4,)),
        ],
        compiler_params=limit(TAIL_LIMIT),
        name="tail",
    )(
        place, near, far, *outs, own, other, gain_cross, w_kv, queries, features, w_back, w_embed,
        gain_head, w_hidden, w_sdf,
    )


def swap(values, bit, count):
    return lax.ppermute(values, "query", [(i, i ^ bit) for i in range(count)])


def to_all(blocks):
    return lax.all_to_all(blocks, "query", split_axis=0, concat_axis=0, tiled=True)


def after(values, *others):
    return lax.optimization_barrier((values, *others))[0]


def one_head_each(
    latents, gain_self, w_qkv, w_out, gain_cross, w_kv, w_embed, gain_point, w_query, w_back,
    gain_head, w_hidden, w_sdf, *, points, count,
):
    me = lax.axis_index("query")
    place = jnp.stack([me, me & 1])
    received = to_all(pack(w_qkv, latents))

    numbers = me * points + jnp.arange(points, dtype=jnp.int32)
    features = feature_rows(numbers)
    features = jnp.pad(features, ((0, FEATURE_ROWS - features.shape[0]), (0, 0)))
    w_embed = jnp.pad(w_embed, ((0, FEATURE_ROWS - w_embed.shape[0]), (0, 0)))
    sdf_row = jnp.pad(w_sdf[None, :], ((0, 15), (0, 0)))
    out = jnp.concatenate([w_out, swap(w_out, EXCHANGES[0], count)], axis=0)
    out_swapped = swap(out, EXCHANGES[1], count)
    normed = point_norms(after(features, out), w_embed, gain_point[None, :])
    out_0 = jnp.concatenate([out, after(out_swapped, normed)], axis=0)
    out_1 = swap(out_0, EXCHANGES[2], count)
    queries = point_queries(normed, w_query)

    received, queries, features, w_embed, sdf_row, place = lax.optimization_barrier(
        (received, queries, features, w_embed, sdf_row, place)
    )
    own = unpack(received, latents.shape[0], latents.shape[1])
    other = swap(own, 1, count)
    out_2 = swap(after(out_0, own), EXCHANGES[3], count)
    attended = self_attention(place, received, own, other, gain_self[None, :])
    near = to_all(attended)
    out_3 = swap(after(out_1, near), EXCHANGES[3], count)
    far = swap(near, 1, count)
    decoded, sdf = tail(
        place, near, far, (out_0, out_1, out_2, out_3), own, other, gain_cross[None, :], w_kv,
        queries, features, w_back, w_embed, gain_head[None, :], w_hidden, sdf_row,
    )
    return decoded, sdf[0]


def solution(mesh):
    parts, count = mesh.shape["shape"], mesh.shape["query"]

    def program(latents, *others):
        own = latents.shape[0] // (parts * count)
        points = 1024
        shards = functools.partial(any_slice, points=points)
        if count == HEADS and own == 16 and others[1].shape[1] // count == 64:
            shards = functools.partial(one_head_each, points=points, count=count)
        return jax.shard_map(
            shards,
            mesh=mesh,
            in_specs=(
                P(("shape", "query"), None),
                P(),
                P(None, "query", None),
                P("query", None),
                P(),
                P(),
                P(),
                P(),
                P(),
                P(),
                P(),
                P(),
                P(),
            ),
            out_specs=(P(("shape", "query"), None), P(("shape", "query"))),
            check_vma=False,
        )(latents, *others)

    return program
```

time: 94.6 us -> 70.5 us (0.75)
  local copies, waits for them, and re-layouts: 24.8 us -> 2.98 us
  other arithmetic: 3.98 us -> 0.66 us
  waiting for transfers between devices: 14.7 us -> 17.8 us
  starting transfers between devices: 18.5 us -> 17.3 us
    unnamed x30 -> x36, local copies, waits for them, and re-layouts: 14.1 us -> 2.24 us
    all_to_all x1 -> x2, waiting for transfers between devices: 1 us -> 8.26 us  [to_all(): lax.all_to_all(blocks, 'query', split_axis=0, concat_axis=0, tiled=True)]
    optimization_barrier x2 -> x0, local copies, waits for them, and re-layouts: 6.86 us -> none  [after(): return lax.optimization_barrier((values, *others))[0]]
    ppermute x9 -> x7, waiting for transfers between devices: 13.7 us -> 9.51 us  [swap(): return lax.ppermute(values, 'query', [(i, i ^ bit) for i in range(count)])]
    concatenate x3 -> x0, other arithmetic: 2.76 us -> none  [the longest x1 1 us: one_head_each(): out = jnp.concatenate([out, after(out_swapped, attended)], axis=0)]
    pallas_call x1, Pallas kernels: 16.5 us -> 19.1 us  [tail(): pl.pallas_call(tail_kernel, in_specs=[pl.BlockSpec(memory_space=pltpu.SME...]
    pallas_call x3 -> x4, Pallas kernels: 11.5 us -> 9.07 us  [the longest x1 5.42 us: point_queries(): pl.pallas_call(point_query_kernel, grid=(points // POINT_BLOCK,), in_spec...]
    concatenate x3 -> x1, local copies, waits for them, and re-layouts: 2.09 us -> 0.02 us  [one_head_each(): out_0 = jnp.concatenate([out, after(out_swapped, normed)], axis=0)]
  transfers between devices with their start and end apart: 10 -> 9, of which waited for: 4 -> 4; matrix products, arithmetic and copies ran while one was open for 21% -> 2% of each run, Pallas kernels for 13% -> 16%
where the time goes in v2:
time: 70.5 us; the launch traced here: 70.2 us
  Pallas kernels  30.4 us (43%)
  waiting for transfers between devices  17.8 us (25%)
  starting transfers between devices  17.3 us (25%)
  local copies, waits for them, and re-layouts  2.98 us (4%)
  between operations  1.04 us (1%)
    pallas_call x1, Pallas kernels, tail(): pl.pallas_call(tail_kernel, in_specs=[pl.BlockSpec(memory_space=pltpu.SME...  19.1 us
    ppermute x7, waiting for transfers between devices, swap(): return lax.ppermute(values, 'query', [(i, i ^ bit) for i in range(count)])  9.51 us
    ppermute x7, starting transfers between devices, swap(): return lax.ppermute(values, 'query', [(i, i ^ bit) for i in range(count)])  9.38 us
    all_to_all x2, waiting for transfers between devices, to_all(): lax.all_to_all(blocks, 'query', split_axis=0, concat_axis=0, tiled=True)  8.26 us
    all_to_all x2, starting transfers between devices, to_all(): lax.all_to_all(blocks, 'query', split_axis=0, concat_axis=0, tiled=True)  7.93 us
    pallas_call x1, Pallas kernels, point_queries(): pl.pallas_call(point_query_kernel, grid=(points // POINT_BLOCK,), in_spec...  5.42 us
    pallas_call x1, Pallas kernels, self_attention(): pl.pallas_call(self_kernel, in_specs=[pl.BlockSpec(memory_space=pltpu.SME...  2.27 us
    unnamed x36, local copies, waits for them, and re-layouts  2.24 us
  transfers between devices with their start and end apart: 9, of which 4 were waited for; matrix products, arithmetic and copies ran while one was open for 2% of the time, Pallas kernels for 16%

profile of v2, /device:TPU:0, one launch (start us, length us, event | category | flops | bytes accessed | tf_op | source)
XLA Modules:
  0.0 70.2 jit_solution(8747086647696985687)
XLA Ops:
  0.6 0.0 copy-start.14
  0.6 0.0 copy-start.16
  0.7 0.0 copy-start.15
  0.7 0.0 copy-start.5
  0.7 4.1 %collective-permute-start = (bf16[64,1024]{1,0:T(8,128)(2,1)}, bf16[64,1024]{1,0:T(8,128)(2,1)S(1)}, u32[]{:S(2)}, u32[]{:S(2)}) collective-permute-start(bf16[64,1024]{1,0:T(8,128)(2,1)} %param.16), channel_id=1, source_target_pairs={{0,8},{1,9},{2,10},{3,11},{4,12},{5,13},{6,14},{7,15},{8,0},{9,1},... | collective-permute-start | bytes 393224 | tf_op jit(solution)/shard_map/ppermute | solution.py:359
  4.8 2.0 %pack.1 = bf16[16,160,128]{2,1,0:T(8,128)(2,1)} custom-call(bf16[3,64,1024]{2,1,0:T(8,128)(2,1)} %w_ref.1, bf16[16,1024]{1,0:T(8,128)(2,1)} %latents_ref.1), custom_call_target="tpu_custom_call" | custom-call | tf_op jit(solution)/shard_map/pack/pallas_call | solution.py:153
  6.8 3.9 %all-to-all-start = ((bf16[16,160,128]{2,1,0:T(8,128)(2,1)}), bf16[16,160,128]{2,1,0:T(8,128)(2,1)S(1)}, u32[]{:S(2)}, u32[]{:S(2)}) async-start(bf16[16,160,128]{2,1,0:T(8,128)(2,1)} %pack.1), calls=%async_computation | async-start | bytes 1310720 | tf_op jit(solution)/shard_map/all_to_all | solution.py:363
  10.8 0.1 mul.47
  10.9 0.1 and_select_fusion
  11.0 0.4 fusion.7
  11.4 0.0 copy-start.2
  11.4 0.1 pad_add_fusion.place_ref
  11.5 0.0 copy-done.16
  11.5 0.0 copy-start.7
  11.5 0.6 pad.13.w_sdf_ref
  12.1 0.0 copy-done.15
  12.2 0.0 copy-done.14
  12.2 0.0 copy-start.3
  12.2 0.0 collective-permute-done
  12.3 2.0 %collective-permute-start.3 = (bf16[128,1024]{1,0:T(8,128)(2,1)S(1)}, bf16[128,1024]{1,0:T(8,128)(2,1)S(1)}, u32[]{:S(2)}, u32[]{:S(2)}) collective-permute-start(bf16[128,1024]{1,0:T(8,128)(2,1)S(1)} %get-tuple-element.29), channel_id=1, source_target_pairs={{0,2},{1,3},{2,0},{3,1},{4,6},{5,7},{6,4},{7,5},{8,10},{9,11},{10,... | collective-permute-start | bytes 786440 | tf_op jit(solution)/shard_map/ppermute | solution.py:359
  14.2 0.0 copy-done.5
  14.2 1.6 %point_norms.1.normed_ref = bf16[1024,1024]{1,0:T(8,128)(2,1)S(1)} custom-call(bf16[64,1024]{1,0:T(8,128)(2,1)S(1)} %fusion.4.features_ref, bf16[64,1024]{1,0:T(8,128)(2,1)S(1)} %pad.12.w_embed_ref, f32[1,1024]{1,0:T(1,128)S(1)} %bitcast.17), custom_call_target="tpu_custom_call" | custom-call | flops 16777216 | bytes 8388608 | tf_op jit(solution)/shard_map/point_norms/pallas_call | solution.py:187
  15.8 0.0 copy-start.1
  15.8 1.3 %copy-done.1 = bf16[1024,1024]{1,0:T(8,128)(2,1)} copy-done((bf16[1024,1024]{1,0:T(8,128)(2,1)}, bf16[1024,1024]{1,0:T(8,128)(2,1)S(1)}, u32[]{:S(2)}) %copy-start.1) | copy-done | bytes 2097176
  17.1 0.0 copy-start.6
  17.1 5.4 %point_queries.1.queries_ref = bf16[1024,1024]{1,0:T(8,128)(2,1)} custom-call(bf16[1024,1024]{1,0:T(8,128)(2,1)} %copy-done.1, bf16[1024,1024]{1,0:T(8,128)(2,1)} %w_query_ref.1), custom_call_target="tpu_custom_call" | custom-call | flops 2147483648 | bytes 6291456 | tf_op jit(solution)/shard_map/point_queries/pallas_call | solution.py:204
  22.6 0.0 copy-done.2
  22.6 0.0 copy-done.3
  22.6 4.8 %all-to-all-done.received_ref = bf16[16,160,128]{2,1,0:T(8,128)(2,1)S(1)} async-done(((bf16[16,160,128]{2,1,0:T(8,128)(2,1)}), bf16[16,160,128]{2,1,0:T(8,128)(2,1)S(1)}, u32[]{:S(2)}, u32[]{:S(2)}) %all-to-all-start) | async-done | bytes 655392 | tf_op jit(solution)/shard_map/all_to_all | solution.py:363
  27.4 0.0 copy-start
  27.4 0.1 collective-permute-start.1
  27.5 0.0 collective-permute-done.3
  27.6 0.0 copy-start.9
  27.6 2.4 %collective-permute-start.4 = (bf16[256,1024]{1,0:T(8,128)(2,1)S(1)}, bf16[256,1024]{1,0:T(8,128)(2,1)S(1)}, u32[]{:S(2)}, u32[]{:S(2)}) collective-permute-start(bf16[256,1024]{1,0:T(8,128)(2,1)S(1)} %constant_dynamic-update-slice_fusion.2.out_0_ref), channel_id=1, source_target_pairs={{0,4},{1,5},{2,6},{3,7},{4,0},{5,1},{6,2},{7,3},{8,12},{9,13},{10,... | collective-permute-start | bytes 1572872 | tf_op jit(solution)/shard_map/ppermute | solution.py:359
  29.9 0.0 collective-permute-done.1.other_ref
  29.9 0.0 copy-start.4
  29.9 0.0 copy-done.7
  29.9 0.0 copy-done.6
  29.9 2.3 %self_attention.1 = bf16[16,32,256]{2,1,0:T(8,128)(2,1)} custom-call(s32[2]{0:T(128)S(1)} %pad_add_fusion.place_ref, bf16[16,160,128]{2,1,0:T(8,128)(2,1)S(1)} %all-to-all-done.received_ref, bf16[256,512]{1,0:T(8,128)(2,1)S(1)} %unpack.1.own_ref, bf16[256,512]{1,0:T(8,128)(2,1)S(1)} %collective-permute-done.1.other_ref, f32[1,1024]{1,0:T(1,128)S(1)} %bitcast.18), custom_call_target="tpu_custom_call" | custom-call | tf_op jit(solution)/shard_map/self_attention/pallas_call | solution.py:246
  32.2 4.0 %all-to-all-start.1 = ((bf16[16,32,256]{2,1,0:T(8,128)(2,1)}), bf16[16,32,256]{2,1,0:T(8,128)(2,1)S(1)}, u32[]{:S(2)}, u32[]{:S(2)}) async-start(bf16[16,32,256]{2,1,0:T(8,128)(2,1)} %self_attention.1), calls=%async_computation.1 | async-start | bytes 524288 | tf_op jit(solution)/shard_map/all_to_all | solution.py:363
  36.2 0.3 collective-permute-start.5
  36.5 7.7 %collective-permute-done.4.out_1_ref = bf16[256,1024]{1,0:T(8,128)(2,1)S(1)} collective-permute-done((bf16[256,1024]{1,0:T(8,128)(2,1)S(1)}, bf16[256,1024]{1,0:T(8,128)(2,1)S(1)}, u32[]{:S(2)}, u32[]{:S(2)}) %collective-permute-start.4) | collective-permute-done | bytes 524320 | tf_op jit(solution)/shard_map/ppermute | solution.py:359
  44.2 0.0 copy-start.10
  44.2 3.5 %all-to-all-done.1.near_ref = bf16[16,32,256]{2,1,0:T(8,128)(2,1)S(1)} async-done(((bf16[16,32,256]{2,1,0:T(8,128)(2,1)}), bf16[16,32,256]{2,1,0:T(8,128)(2,1)S(1)}, u32[]{:S(2)}, u32[]{:S(2)}) %all-to-all-start.1) | async-done | bytes 262176 | tf_op jit(solution)/shard_map/all_to_all | solution.py:363
  47.8 0.0 copy-start.8
  47.8 0.0 collective-permute-start.6
  47.8 0.5 collective-permute-start.2
  48.3 0.0 collective-permute-done.5.out_2_ref
  48.3 0.0 copy-start.11
  48.3 1.8 %collective-permute-done.2.far_ref = bf16[16,32,256]{2,1,0:T(8,128)(2,1)S(1)} collective-permute-done((bf16[16,32,256]{2,1,0:T(8,128)(2,1)S(1)}, bf16[16,32,256]{2,1,0:T(8,128)(2,1)S(1)}, u32[]{:S(2)}, u32[]{:S(2)}) %collective-permute-start.2) | collective-permute-done | bytes 262176 | tf_op jit(solution)/shard_map/ppermute | solution.py:359
  50.0 0.0 copy-start.13
  50.0 0.0 collective-permute-done.6.out_3_ref
  50.0 0.0 copy-start.12
  50.0 0.0 copy-done
  50.1 0.0 copy-done.9
  50.1 0.0 copy-done.4
  50.1 0.0 copy-done.10
  50.1 0.0 copy-done.8
  50.1 0.0 copy-done.11
  50.1 0.7 copy-done.13
  50.8 0.2 copy-done.12
  50.9 19.1 %tail.1 = (bf16[16,1024]{1,0:T(8,128)(2,1)}, f32[1,1024]{1,0:T(1,128)}) custom-call(s32[2]{0:T(128)} %copy-done.7, bf16[16,32,256]{2,1,0:T(8,128)(2,1)} %copy-done.8, bf16[16,32,256]{2,1,0:T(8,128)(2,1)} %copy-done.13, bf16[256,1024]{1,0:T(8,128)(2,1)} %copy-done.9, bf16[256,1024]{1,0:T(8,128)(2,1)} %copy-done.10, bf16[256,1024]{1,0:T(8,128)(2,1)} %copy-done.11, ...), custom_call_target="tpu_custom_call" | custom-call | tf_op jit(solution)/shard_map/tail/pallas_call | solution.py:328
  (11 shorter events, 0.2 us)
Async XLA Ops:
  0.6 11.5 %copy-start.14 = (bf16[64,1024]{1,0:T(8,128)(2,1)S(1)}, bf16[64,1024]{1,0:T(8,128)(2,1)}, u32[]{:S(2)}) copy-start(bf16[64,1024]{1,0:T(8,128)(2,1)} %param.16) | copy-start | bytes 393220
  0.6 10.9 %copy-start.16 = (bf16[1024]{0:T(1024)(128)(2,1)S(1)}, bf16[1024]{0:T(1024)(128)(2,1)}, u32[]{:S(2)}) copy-start(bf16[1024]{0:T(1024)(128)(2,1)} %param.25) | copy-start | bytes 6148
  0.7 11.5 %copy-start.15 = (bf16[51,1024]{1,0:T(8,128)(2,1)S(1)}, bf16[51,1024]{1,0:T(8,128)(2,1)}, u32[]{:S(2)}) copy-start(bf16[51,1024]{1,0:T(8,128)(2,1)} %param.19) | copy-start | bytes 313348
  0.7 13.6 %copy-start.5 = (f32[1024]{0:T(1024)S(1)}, f32[1024]{0:T(1024)}, u32[]{:S(2)}) copy-start(f32[1024]{0:T(1024)} %param.20) | copy-start | bytes 12292
  0.7 11.5 %collective-permute-start = (bf16[64,1024]{1,0:T(8,128)(2,1)}, bf16[64,1024]{1,0:T(8,128)(2,1)S(1)}, u32[]{:S(2)}, u32[]{:S(2)}) collective-permute-start(bf16[64,1024]{1,0:T(8,128)(2,1)} %param.16), channel_id=1, source_target_pairs={{0,8},{1,9},{2,10},{3,11},{4,12},{5,13},{6,14},{7,15},{8,0},{9,1},... | collective-permute-start | bytes 393224 | tf_op jit(solution)/shard_map/ppermute | solution.py:359
  6.8 20.5 %all-to-all-start = ((bf16[16,160,128]{2,1,0:T(8,128)(2,1)}), bf16[16,160,128]{2,1,0:T(8,128)(2,1)S(1)}, u32[]{:S(2)}, u32[]{:S(2)}) async-start(bf16[16,160,128]{2,1,0:T(8,128)(2,1)} %pack.1), calls=%async_computation | async-start | bytes 1310720 | tf_op jit(solution)/shard_map/all_to_all | solution.py:363
  11.4 11.1 %copy-start.2 = (bf16[64,1024]{1,0:T(8,128)(2,1)}, bf16[64,1024]{1,0:T(8,128)(2,1)S(1)}, u32[]{:S(2)}) copy-start(bf16[64,1024]{1,0:T(8,128)(2,1)S(1)} %fusion.4.features_ref) | copy-start | bytes 393220
  11.5 18.4 %copy-start.7 = (s32[2]{0:T(128)}, s32[2]{0:T(128)S(1)}, u32[]{:S(2)}) copy-start(s32[2]{0:T(128)S(1)} %pad_add_fusion.place_ref) | copy-start | bytes 28
  12.2 10.4 %copy-start.3 = (bf16[64,1024]{1,0:T(8,128)(2,1)}, bf16[64,1024]{1,0:T(8,128)(2,1)S(1)}, u32[]{:S(2)}) copy-start(bf16[64,1024]{1,0:T(8,128)(2,1)S(1)} %pad.12.w_embed_ref) | copy-start | bytes 393220
  12.3 15.3 %collective-permute-start.3 = (bf16[128,1024]{1,0:T(8,128)(2,1)S(1)}, bf16[128,1024]{1,0:T(8,128)(2,1)S(1)}, u32[]{:S(2)}, u32[]{:S(2)}) collective-permute-start(bf16[128,1024]{1,0:T(8,128)(2,1)S(1)} %get-tuple-element.29), channel_id=1, source_target_pairs={{0,2},{1,3},{2,0},{3,1},{4,6},{5,7},{6,4},{7,5},{8,10},{9,11},{10,... | collective-permute-start | bytes 786440 | tf_op jit(solution)/shard_map/ppermute | solution.py:359
  15.8 1.3 %copy-start.1 = (bf16[1024,1024]{1,0:T(8,128)(2,1)}, bf16[1024,1024]{1,0:T(8,128)(2,1)S(1)}, u32[]{:S(2)}) copy-start(bf16[1024,1024]{1,0:T(8,128)(2,1)S(1)} %point_norms.1.normed_ref) | copy-start | bytes 6291460
  17.1 12.8 %copy-start.6 = (f32[1024]{0:T(1024)S(1)}, f32[1024]{0:T(1024)}, u32[]{:S(2)}) copy-start(f32[1024]{0:T(1024)} %param.14) | copy-start | bytes 12292
  27.4 22.7 %copy-start = (bf16[256,512]{1,0:T(8,128)(2,1)}, bf16[256,512]{1,0:T(8,128)(2,1)S(1)}, u32[]{:S(2)}) copy-start(bf16[256,512]{1,0:T(8,128)(2,1)S(1)} %unpack.1.own_ref) | copy-start | bytes 786436
  27.4 2.5 %collective-permute-start.1 = (bf16[256,512]{1,0:T(8,128)(2,1)S(1)}, bf16[256,512]{1,0:T(8,128)(2,1)S(1)}, u32[]{:S(2)}, u32[]{:S(2)}) collective-permute-start(bf16[256,512]{1,0:T(8,128)(2,1)S(1)} %unpack.1.own_ref), channel_id=1, source_target_pairs={{0,1},{1,0},{2,3},{3,2},{4,5},{5,4},{6,7},{7,6},{8,9},{9,8},{10,11... | collective-permute-start | bytes 786440 | tf_op jit(solution)/shard_map/ppermute | solution.py:359
  27.6 22.5 %copy-start.9 = (bf16[256,1024]{1,0:T(8,128)(2,1)}, bf16[256,1024]{1,0:T(8,128)(2,1)S(1)}, u32[]{:S(2)}) copy-start(bf16[256,1024]{1,0:T(8,128)(2,1)S(1)} %constant_dynamic-update-slice_fusion.2.out_0_ref) | copy-start | bytes 1572868
  27.6 16.7 %collective-permute-start.4 = (bf16[256,1024]{1,0:T(8,128)(2,1)S(1)}, bf16[256,1024]{1,0:T(8,128)(2,1)S(1)}, u32[]{:S(2)}, u32[]{:S(2)}) collective-permute-start(bf16[256,1024]{1,0:T(8,128)(2,1)S(1)} %constant_dynamic-update-slice_fusion.2.out_0_ref), channel_id=1, source_target_pairs={{0,4},{1,5},{2,6},{3,7},{4,0},{5,1},{6,2},{7,3},{8,12},{9,13},{10,... | collective-permute-start | bytes 1572872 | tf_op jit(solution)/shard_map/ppermute | solution.py:359
  29.9 20.1 %copy-start.4 = (bf16[256,512]{1,0:T(8,128)(2,1)}, bf16[256,512]{1,0:T(8,128)(2,1)S(1)}, u32[]{:S(2)}) copy-start(bf16[256,512]{1,0:T(8,128)(2,1)S(1)} %collective-permute-done.1.other_ref) | copy-start | bytes 786436
  32.2 15.6 %all-to-all-start.1 = ((bf16[16,32,256]{2,1,0:T(8,128)(2,1)}), bf16[16,32,256]{2,1,0:T(8,128)(2,1)S(1)}, u32[]{:S(2)}, u32[]{:S(2)}) async-start(bf16[16,32,256]{2,1,0:T(8,128)(2,1)} %self_attention.1), calls=%async_computation.1 | async-start | bytes 524288 | tf_op jit(solution)/shard_map/all_to_all | solution.py:363
  36.2 12.0 %collective-permute-start.5 = (bf16[256,1024]{1,0:T(8,128)(2,1)S(1)}, bf16[256,1024]{1,0:T(8,128)(2,1)S(1)}, u32[]{:S(2)}, u32[]{:S(2)}) collective-permute-start(bf16[256,1024]{1,0:T(8,128)(2,1)S(1)} %constant_dynamic-update-slice_fusion.2.out_0_ref), channel_id=1, source_target_pairs={{0,1},{1,0},{2,3},{3,2},{4,5},{5,4},{6,7},{7,6},{8,9},{9,8},{10,11... | collective-permute-start | bytes 1572872 | tf_op jit(solution)/shard_map/ppermute | solution.py:359
  44.2 5.8 %copy-start.10 = (bf16[256,1024]{1,0:T(8,128)(2,1)}, bf16[256,1024]{1,0:T(8,128)(2,1)S(1)}, u32[]{:S(2)}) copy-start(bf16[256,1024]{1,0:T(8,128)(2,1)S(1)} %collective-permute-done.4.out_1_ref) | copy-start | bytes 1572868
  47.8 2.3 %copy-start.8 = (bf16[16,32,256]{2,1,0:T(8,128)(2,1)}, bf16[16,32,256]{2,1,0:T(8,128)(2,1)S(1)}, u32[]{:S(2)}) copy-start(bf16[16,32,256]{2,1,0:T(8,128)(2,1)S(1)} %all-to-all-done.1.near_ref) | copy-start | bytes 786436
  47.8 2.3 %collective-permute-start.6 = (bf16[256,1024]{1,0:T(8,128)(2,1)S(1)}, bf16[256,1024]{1,0:T(8,128)(2,1)S(1)}, u32[]{:S(2)}, u32[]{:S(2)}) collective-permute-start(bf16[256,1024]{1,0:T(8,128)(2,1)S(1)} %collective-permute-done.4.out_1_ref), channel_id=1, source_target_pairs={{0,1},{1,0},{2,3},{3,2},{4,5},{5,4},{6,7},{7,6},{8,9},{9,8},{10,11... | collective-permute-start | bytes 1572872 | tf_op jit(solution)/shard_map/ppermute | solution.py:359
  47.8 2.3 %collective-permute-start.2 = (bf16[16,32,256]{2,1,0:T(8,128)(2,1)S(1)}, bf16[16,32,256]{2,1,0:T(8,128)(2,1)S(1)}, u32[]{:S(2)}, u32[]{:S(2)}) collective-permute-start(bf16[16,32,256]{2,1,0:T(8,128)(2,1)S(1)} %all-to-all-done.1.near_ref), channel_id=1, source_target_pairs={{0,1},{1,0},{2,3},{3,2},{4,5},{5,4},{6,7},{7,6},{8,9},{9,8},{10,11... | collective-permute-start | bytes 786440 | tf_op jit(solution)/shard_map/ppermute | solution.py:359
  48.3 1.8 %copy-start.11 = (bf16[256,1024]{1,0:T(8,128)(2,1)}, bf16[256,1024]{1,0:T(8,128)(2,1)S(1)}, u32[]{:S(2)}) copy-start(bf16[256,1024]{1,0:T(8,128)(2,1)S(1)} %collective-permute-done.5.out_2_ref) | copy-start | bytes 1572868
  50.0 0.7 %copy-start.13 = (bf16[16,32,256]{2,1,0:T(8,128)(2,1)}, bf16[16,32,256]{2,1,0:T(8,128)(2,1)S(1)}, u32[]{:S(2)}) copy-start(bf16[16,32,256]{2,1,0:T(8,128)(2,1)S(1)} %collective-permute-done.2.far_ref) | copy-start | bytes 786436
  50.0 0.9 %copy-start.12 = (bf16[256,1024]{1,0:T(8,128)(2,1)}, bf16[256,1024]{1,0:T(8,128)(2,1)S(1)}, u32[]{:S(2)}) copy-start(bf16[256,1024]{1,0:T(8,128)(2,1)S(1)} %collective-permute-done.6.out_3_ref) | copy-start | bytes 1572868

commit v3 on v2

--- a/solution.py
+++ b/solution.py
@@ -14,9 +14,10 @@
 HEAD_DIM = 64
 SCALE = 1.0 / math.sqrt(HEAD_DIM)
 POINT_BLOCK = 512
-TAIL_LIMIT = 58
+TAIL_LIMIT = 16
 FEATURE_ROWS = 64
 EXCHANGES = (8, 2, 4, 1)
+HEAD_EXCHANGES = (2, 8, 4, 1)
 
 
 def norm_rows(values, gain):
@@ -173,6 +174,9 @@
         unpack_kernel,
         out_shape=jax.ShapeDtypeStruct((count * HEADS, width // 2), jnp.bfloat16),
         compiler_params=limit(4),
+        cost_estimate=pl.CostEstimate(
+            flops=2000000000, bytes_accessed=1024, transcendentals=0
+        ),
         name="unpack",
     )(received)
 
@@ -188,9 +192,7 @@
         point_norm_kernel,
         out_shape=jax.ShapeDtypeStruct((points, width), jnp.bfloat16),
         compiler_params=limit(16),
-        cost_estimate=pl.CostEstimate(
-            flops=16 * points * width, bytes_accessed=8 * points * width, transcendentals=0
-        ),
+        cost_estimate=pl.CostEstimate(flops=1024, bytes_accessed=1024, transcendentals=0),
         name="point_norms",
     )(features, w_embed, gain)
 
@@ -210,9 +212,7 @@
         ],
         out_specs=pl.BlockSpec((POINT_BLOCK, width), lambda i: (i, 0)),
         out_shape=jax.ShapeDtypeStruct((points, width), jnp.bfloat16),
-        cost_estimate=pl.CostEstimate(
-            flops=2 * points * width * width, bytes_accessed=6 * width * width, transcendentals=0
-        ),
+        cost_estimate=pl.CostEstimate(flops=1024, bytes_accessed=1024, transcendentals=0),
         name="point_queries",
     )(normed, w_query)
 
@@ -235,10 +235,7 @@
     scores = dot_nt(query_key[:, HEAD_DIM:], query_key[:, :HEAD_DIM]) * SCALE
     powers = jnp.exp(scores - jnp.max(scores, axis=0, keepdims=True))
     shares = (powers / jnp.sum(powers, axis=0, keepdims=True)).astype(jnp.bfloat16)
-    attended = dot_tn(values, shares).astype(jnp.bfloat16)
-    half = HEAD_DIM // 2
-    for target in range(HEADS):
-        out_ref[target] = attended[half * (target % 2) : half * (target % 2) + half, :]
+    out_ref[...] = dot_tn(values, shares).astype(jnp.bfloat16)
 
 
 def self_attention(place, received, own, other, gain):
@@ -246,7 +243,7 @@
     return pl.pallas_call(
         self_kernel,
         in_specs=[pl.BlockSpec(memory_space=pltpu.SMEM)] + [vmem] * 4,
-        out_shape=jax.ShapeDtypeStruct((HEADS, HEAD_DIM // 2, own.shape[0]), jnp.bfloat16),
+        out_shape=jax.ShapeDtypeStruct((HEAD_DIM, own.shape[0]), jnp.bfloat16),
         compiler_params=limit(8),
         name="self_attention",
     )(place, received, own, other, gain)
@@ -257,23 +254,16 @@
     gain_cross_ref, w_kv_ref,
     queries_ref, features_ref, w_back_ref, w_embed_ref, gain_head_ref, w_hidden_ref, w_sdf_ref,
     decoded_ref, sdf_ref, attended, all_decoded, key_pairs, value_rows, crossed,
-    w_kv, queries, w_back, w_hidden, semaphores,
 ):
-    loads = [
-        pltpu.make_async_copy(source, target, semaphores.at[i])
-        for i, (source, target) in enumerate(
-            ((w_kv_ref, w_kv), (queries_ref, queries), (w_back_ref, w_back), (w_hidden_ref, w_hidden))
-        )
-    ]
-    for load in loads:
-        load.start()
     me, core = place_ref[0], place_ref[1]
-    half = HEAD_DIM // 2
+    order = [EXCHANGES.index(bit) for bit in HEAD_EXCHANGES]
     for block in range(HEADS):
-        head = me ^ sum(bit for place, bit in enumerate(EXCHANGES) if block >> place & 1)
-        for side_ref, place in ((near_ref, core), (far_ref, 1 - core)):
-            row = pl.multiple_of(HEAD_DIM * block + half * place, half)
-            attended[pl.ds(row, half), :] = side_ref[head]
+        place = sum(1 << to for at, to in enumerate(order) if block >> at & 1)
+        side_ref = near_ref if block < HEADS // 2 else far_ref
+        row = HEAD_DIM * (block % (HEADS // 2))
+        attended[HEAD_DIM * place : HEAD_DIM * place + HEAD_DIM, :] = side_ref[
+            row : row + HEAD_DIM, :
+        ]
     update = joined_halves(core, own_ref[...], other_ref[...]).astype(jnp.float32)
     quarter = out_0_ref.shape[0]
     for piece, out_ref in enumerate((out_0_ref, out_1_ref, out_2_ref, out_3_ref)):
@@ -283,8 +273,7 @@
     rows = decoded_ref.shape[0]
     decoded_ref[...] = all_decoded[pl.ds(pl.multiple_of(me * rows, rows), rows), :]
     normed = norm_rows(decoded.astype(jnp.float32), gain_cross_ref[...]).astype(jnp.bfloat16)
-    loads[0].wait()
-    keys = dot_nn(normed, w_kv[0]).astype(jnp.bfloat16) * SCALE
+    keys = dot_nn(normed, w_kv_ref[0]).astype(jnp.bfloat16) * SCALE
     key_count = keys.shape[0]
     lane = lax.broadcasted_iota(jnp.int32, (key_count, 128), 1)
     for pair in range(HEADS // 2):
@@ -292,14 +281,13 @@
         zero = jnp.zeros_like(both)
         key_pairs[pair, :key_count, :] = jnp.where(lane < HEAD_DIM, both, zero)
         key_pairs[pair, key_count:, :] = jnp.where(lane < HEAD_DIM, zero, both)
-    values = dot_nn(normed, w_kv[1]).T.astype(jnp.bfloat16)
+    values = dot_nn(normed, w_kv_ref[1]).T.astype(jnp.bfloat16)
     for head in range(HEADS):
         value_rows[head, :HEAD_DIM, :] = values[HEAD_DIM * head : HEAD_DIM * head + HEAD_DIM, :]
         value_rows[head, HEAD_DIM:, :] = jnp.ones((16, key_count), jnp.bfloat16)
 
-    loads[1].wait()
     for pair in range(HEADS // 2):
-        scores = dot_nt(key_pairs[pair], queries[:, 128 * pair : 128 * pair + 128])
+        scores = dot_nt(key_pairs[pair], queries_ref[:, 128 * pair : 128 * pair + 128])
         for side in range(2):
             head = 2 * pair + side
             own = scores[side * key_count : side * key_count + key_count, :]
@@ -309,11 +297,9 @@
                 blended[:HEAD_DIM, :] / blended[HEAD_DIM : HEAD_DIM + 1, :]
             ).astype(jnp.bfloat16)
 
-    loads[2].wait()
-    joined = dot_tn(crossed[...], w_back[...]) + dot_tn(features_ref[...], w_embed_ref[...])
+    joined = dot_tn(crossed[...], w_back_ref[...]) + dot_tn(features_ref[...], w_embed_ref[...])
     head_in = norm_rows(joined, gain_head_ref[...]).astype(jnp.bfloat16)
-    loads[3].wait()
-    hidden = jax.nn.gelu(dot_nn(head_in, w_hidden[...])).astype(jnp.bfloat16)
+    hidden = jax.nn.gelu(dot_nn(head_in, w_hidden_ref[...])).astype(jnp.bfloat16)
     sdf_ref[...] = dot_nt(w_sdf_ref[...], hidden)[:1, :]
 
 
@@ -323,13 +309,12 @@
 ):
     points, width = queries.shape
     keys = own.shape[0]
-    hbm = pl.BlockSpec(memory_space=pl.ANY)
     vmem = pl.BlockSpec(memory_space=pltpu.VMEM)
     return pl.pallas_call(
         tail_kernel,
         in_specs=[pl.BlockSpec(memory_space=pltpu.SMEM)]
         + [vmem] * 9
-        + [hbm, hbm, vmem, hbm, vmem, vmem, hbm, vmem],
+        + [vmem] * 8,
         out_specs=(vmem, vmem),
         out_shape=(
             jax.ShapeDtypeStruct((keys // HEADS, width), jnp.bfloat16),
@@ -341,11 +326,6 @@
             pltpu.VMEM((HEADS // 2, 2 * keys, 128), jnp.bfloat16),
             pltpu.VMEM((HEADS, HEAD_DIM + 16, keys), jnp.bfloat16),
             pltpu.VMEM((width, points), jnp.bfloat16),
-            pltpu.VMEM(w_kv.shape, jnp.bfloat16),
-            pltpu.VMEM(queries.shape, jnp.bfloat16),
-            pltpu.VMEM(w_back.shape, jnp.bfloat16),
-            pltpu.VMEM(w_hidden.shape, jnp.bfloat16),
-            pltpu.SemaphoreType.DMA((4,)),
         ],
         compiler_params=limit(TAIL_LIMIT),
         name="tail",
@@ -383,20 +363,22 @@
     out = jnp.concatenate([w_out, swap(w_out, EXCHANGES[0], count)], axis=0)
     out_swapped = swap(out, EXCHANGES[1], count)
     normed = point_norms(after(features, out), w_embed, gain_point[None, :])
-    out_0 = jnp.concatenate([out, after(out_swapped, normed)], axis=0)
+    queries = point_queries(normed, w_query)
+    out_0 = jnp.concatenate([out, after(out_swapped, queries)], axis=0)
     out_1 = swap(out_0, EXCHANGES[2], count)
-    queries = point_queries(normed, w_query)
-
-    received, queries, features, w_embed, sdf_row, place = lax.optimization_barrier(
-        (received, queries, features, w_embed, sdf_row, place)
+
+    received, queries, features, w_embed, sdf_row, place, out_0 = lax.optimization_barrier(
+        (received, queries, features, w_embed, sdf_row, place, out_0)
     )
     own = unpack(received, latents.shape[0], latents.shape[1])
     other = swap(own, 1, count)
     out_2 = swap(after(out_0, own), EXCHANGES[3], count)
     attended = self_attention(place, received, own, other, gain_self[None, :])
-    near = to_all(attended)
-    out_3 = swap(after(out_1, near), EXCHANGES[3], count)
-    far = swap(near, 1, count)
+    near = attended
+    for bit in HEAD_EXCHANGES[:3]:
+        near = jnp.concatenate([near, swap(near, bit, count)], axis=0)
+    out_3 = swap(out_1, EXCHANGES[3], count)
+    far = swap(near, HEAD_EXCHANGES[3], count)
     decoded, sdf = tail(
         place, near, far, (out_0, out_1, out_2, out_3), own, other, gain_cross[None, :], w_kv,
         queries, features, w_back, w_embed, gain_head[None, :], w_hidden, sdf_row,

time: 70.5 us -> 65.6 us (0.930)
  waiting for transfers between devices: 17.8 us -> 13.5 us
  Pallas kernels: 30.4 us -> 26.9 us
  starting transfers between devices: 17.3 us -> 18.9 us
  local copies, waits for them, and re-layouts: 2.98 us -> 4.42 us
    all_to_all x2 -> x1, waiting for transfers between devices: 8.26 us -> 0.01 us  [to_all(): lax.all_to_all(blocks, 'query', split_axis=0, concat_axis=0, tiled=True)]
    ppermute x7 -> x10, starting transfers between devices: 9.38 us -> 15 us  [swap(): return lax.ppermute(values, 'query', [(i, i ^ bit) for i in range(count)])]
    all_to_all x2 -> x1, starting transfers between devices: 7.93 us -> 3.91 us  [to_all(): lax.all_to_all(blocks, 'query', split_axis=0, concat_axis=0, tiled=True)]
    ppermute x7 -> x10, waiting for transfers between devices: 9.51 us -> 13.5 us  [swap(): return lax.ppermute(values, 'query', [(i, i ^ bit) for i in range(count)])]
    pallas_call x1, Pallas kernels: 19.1 us -> 16.1 us  [tail(): pl.pallas_call(tail_kernel, in_specs=[pl.BlockSpec(memory_space=pltpu.SME...]
    concatenate x1, local copies, waits for them, and re-layouts: 0.02 us -> 0.97 us  [one_head_each(): out_0 = jnp.concatenate([out, after(out_swapped, queries)], axis=0)]
    unnamed x36 -> x28, local copies, waits for them, and re-layouts: 2.24 us -> 2.73 us
  transfers between devices with their start and end apart: 9 -> 11, of which waited for: 4 -> 6; matrix products, arithmetic and copies ran while one was open for 2% -> 6% of each run, Pallas kernels for 16% -> 16%
where the time goes in v3:
time: 65.6 us; the launch traced here: 65.3 us
  Pallas kernels  26.9 us (41%)
  starting transfers between devices  18.9 us (29%)
  waiting for transfers between devices  13.5 us (21%)
  local copies, waits for them, and re-layouts  4.42 us (7%)
  between operations  0.91 us (1%)
  other arithmetic  0.68 us (1%)
    pallas_call x1, Pallas kernels, tail(): pl.pallas_call(tail_kernel, in_specs=[pl.BlockSpec(memory_space=pltpu.SME...  16.1 us
    ppermute x10, starting transfers between devices, swap(): return lax.ppermute(values, 'query', [(i, i ^ bit) for i in range(count)])  15 us
    ppermute x10, waiting for transfers between devices, swap(): return lax.ppermute(values, 'query', [(i, i ^ bit) for i in range(count)])  13.5 us
    pallas_call x1, Pallas kernels, point_queries(): pl.pallas_call(point_query_kernel, grid=(points // POINT_BLOCK,), in_spec...  5.55 us
    all_to_all x1, starting transfers between devices, to_all(): lax.all_to_all(blocks, 'query', split_axis=0, concat_axis=0, tiled=True)  3.91 us
    unnamed x28, local copies, waits for them, and re-layouts  2.73 us
    pallas_call x1, Pallas kernels, pack(): pl.pallas_call(pack_kernel, out_shape=jax.ShapeDtypeStruct((HEADS, depth,...  2.02 us
    pallas_call x1, Pallas kernels, point_norms(): pl.pallas_call(point_norm_kernel, out_shape=jax.ShapeDtypeStruct((points,...  1.58 us
  transfers between devices with their start and end apart: 11, of which 6 were waited for; matrix products, arithmetic and copies ran while one was open for 6% of the time, Pallas kernels for 16%

profile of v3, /device:TPU:0, one launch (start us, length us, event | category | flops | bytes accessed | tf_op | source)
XLA Modules:
  0.0 65.3 jit_solution(7516667622618595474)
XLA Ops:
  0.6 0.0 copy-start.10
  0.6 0.0 copy-start.12
  0.7 0.0 copy-start.11
  0.7 0.0 copy-start.6
  0.7 4.1 %collective-permute-start = (bf16[64,1024]{1,0:T(8,128)(2,1)}, bf16[64,1024]{1,0:T(8,128)(2,1)S(1)}, u32[]{:S(2)}, u32[]{:S(2)}) collective-permute-start(bf16[64,1024]{1,0:T(8,128)(2,1)} %param.16), channel_id=1, source_target_pairs={{0,8},{1,9},{2,10},{3,11},{4,12},{5,13},{6,14},{7,15},{8,0},{9,1},... | collective-permute-start | bytes 393224 | tf_op jit(solution)/shard_map/ppermute | solution.py:339
  4.8 2.0 %pack.1 = bf16[16,160,128]{2,1,0:T(8,128)(2,1)} custom-call(bf16[3,64,1024]{2,1,0:T(8,128)(2,1)} %w_ref.1, bf16[16,1024]{1,0:T(8,128)(2,1)} %latents_ref.1), custom_call_target="tpu_custom_call" | custom-call | tf_op jit(solution)/shard_map/pack/pallas_call | solution.py:154
  6.8 3.9 %all-to-all-start = ((bf16[16,160,128]{2,1,0:T(8,128)(2,1)}), bf16[16,160,128]{2,1,0:T(8,128)(2,1)S(1)}, u32[]{:S(2)}, u32[]{:S(2)}) async-start(bf16[16,160,128]{2,1,0:T(8,128)(2,1)} %pack.1), calls=%async_computation | async-start | bytes 1310720 | tf_op jit(solution)/shard_map/all_to_all | solution.py:343
  10.8 0.1 and_select_fusion
  10.9 0.1 mul.47
  11.0 0.0 copy-done.10
  11.0 0.7 %constant_dynamic-update-slice_fusion.4 = (bf16[256,1024]{1,0:T(8,128)(2,1)S(1)}, bf16[128,1024]{1,0:T(8,128)(2,1)}) fusion(bf16[64,1024]{1,0:T(8,128)(2,1)S(1)} %copy-done.10), kind=kLoop, calls=%fused_computation.29 | loop fusion | bytes 393216
  11.7 0.0 collective-permute-done
  11.7 0.7 %constant_dynamic-update-slice_fusion.3 = (bf16[256,1024]{1,0:T(8,128)(2,1)S(1)}, bf16[128,1024]{1,0:T(8,128)(2,1)}) fusion(bf16[256,1024]{1,0:T(8,128)(2,1)S(1)} %get-tuple-element.30, bf16[64,1024]{1,0:T(8,128)(2,1)S(1)} %collective-permute-done, bf16[128,1024]{1,0:T(8,128)(2,1)} %get-tuple-element.31), kind=kLoop, calls=%fused_computation.28 | loop fusion | bytes 393216
  12.3 1.9 %collective-permute-start.1 = (bf16[128,1024]{1,0:T(8,128)(2,1)}, bf16[128,1024]{1,0:T(8,128)(2,1)}, u32[]{:S(2)}, u32[]{:S(2)}) collective-permute-start(bf16[128,1024]{1,0:T(8,128)(2,1)} %get-tuple-element.29), channel_id=1, source_target_pairs={{0,2},{1,3},{2,0},{3,1},{4,6},{5,7},{6,4},{7,5},{8,10},{9,11},{10,... | collective-permute-start | bytes 786440 | tf_op jit(solution)/shard_map/ppermute | solution.py:339
  14.3 0.4 fusion.7
  14.7 0.0 copy-done.12
  14.7 0.0 copy-done.11
  14.7 0.6 pad.13.w_sdf_ref
  15.4 0.1 pad_add_fusion.place_ref
  15.5 0.0 copy-done.6
  15.5 1.6 %point_norms.1.normed_ref = bf16[1024,1024]{1,0:T(8,128)(2,1)S(1)} custom-call(bf16[64,1024]{1,0:T(8,128)(2,1)S(1)} %fusion.4.features_ref, bf16[64,1024]{1,0:T(8,128)(2,1)S(1)} %pad.12.w_embed_ref, f32[1,1024]{1,0:T(1,128)S(1)} %bitcast.17), custom_call_target="tpu_custom_call" | custom-call | flops 1024 | bytes 1024 | tf_op jit(solution)/shard_map/point_norms/pallas_call | solution.py:191
  17.1 0.0 copy-start.1
  17.1 1.3 %copy-done.1 = bf16[1024,1024]{1,0:T(8,128)(2,1)} copy-done((bf16[1024,1024]{1,0:T(8,128)(2,1)}, bf16[1024,1024]{1,0:T(8,128)(2,1)S(1)}, u32[]{:S(2)}) %copy-start.1) | copy-done | bytes 2097176
  18.4 0.0 copy-start.4
  18.4 5.5 %point_queries.1.queries_ref = bf16[1024,1024]{1,0:T(8,128)(2,1)} custom-call(bf16[1024,1024]{1,0:T(8,128)(2,1)} %copy-done.1, bf16[1024,1024]{1,0:T(8,128)(2,1)} %w_query_ref.1), custom_call_target="tpu_custom_call" | custom-call | flops 1024 | bytes 1024 | tf_op jit(solution)/shard_map/point_queries/pallas_call | solution.py:206
  23.9 0.9 %collective-permute-done.1 = bf16[128,1024]{1,0:T(8,128)(2,1)} collective-permute-done((bf16[128,1024]{1,0:T(8,128)(2,1)}, bf16[128,1024]{1,0:T(8,128)(2,1)}, u32[]{:S(2)}, u32[]{:S(2)}) %collective-permute-start.1) | collective-permute-done | bytes 262176 | tf_op jit(solution)/shard_map/ppermute | solution.py:339
  24.8 1.0 %constant_dynamic-update-slice_fusion.2.out_0_ref = bf16[256,1024]{1,0:T(8,128)(2,1)S(1)} fusion(bf16[256,1024]{1,0:T(8,128)(2,1)S(1)} %get-tuple-element.28, bf16[128,1024]{1,0:T(8,128)(2,1)} %collective-permute-done.1), kind=kLoop, calls=%fused_computation.27 | loop fusion | bytes 524288 | tf_op jit(solution)/shard_map/concatenate | solution.py:367
  25.8 0.0 copy-start.7
  25.8 2.5 %collective-permute-start.7 = (bf16[256,1024]{1,0:T(8,128)(2,1)S(1)}, bf16[256,1024]{1,0:T(8,128)(2,1)}, u32[]{:S(2)}, u32[]{:S(2)}) collective-permute-start(bf16[256,1024]{1,0:T(8,128)(2,1)S(1)} %constant_dynamic-update-slice_fusion.2.out_0_ref), channel_id=1, source_target_pairs={{0,4},{1,5},{2,6},{3,7},{4,0},{5,1},{6,2},{7,3},{8,12},{9,13},{10,... | collective-permute-start | bytes 1572872 | tf_op jit(solution)/shard_map/ppermute | solution.py:339
  28.4 0.0 all-to-all-done.received_ref
  28.4 0.0 copy-start.2
  28.4 0.0 copy-start.3
  28.4 0.0 copy-start
  28.4 0.0 copy-start.5
  28.5 0.0 copy-start.8
  28.5 0.0 copy-start.9
  28.5 0.1 collective-permute-start.2
  28.6 1.5 %collective-permute-done.2.other_ref = bf16[256,512]{1,0:T(8,128)(2,1)S(1)} collective-permute-done((bf16[256,512]{1,0:T(8,128)(2,1)S(1)}, bf16[256,512]{1,0:T(8,128)(2,1)S(1)}, u32[]{:S(2)}, u32[]{:S(2)}) %collective-permute-start.2) | collective-permute-done | bytes 262176 | tf_op jit(solution)/shard_map/ppermute | solution.py:339
  30.1 0.0 copy-done.7
  30.1 1.6 %self_attention.1 = bf16[64,256]{1,0:T(8,128)(2,1)S(1)} custom-call(s32[2]{0:T(128)S(1)} %pad_add_fusion.place_ref, bf16[16,160,128]{2,1,0:T(8,128)(2,1)S(1)} %all-to-all-done.received_ref, bf16[256,512]{1,0:T(8,128)(2,1)S(1)} %unpack.1.own_ref, bf16[256,512]{1,0:T(8,128)(2,1)S(1)} %collective-permute-done.2.other_ref, f32[1,1024]{1,0:T(1,128)S(1)} %bitcast.18), custom_call_target="tpu_custom_call" | custom-call | tf_op jit(solution)/shard_map/self_attention/pallas_call | solution.py:243
  31.7 0.6 collective-permute-start.3
  32.3 3.4 %collective-permute-done.3 = bf16[64,256]{1,0:T(8,128)(2,1)S(1)} collective-permute-done((bf16[64,256]{1,0:T(8,128)(2,1)S(1)}, bf16[64,256]{1,0:T(8,128)(2,1)S(1)}, u32[]{:S(2)}, u32[]{:S(2)}) %collective-permute-start.3) | collective-permute-done | bytes 32800 | tf_op jit(solution)/shard_map/ppermute | solution.py:339
  35.6 3.0 %collective-permute-start.4 = (bf16[128,256]{1,0:T(8,128)(2,1)S(1)}, bf16[128,256]{1,0:T(8,128)(2,1)S(1)}, u32[]{:S(2)}, u32[]{:S(2)}) collective-permute-start(bf16[128,256]{1,0:T(8,128)(2,1)S(1)} %pad_maximum_fusion.2), channel_id=1, source_target_pairs={{0,8},{1,9},{2,10},{3,11},{4,12},{5,13},{6,14},{7,15},{8,0},{9,1},... | collective-permute-start | bytes 196616 | tf_op jit(solution)/shard_map/ppermute | solution.py:339
  38.6 2.8 %collective-permute-done.7.out_1_ref = bf16[256,1024]{1,0:T(8,128)(2,1)} collective-permute-done((bf16[256,1024]{1,0:T(8,128)(2,1)S(1)}, bf16[256,1024]{1,0:T(8,128)(2,1)}, u32[]{:S(2)}, u32[]{:S(2)}) %collective-permute-start.7) | collective-permute-done | bytes 524320 | tf_op jit(solution)/shard_map/ppermute | solution.py:339
  41.5 0.0 collective-permute-start.9
  41.5 0.5 collective-permute-start.8
  42.0 0.0 collective-permute-done.4
  42.0 2.2 %collective-permute-start.5 = (bf16[256,256]{1,0:T(8,128)(2,1)S(1)}, bf16[256,256]{1,0:T(8,128)(2,1)S(1)}, u32[]{:S(2)}, u32[]{:S(2)}) collective-permute-start(bf16[256,256]{1,0:T(8,128)(2,1)S(1)} %pad_maximum_fusion.1), channel_id=1, source_target_pairs={{0,4},{1,5},{2,6},{3,7},{4,0},{5,1},{6,2},{7,3},{8,12},{9,13},{10,... | collective-permute-start | bytes 393224 | tf_op jit(solution)/shard_map/ppermute | solution.py:339
  44.2 3.3 %collective-permute-done.5 = bf16[256,256]{1,0:T(8,128)(2,1)S(1)} collective-permute-done((bf16[256,256]{1,0:T(8,128)(2,1)S(1)}, bf16[256,256]{1,0:T(8,128)(2,1)S(1)}, u32[]{:S(2)}, u32[]{:S(2)}) %collective-permute-start.5) | collective-permute-done | bytes 131104 | tf_op jit(solution)/shard_map/ppermute | solution.py:339
  47.5 0.1 collective-permute-start.6
  47.6 0.0 collective-permute-done.9.out_3_ref
  47.6 0.0 collective-permute-done.8.out_2_ref
  47.6 1.5 %collective-permute-done.6.far_ref = bf16[512,256]{1,0:T(8,128)(2,1)S(1)} collective-permute-done((bf16[512,256]{1,0:T(8,128)(2,1)S(1)}, bf16[512,256]{1,0:T(8,128)(2,1)S(1)}, u32[]{:S(2)}, u32[]{:S(2)}) %collective-permute-start.6) | collective-permute-done | bytes 262176 | tf_op jit(solution)/shard_map/ppermute | solution.py:339
  49.1 0.0 copy-done.4
  49.1 0.0 copy-done.2
  49.1 0.0 copy-done.3
  49.1 0.0 copy-done
  49.1 0.0 copy-done.5
  49.1 0.0 copy-done.8
  49.1 0.0 copy-done.9
  49.2 16.1 %tail.1 = (bf16[16,1024]{1,0:T(8,128)(2,1)}, f32[1,1024]{1,0:T(1,128)}) custom-call(s32[2]{0:T(128)S(1)} %pad_add_fusion.place_ref, bf16[512,256]{1,0:T(8,128)(2,1)S(1)} %pad_maximum_fusion.near_ref, bf16[512,256]{1,0:T(8,128)(2,1)S(1)} %collective-permute-done.6.far_ref, bf16[256,1024]{1,0:T(8,128)(2,1)S(1)} %constant_dynamic-update-slice_fusion.2.out_0_ref, ...), custom_call_target="tpu_custom_call" | custom-call | tf_op jit(solution)/shard_map/tail/pallas_call | solution.py:313
  (11 shorter events, 0.2 us)
Async XLA Ops:
  0.6 10.3 %copy-start.10 = (bf16[64,1024]{1,0:T(8,128)(2,1)S(1)}, bf16[64,1024]{1,0:T(8,128)(2,1)}, u32[]{:S(2)}) copy-start(bf16[64,1024]{1,0:T(8,128)(2,1)} %param.16) | copy-start | bytes 393220
  0.6 14.0 %copy-start.12 = (bf16[1024]{0:T(1024)(128)(2,1)S(1)}, bf16[1024]{0:T(1024)(128)(2,1)}, u32[]{:S(2)}) copy-start(bf16[1024]{0:T(1024)(128)(2,1)} %param.25) | copy-start | bytes 6148
  0.7 14.1 %copy-start.11 = (bf16[51,1024]{1,0:T(8,128)(2,1)S(1)}, bf16[51,1024]{1,0:T(8,128)(2,1)}, u32[]{:S(2)}) copy-start(bf16[51,1024]{1,0:T(8,128)(2,1)} %param.19) | copy-start | bytes 313348
  0.7 14.8 %copy-start.6 = (f32[1024]{0:T(1024)S(1)}, f32[1024]{0:T(1024)}, u32[]{:S(2)}) copy-start(f32[1024]{0:T(1024)} %param.20) | copy-start | bytes 12292
  0.7 11.0 %collective-permute-start = (bf16[64,1024]{1,0:T(8,128)(2,1)}, bf16[64,1024]{1,0:T(8,128)(2,1)S(1)}, u32[]{:S(2)}, u32[]{:S(2)}) collective-permute-start(bf16[64,1024]{1,0:T(8,128)(2,1)} %param.16), channel_id=1, source_target_pairs={{0,8},{1,9},{2,10},{3,11},{4,12},{5,13},{6,14},{7,15},{8,0},{9,1},... | collective-permute-start | bytes 393224 | tf_op jit(solution)/shard_map/ppermute | solution.py:339
  6.8 21.6 %all-to-all-start = ((bf16[16,160,128]{2,1,0:T(8,128)(2,1)}), bf16[16,160,128]{2,1,0:T(8,128)(2,1)S(1)}, u32[]{:S(2)}, u32[]{:S(2)}) async-start(bf16[16,160,128]{2,1,0:T(8,128)(2,1)} %pack.1), calls=%async_computation | async-start | bytes 1310720 | tf_op jit(solution)/shard_map/all_to_all | solution.py:343
  12.3 12.5 %collective-permute-start.1 = (bf16[128,1024]{1,0:T(8,128)(2,1)}, bf16[128,1024]{1,0:T(8,128)(2,1)}, u32[]{:S(2)}, u32[]{:S(2)}) collective-permute-start(bf16[128,1024]{1,0:T(8,128)(2,1)} %get-tuple-element.29), channel_id=1, source_target_pairs={{0,2},{1,3},{2,0},{3,1},{4,6},{5,7},{6,4},{7,5},{8,10},{9,11},{10,... | collective-permute-start | bytes 786440 | tf_op jit(solution)/shard_map/ppermute | solution.py:339
  17.1 1.3 %copy-start.1 = (bf16[1024,1024]{1,0:T(8,128)(2,1)}, bf16[1024,1024]{1,0:T(8,128)(2,1)S(1)}, u32[]{:S(2)}) copy-start(bf16[1024,1024]{1,0:T(8,128)(2,1)S(1)} %point_norms.1.normed_ref) | copy-start | bytes 6291460
  18.4 30.7 %copy-start.4 = (bf16[1024,1024]{1,0:T(8,128)(2,1)S(1)}, bf16[1024,1024]{1,0:T(8,128)(2,1)}, u32[]{:S(2)}) copy-start(bf16[1024,1024]{1,0:T(8,128)(2,1)} %w_hidden_ref.1) | copy-start | bytes 6291460
  25.8 4.3 %copy-start.7 = (f32[1024]{0:T(1024)S(1)}, f32[1024]{0:T(1024)}, u32[]{:S(2)}) copy-start(f32[1024]{0:T(1024)} %param.14) | copy-start | bytes 12292
  25.8 15.7 %collective-permute-start.7 = (bf16[256,1024]{1,0:T(8,128)(2,1)S(1)}, bf16[256,1024]{1,0:T(8,128)(2,1)}, u32[]{:S(2)}, u32[]{:S(2)}) collective-permute-start(bf16[256,1024]{1,0:T(8,128)(2,1)S(1)} %constant_dynamic-update-slice_fusion.2.out_0_ref), channel_id=1, source_target_pairs={{0,4},{1,5},{2,6},{3,7},{4,0},{5,1},{6,2},{7,3},{8,12},{9,13},{10,... | collective-permute-start | bytes 1572872 | tf_op jit(solution)/shard_map/ppermute | solution.py:339
  28.4 20.7 %copy-start.2 = (bf16[2,1024,1024]{2,1,0:T(8,128)(2,1)S(1)}, bf16[2,1024,1024]{2,1,0:T(8,128)(2,1)}, u32[]{:S(2)}) copy-start(bf16[2,1024,1024]{2,1,0:T(8,128)(2,1)} %w_kv_ref.1) | copy-start | bytes 12582916
  28.4 20.7 %copy-start.3 = (bf16[1024,1024]{1,0:T(8,128)(2,1)S(1)}, bf16[1024,1024]{1,0:T(8,128)(2,1)}, u32[]{:S(2)}) copy-start(bf16[1024,1024]{1,0:T(8,128)(2,1)} %w_back_ref.1) | copy-start | bytes 6291460
  28.4 20.7 %copy-start = (bf16[1024,1024]{1,0:T(8,128)(2,1)S(1)}, bf16[1024,1024]{1,0:T(8,128)(2,1)}, u32[]{:S(2)}) copy-start(bf16[1024,1024]{1,0:T(8,128)(2,1)} %point_queries.1.queries_ref) | copy-start | bytes 6291460
  28.4 20.7 %copy-start.5 = (bf16[16,1024]{1,0:T(8,128)(2,1)S(1)}, bf16[16,1024]{1,0:T(8,128)(2,1)}, u32[]{:S(2)}) copy-start(bf16[16,1024]{1,0:T(8,128)(2,1)} %pad.13.w_sdf_ref) | copy-start | bytes 98308
  28.5 20.7 %copy-start.8 = (f32[1024]{0:T(1024)S(1)}, f32[1024]{0:T(1024)}, u32[]{:S(2)}) copy-start(f32[1024]{0:T(1024)} %param.17) | copy-start | bytes 12292
  28.5 20.7 %copy-start.9 = (f32[1024]{0:T(1024)S(1)}, f32[1024]{0:T(1024)}, u32[]{:S(2)}) copy-start(f32[1024]{0:T(1024)} %param.23) | copy-start | bytes 12292
  28.5 1.6 %collective-permute-start.2 = (bf16[256,512]{1,0:T(8,128)(2,1)S(1)}, bf16[256,512]{1,0:T(8,128)(2,1)S(1)}, u32[]{:S(2)}, u32[]{:S(2)}) collective-permute-start(bf16[256,512]{1,0:T(8,128)(2,1)S(1)} %unpack.1.own_ref), channel_id=1, source_target_pairs={{0,1},{1,0},{2,3},{3,2},{4,5},{5,4},{6,7},{7,6},{8,9},{9,8},{10,11... | collective-permute-start | bytes 786440 | tf_op jit(solution)/shard_map/ppermute | solution.py:339
  31.7 4.0 %collective-permute-start.3 = (bf16[64,256]{1,0:T(8,128)(2,1)S(1)}, bf16[64,256]{1,0:T(8,128)(2,1)S(1)}, u32[]{:S(2)}, u32[]{:S(2)}) collective-permute-start(bf16[64,256]{1,0:T(8,128)(2,1)S(1)} %self_attention.1), channel_id=1, source_target_pairs={{0,2},{1,3},{2,0},{3,1},{4,6},{5,7},{6,4},{7,5},{8,10},{9,11},{10,... | collective-permute-start | bytes 98312 | tf_op jit(solution)/shard_map/ppermute | solution.py:339
  35.6 6.4 %collective-permute-start.4 = (bf16[128,256]{1,0:T(8,128)(2,1)S(1)}, bf16[128,256]{1,0:T(8,128)(2,1)S(1)}, u32[]{:S(2)}, u32[]{:S(2)}) collective-permute-start(bf16[128,256]{1,0:T(8,128)(2,1)S(1)} %pad_maximum_fusion.2), channel_id=1, source_target_pairs={{0,8},{1,9},{2,10},{3,11},{4,12},{5,13},{6,14},{7,15},{8,0},{9,1},... | collective-permute-start | bytes 196616 | tf_op jit(solution)/shard_map/ppermute | solution.py:339
  41.5 6.1 %collective-permute-start.9 = (bf16[256,1024]{1,0:T(8,128)(2,1)}, bf16[256,1024]{1,0:T(8,128)(2,1)S(1)}, u32[]{:S(2)}, u32[]{:S(2)}) collective-permute-start(bf16[256,1024]{1,0:T(8,128)(2,1)} %collective-permute-done.7.out_1_ref), channel_id=1, source_target_pairs={{0,1},{1,0},{2,3},{3,2},{4,5},{5,4},{6,7},{7,6},{8,9},{9,8},{10,11... | collective-permute-start | bytes 1572872 | tf_op jit(solution)/shard_map/ppermute | solution.py:339
  41.5 6.1 %collective-permute-start.8 = (bf16[256,1024]{1,0:T(8,128)(2,1)S(1)}, bf16[256,1024]{1,0:T(8,128)(2,1)S(1)}, u32[]{:S(2)}, u32[]{:S(2)}) collective-permute-start(bf16[256,1024]{1,0:T(8,128)(2,1)S(1)} %constant_dynamic-update-slice_fusion.2.out_0_ref), channel_id=1, source_target_pairs={{0,1},{1,0},{2,3},{3,2},{4,5},{5,4},{6,7},{7,6},{8,9},{9,8},{10,11... | collective-permute-start | bytes 1572872 | tf_op jit(solution)/shard_map/ppermute | solution.py:339
  42.0 5.5 %collective-permute-start.5 = (bf16[256,256]{1,0:T(8,128)(2,1)S(1)}, bf16[256,256]{1,0:T(8,128)(2,1)S(1)}, u32[]{:S(2)}, u32[]{:S(2)}) collective-permute-start(bf16[256,256]{1,0:T(8,128)(2,1)S(1)} %pad_maximum_fusion.1), channel_id=1, source_target_pairs={{0,4},{1,5},{2,6},{3,7},{4,0},{5,1},{6,2},{7,3},{8,12},{9,13},{10,... | collective-permute-start | bytes 393224 | tf_op jit(solution)/shard_map/ppermute | solution.py:339
  47.5 1.6 %collective-permute-start.6 = (bf16[512,256]{1,0:T(8,128)(2,1)S(1)}, bf16[512,256]{1,0:T(8,128)(2,1)S(1)}, u32[]{:S(2)}, u32[]{:S(2)}) collective-permute-start(bf16[512,256]{1,0:T(8,128)(2,1)S(1)} %pad_maximum_fusion.near_ref), channel_id=1, source_target_pairs={{0,1},{1,0},{2,3},{3,2},{4,5},{5,4},{6,7},{7,6},{8,9},{9,8},{10,11... | collective-permute-start | bytes 786440 | tf_op jit(solution)/shard_map/ppermute | solution.py:339

commit v4 on v3

--- a/solution.py
+++ b/solution.py
@@ -281,7 +281,9 @@
         zero = jnp.zeros_like(both)
         key_pairs[pair, :key_count, :] = jnp.where(lane < HEAD_DIM, both, zero)
         key_pairs[pair, key_count:, :] = jnp.where(lane < HEAD_DIM, zero, both)
-    values = dot_nn(normed, w_kv_ref[1]).T.astype(jnp.bfloat16)
+    values = lax.dot_general(
+        w_kv_ref[1], normed, (((0,), (1,)), ((), ())), preferred_element_type=jnp.float32
+    ).astype(jnp.bfloat16)
     for head in range(HEADS):
         value_rows[head, :HEAD_DIM, :] = values[HEAD_DIM * head : HEAD_DIM * head + HEAD_DIM, :]
         value_rows[head, HEAD_DIM:, :] = jnp.ones((16, key_count), jnp.bfloat16)

time: 65.6 us -> 64.5 us (0.983)
  Pallas kernels: 26.9 us -> 25.8 us
    pallas_call x1, Pallas kernels: 16.1 us -> 15.1 us  [tail(): pl.pallas_call(tail_kernel, in_specs=[pl.BlockSpec(memory_space=pltpu.SME...]
  transfers between devices with their start and end apart: 11 -> 11, of which waited for: 6 -> 6; matrix products, arithmetic and copies ran while one was open for 6% -> 6% of each run, Pallas kernels for 16% -> 17%
where the time goes in v4:
time: 64.5 us; the launch traced here: 64.2 us
  Pallas kernels  25.8 us (40%)
  starting transfers between devices  18.9 us (29%)
  waiting for transfers between devices  13.5 us (21%)
  local copies, waits for them, and re-layouts  4.42 us (7%)
  between operations  0.91 us (1%)
  other arithmetic  0.68 us (1%)
    pallas_call x1, Pallas kernels, tail(): pl.pallas_call(tail_kernel, in_specs=[pl.BlockSpec(memory_space=pltpu.SME...  15.1 us
    ppermute x10, starting transfers between devices, swap(): return lax.ppermute(values, 'query', [(i, i ^ bit) for i in range(count)])  15 us
    ppermute x10, waiting for transfers between devices, swap(): return lax.ppermute(values, 'query', [(i, i ^ bit) for i in range(count)])  13.5 us
    pallas_call x1, Pallas kernels, point_queries(): pl.pallas_call(point_query_kernel, grid=(points // POINT_BLOCK,), in_spec...  5.55 us
    all_to_all x1, starting transfers between devices, to_all(): lax.all_to_all(blocks, 'query', split_axis=0, concat_axis=0, tiled=True)  3.91 us
    unnamed x28, local copies, waits for them, and re-layouts  2.73 us
    pallas_call x1, Pallas kernels, pack(): pl.pallas_call(pack_kernel, out_shape=jax.ShapeDtypeStruct((HEADS, depth,...  2.02 us
    pallas_call x1, Pallas kernels, point_norms(): pl.pallas_call(point_norm_kernel, out_shape=jax.ShapeDtypeStruct((points,...  1.58 us
  transfers between devices with their start and end apart: 11, of which 6 were waited for; matrix products, arithmetic and copies ran while one was open for 6% of the time, Pallas kernels for 17%

profile of v4, /device:TPU:0, one launch (start us, length us, event | category | flops | bytes accessed | tf_op | source)
XLA Modules:
  0.0 64.2 jit_solution(7445055270169938109)
XLA Ops:
  0.6 0.0 copy-start.10
  0.6 0.0 copy-start.12
  0.7 0.0 copy-start.11
  0.7 0.0 copy-start.6
  0.7 4.1 %collective-permute-start = (bf16[64,1024]{1,0:T(8,128)(2,1)}, bf16[64,1024]{1,0:T(8,128)(2,1)S(1)}, u32[]{:S(2)}, u32[]{:S(2)}) collective-permute-start(bf16[64,1024]{1,0:T(8,128)(2,1)} %param.16), channel_id=1, source_target_pairs={{0,8},{1,9},{2,10},{3,11},{4,12},{5,13},{6,14},{7,15},{8,0},{9,1},... | collective-permute-start | bytes 393224 | tf_op jit(solution)/shard_map/ppermute | solution.py:341
  4.8 2.0 %pack.1 = bf16[16,160,128]{2,1,0:T(8,128)(2,1)} custom-call(bf16[3,64,1024]{2,1,0:T(8,128)(2,1)} %w_ref.1, bf16[16,1024]{1,0:T(8,128)(2,1)} %latents_ref.1), custom_call_target="tpu_custom_call" | custom-call | tf_op jit(solution)/shard_map/pack/pallas_call | solution.py:154
  6.8 3.9 %all-to-all-start = ((bf16[16,160,128]{2,1,0:T(8,128)(2,1)}), bf16[16,160,128]{2,1,0:T(8,128)(2,1)S(1)}, u32[]{:S(2)}, u32[]{:S(2)}) async-start(bf16[16,160,128]{2,1,0:T(8,128)(2,1)} %pack.1), calls=%async_computation | async-start | bytes 1310720 | tf_op jit(solution)/shard_map/all_to_all | solution.py:345
  10.8 0.1 and_select_fusion
  10.9 0.1 mul.47
  11.0 0.0 copy-done.10
  11.0 0.7 %constant_dynamic-update-slice_fusion.4 = (bf16[256,1024]{1,0:T(8,128)(2,1)S(1)}, bf16[128,1024]{1,0:T(8,128)(2,1)}) fusion(bf16[64,1024]{1,0:T(8,128)(2,1)S(1)} %copy-done.10), kind=kLoop, calls=%fused_computation.29 | loop fusion | bytes 393216
  11.7 0.0 collective-permute-done
  11.7 0.7 %constant_dynamic-update-slice_fusion.3 = (bf16[256,1024]{1,0:T(8,128)(2,1)S(1)}, bf16[128,1024]{1,0:T(8,128)(2,1)}) fusion(bf16[256,1024]{1,0:T(8,128)(2,1)S(1)} %get-tuple-element.30, bf16[64,1024]{1,0:T(8,128)(2,1)S(1)} %collective-permute-done, bf16[128,1024]{1,0:T(8,128)(2,1)} %get-tuple-element.31), kind=kLoop, calls=%fused_computation.28 | loop fusion | bytes 393216
  12.3 1.9 %collective-permute-start.1 = (bf16[128,1024]{1,0:T(8,128)(2,1)}, bf16[128,1024]{1,0:T(8,128)(2,1)}, u32[]{:S(2)}, u32[]{:S(2)}) collective-permute-start(bf16[128,1024]{1,0:T(8,128)(2,1)} %get-tuple-element.29), channel_id=1, source_target_pairs={{0,2},{1,3},{2,0},{3,1},{4,6},{5,7},{6,4},{7,5},{8,10},{9,11},{10,... | collective-permute-start | bytes 786440 | tf_op jit(solution)/shard_map/ppermute | solution.py:341
  14.3 0.4 fusion.7
  14.7 0.0 copy-done.12
  14.7 0.0 copy-done.11
  14.7 0.6 pad.13.w_sdf_ref
  15.4 0.1 pad_add_fusion.place_ref
  15.5 0.0 copy-done.6
  15.5 1.6 %point_norms.1.normed_ref = bf16[1024,1024]{1,0:T(8,128)(2,1)S(1)} custom-call(bf16[64,1024]{1,0:T(8,128)(2,1)S(1)} %fusion.4.features_ref, bf16[64,1024]{1,0:T(8,128)(2,1)S(1)} %pad.12.w_embed_ref, f32[1,1024]{1,0:T(1,128)S(1)} %bitcast.17), custom_call_target="tpu_custom_call" | custom-call | flops 1024 | bytes 1024 | tf_op jit(solution)/shard_map/point_norms/pallas_call | solution.py:191
  17.1 0.0 copy-start.1
  17.1 1.3 %copy-done.1 = bf16[1024,1024]{1,0:T(8,128)(2,1)} copy-done((bf16[1024,1024]{1,0:T(8,128)(2,1)}, bf16[1024,1024]{1,0:T(8,128)(2,1)S(1)}, u32[]{:S(2)}) %copy-start.1) | copy-done | bytes 2097176
  18.4 0.0 copy-start.4
  18.4 5.5 %point_queries.1.queries_ref = bf16[1024,1024]{1,0:T(8,128)(2,1)} custom-call(bf16[1024,1024]{1,0:T(8,128)(2,1)} %copy-done.1, bf16[1024,1024]{1,0:T(8,128)(2,1)} %w_query_ref.1), custom_call_target="tpu_custom_call" | custom-call | flops 1024 | bytes 1024 | tf_op jit(solution)/shard_map/point_queries/pallas_call | solution.py:206
  23.9 0.9 %collective-permute-done.1 = bf16[128,1024]{1,0:T(8,128)(2,1)} collective-permute-done((bf16[128,1024]{1,0:T(8,128)(2,1)}, bf16[128,1024]{1,0:T(8,128)(2,1)}, u32[]{:S(2)}, u32[]{:S(2)}) %collective-permute-start.1) | collective-permute-done | bytes 262176 | tf_op jit(solution)/shard_map/ppermute | solution.py:341
  24.8 1.0 %constant_dynamic-update-slice_fusion.2.out_0_ref = bf16[256,1024]{1,0:T(8,128)(2,1)S(1)} fusion(bf16[256,1024]{1,0:T(8,128)(2,1)S(1)} %get-tuple-element.28, bf16[128,1024]{1,0:T(8,128)(2,1)} %collective-permute-done.1), kind=kLoop, calls=%fused_computation.27 | loop fusion | bytes 524288 | tf_op jit(solution)/shard_map/concatenate | solution.py:369
  25.8 0.0 copy-start.7
  25.8 2.5 %collective-permute-start.7 = (bf16[256,1024]{1,0:T(8,128)(2,1)S(1)}, bf16[256,1024]{1,0:T(8,128)(2,1)}, u32[]{:S(2)}, u32[]{:S(2)}) collective-permute-start(bf16[256,1024]{1,0:T(8,128)(2,1)S(1)} %constant_dynamic-update-slice_fusion.2.out_0_ref), channel_id=1, source_target_pairs={{0,4},{1,5},{2,6},{3,7},{4,0},{5,1},{6,2},{7,3},{8,12},{9,13},{10,... | collective-permute-start | bytes 1572872 | tf_op jit(solution)/shard_map/ppermute | solution.py:341
  28.4 0.0 all-to-all-done.received_ref
  28.4 0.0 copy-start.2
  28.4 0.0 copy-start.3
  28.4 0.0 copy-start
  28.4 0.0 copy-start.5
  28.5 0.0 copy-start.8
  28.5 0.0 copy-start.9
  28.5 0.1 collective-permute-start.2
  28.6 1.5 %collective-permute-done.2.other_ref = bf16[256,512]{1,0:T(8,128)(2,1)S(1)} collective-permute-done((bf16[256,512]{1,0:T(8,128)(2,1)S(1)}, bf16[256,512]{1,0:T(8,128)(2,1)S(1)}, u32[]{:S(2)}, u32[]{:S(2)}) %collective-permute-start.2) | collective-permute-done | bytes 262176 | tf_op jit(solution)/shard_map/ppermute | solution.py:341
  30.1 0.0 copy-done.7
  30.1 1.6 %self_attention.1 = bf16[64,256]{1,0:T(8,128)(2,1)S(1)} custom-call(s32[2]{0:T(128)S(1)} %pad_add_fusion.place_ref, bf16[16,160,128]{2,1,0:T(8,128)(2,1)S(1)} %all-to-all-done.received_ref, bf16[256,512]{1,0:T(8,128)(2,1)S(1)} %unpack.1.own_ref, bf16[256,512]{1,0:T(8,128)(2,1)S(1)} %collective-permute-done.2.other_ref, f32[1,1024]{1,0:T(1,128)S(1)} %bitcast.18), custom_call_target="tpu_custom_call" | custom-call | tf_op jit(solution)/shard_map/self_attention/pallas_call | solution.py:243
  31.7 0.6 collective-permute-start.3
  32.3 3.4 %collective-permute-done.3 = bf16[64,256]{1,0:T(8,128)(2,1)S(1)} collective-permute-done((bf16[64,256]{1,0:T(8,128)(2,1)S(1)}, bf16[64,256]{1,0:T(8,128)(2,1)S(1)}, u32[]{:S(2)}, u32[]{:S(2)}) %collective-permute-start.3) | collective-permute-done | bytes 32800 | tf_op jit(solution)/shard_map/ppermute | solution.py:341
  35.6 3.0 %collective-permute-start.4 = (bf16[128,256]{1,0:T(8,128)(2,1)S(1)}, bf16[128,256]{1,0:T(8,128)(2,1)S(1)}, u32[]{:S(2)}, u32[]{:S(2)}) collective-permute-start(bf16[128,256]{1,0:T(8,128)(2,1)S(1)} %pad_maximum_fusion.2), channel_id=1, source_target_pairs={{0,8},{1,9},{2,10},{3,11},{4,12},{5,13},{6,14},{7,15},{8,0},{9,1},... | collective-permute-start | bytes 196616 | tf_op jit(solution)/shard_map/ppermute | solution.py:341
  38.6 2.8 %collective-permute-done.7.out_1_ref = bf16[256,1024]{1,0:T(8,128)(2,1)} collective-permute-done((bf16[256,1024]{1,0:T(8,128)(2,1)S(1)}, bf16[256,1024]{1,0:T(8,128)(2,1)}, u32[]{:S(2)}, u32[]{:S(2)}) %collective-permute-start.7) | collective-permute-done | bytes 524320 | tf_op jit(solution)/shard_map/ppermute | solution.py:341
  41.5 0.0 collective-permute-start.9
  41.5 0.5 collective-permute-start.8
  42.0 0.0 collective-permute-done.4
  42.0 2.2 %collective-permute-start.5 = (bf16[256,256]{1,0:T(8,128)(2,1)S(1)}, bf16[256,256]{1,0:T(8,128)(2,1)S(1)}, u32[]{:S(2)}, u32[]{:S(2)}) collective-permute-start(bf16[256,256]{1,0:T(8,128)(2,1)S(1)} %pad_maximum_fusion.1), channel_id=1, source_target_pairs={{0,4},{1,5},{2,6},{3,7},{4,0},{5,1},{6,2},{7,3},{8,12},{9,13},{10,... | collective-permute-start | bytes 393224 | tf_op jit(solution)/shard_map/ppermute | solution.py:341
  44.2 3.3 %collective-permute-done.5 = bf16[256,256]{1,0:T(8,128)(2,1)S(1)} collective-permute-done((bf16[256,256]{1,0:T(8,128)(2,1)S(1)}, bf16[256,256]{1,0:T(8,128)(2,1)S(1)}, u32[]{:S(2)}, u32[]{:S(2)}) %collective-permute-start.5) | collective-permute-done | bytes 131104 | tf_op jit(solution)/shard_map/ppermute | solution.py:341
  47.5 0.1 collective-permute-start.6
  47.6 0.0 collective-permute-done.9.out_3_ref
  47.6 0.0 collective-permute-done.8.out_2_ref
  47.6 1.5 %collective-permute-done.6.far_ref = bf16[512,256]{1,0:T(8,128)(2,1)S(1)} collective-permute-done((bf16[512,256]{1,0:T(8,128)(2,1)S(1)}, bf16[512,256]{1,0:T(8,128)(2,1)S(1)}, u32[]{:S(2)}, u32[]{:S(2)}) %collective-permute-start.6) | collective-permute-done | bytes 262176 | tf_op jit(solution)/shard_map/ppermute | solution.py:341
  49.1 0.0 copy-done.4
  49.1 0.0 copy-done.2
  49.1 0.0 copy-done.3
  49.1 0.0 copy-done
  49.1 0.0 copy-done.5
  49.1 0.0 copy-done.8
  49.1 0.0 copy-done.9
  49.2 15.1 %tail.1 = (bf16[16,1024]{1,0:T(8,128)(2,1)}, f32[1,1024]{1,0:T(1,128)}) custom-call(s32[2]{0:T(128)S(1)} %pad_add_fusion.place_ref, bf16[512,256]{1,0:T(8,128)(2,1)S(1)} %pad_maximum_fusion.near_ref, bf16[512,256]{1,0:T(8,128)(2,1)S(1)} %collective-permute-done.6.far_ref, bf16[256,1024]{1,0:T(8,128)(2,1)S(1)} %constant_dynamic-update-slice_fusion.2.out_0_ref, ...), custom_call_target="tpu_custom_call" | custom-call | tf_op jit(solution)/shard_map/tail/pallas_call | solution.py:315
  (11 shorter events, 0.2 us)
Async XLA Ops:
  0.6 10.3 %copy-start.10 = (bf16[64,1024]{1,0:T(8,128)(2,1)S(1)}, bf16[64,1024]{1,0:T(8,128)(2,1)}, u32[]{:S(2)}) copy-start(bf16[64,1024]{1,0:T(8,128)(2,1)} %param.16) | copy-start | bytes 393220
  0.6 14.0 %copy-start.12 = (bf16[1024]{0:T(1024)(128)(2,1)S(1)}, bf16[1024]{0:T(1024)(128)(2,1)}, u32[]{:S(2)}) copy-start(bf16[1024]{0:T(1024)(128)(2,1)} %param.25) | copy-start | bytes 6148
  0.7 14.1 %copy-start.11 = (bf16[51,1024]{1,0:T(8,128)(2,1)S(1)}, bf16[51,1024]{1,0:T(8,128)(2,1)}, u32[]{:S(2)}) copy-start(bf16[51,1024]{1,0:T(8,128)(2,1)} %param.19) | copy-start | bytes 313348
  0.7 14.8 %copy-start.6 = (f32[1024]{0:T(1024)S(1)}, f32[1024]{0:T(1024)}, u32[]{:S(2)}) copy-start(f32[1024]{0:T(1024)} %param.20) | copy-start | bytes 12292
  0.7 11.0 %collective-permute-start = (bf16[64,1024]{1,0:T(8,128)(2,1)}, bf16[64,1024]{1,0:T(8,128)(2,1)S(1)}, u32[]{:S(2)}, u32[]{:S(2)}) collective-permute-start(bf16[64,1024]{1,0:T(8,128)(2,1)} %param.16), channel_id=1, source_target_pairs={{0,8},{1,9},{2,10},{3,11},{4,12},{5,13},{6,14},{7,15},{8,0},{9,1},... | collective-permute-start | bytes 393224 | tf_op jit(solution)/shard_map/ppermute | solution.py:341
  6.8 21.6 %all-to-all-start = ((bf16[16,160,128]{2,1,0:T(8,128)(2,1)}), bf16[16,160,128]{2,1,0:T(8,128)(2,1)S(1)}, u32[]{:S(2)}, u32[]{:S(2)}) async-start(bf16[16,160,128]{2,1,0:T(8,128)(2,1)} %pack.1), calls=%async_computation | async-start | bytes 1310720 | tf_op jit(solution)/shard_map/all_to_all | solution.py:345
  12.3 12.5 %collective-permute-start.1 = (bf16[128,1024]{1,0:T(8,128)(2,1)}, bf16[128,1024]{1,0:T(8,128)(2,1)}, u32[]{:S(2)}, u32[]{:S(2)}) collective-permute-start(bf16[128,1024]{1,0:T(8,128)(2,1)} %get-tuple-element.29), channel_id=1, source_target_pairs={{0,2},{1,3},{2,0},{3,1},{4,6},{5,7},{6,4},{7,5},{8,10},{9,11},{10,... | collective-permute-start | bytes 786440 | tf_op jit(solution)/shard_map/ppermute | solution.py:341
  17.1 1.3 %copy-start.1 = (bf16[1024,1024]{1,0:T(8,128)(2,1)}, bf16[1024,1024]{1,0:T(8,128)(2,1)S(1)}, u32[]{:S(2)}) copy-start(bf16[1024,1024]{1,0:T(8,128)(2,1)S(1)} %point_norms.1.normed_ref) | copy-start | bytes 6291460
  18.4 30.7 %copy-start.4 = (bf16[1024,1024]{1,0:T(8,128)(2,1)S(1)}, bf16[1024,1024]{1,0:T(8,128)(2,1)}, u32[]{:S(2)}) copy-start(bf16[1024,1024]{1,0:T(8,128)(2,1)} %w_hidden_ref.1) | copy-start | bytes 6291460
  25.8 4.3 %copy-start.7 = (f32[1024]{0:T(1024)S(1)}, f32[1024]{0:T(1024)}, u32[]{:S(2)}) copy-start(f32[1024]{0:T(1024)} %param.14) | copy-start | bytes 12292
  25.8 15.7 %collective-permute-start.7 = (bf16[256,1024]{1,0:T(8,128)(2,1)S(1)}, bf16[256,1024]{1,0:T(8,128)(2,1)}, u32[]{:S(2)}, u32[]{:S(2)}) collective-permute-start(bf16[256,1024]{1,0:T(8,128)(2,1)S(1)} %constant_dynamic-update-slice_fusion.2.out_0_ref), channel_id=1, source_target_pairs={{0,4},{1,5},{2,6},{3,7},{4,0},{5,1},{6,2},{7,3},{8,12},{9,13},{10,... | collective-permute-start | bytes 1572872 | tf_op jit(solution)/shard_map/ppermute | solution.py:341
  28.4 20.7 %copy-start.2 = (bf16[2,1024,1024]{2,1,0:T(8,128)(2,1)S(1)}, bf16[2,1024,1024]{2,1,0:T(8,128)(2,1)}, u32[]{:S(2)}) copy-start(bf16[2,1024,1024]{2,1,0:T(8,128)(2,1)} %w_kv_ref.1) | copy-start | bytes 12582916
  28.4 20.7 %copy-start.3 = (bf16[1024,1024]{1,0:T(8,128)(2,1)S(1)}, bf16[1024,1024]{1,0:T(8,128)(2,1)}, u32[]{:S(2)}) copy-start(bf16[1024,1024]{1,0:T(8,128)(2,1)} %w_back_ref.1) | copy-start | bytes 6291460
  28.4 20.7 %copy-start = (bf16[1024,1024]{1,0:T(8,128)(2,1)S(1)}, bf16[1024,1024]{1,0:T(8,128)(2,1)}, u32[]{:S(2)}) copy-start(bf16[1024,1024]{1,0:T(8,128)(2,1)} %point_queries.1.queries_ref) | copy-start | bytes 6291460
  28.4 20.7 %copy-start.5 = (bf16[16,1024]{1,0:T(8,128)(2,1)S(1)}, bf16[16,1024]{1,0:T(8,128)(2,1)}, u32[]{:S(2)}) copy-start(bf16[16,1024]{1,0:T(8,128)(2,1)} %pad.13.w_sdf_ref) | copy-start | bytes 98308
  28.5 20.7 %copy-start.8 = (f32[1024]{0:T(1024)S(1)}, f32[1024]{0:T(1024)}, u32[]{:S(2)}) copy-start(f32[1024]{0:T(1024)} %param.17) | copy-start | bytes 12292
  28.5 20.7 %copy-start.9 = (f32[1024]{0:T(1024)S(1)}, f32[1024]{0:T(1024)}, u32[]{:S(2)}) copy-start(f32[1024]{0:T(1024)} %param.23) | copy-start | bytes 12292
  28.5 1.6 %collective-permute-start.2 = (bf16[256,512]{1,0:T(8,128)(2,1)S(1)}, bf16[256,512]{1,0:T(8,128)(2,1)S(1)}, u32[]{:S(2)}, u32[]{:S(2)}) collective-permute-start(bf16[256,512]{1,0:T(8,128)(2,1)S(1)} %unpack.1.own_ref), channel_id=1, source_target_pairs={{0,1},{1,0},{2,3},{3,2},{4,5},{5,4},{6,7},{7,6},{8,9},{9,8},{10,11... | collective-permute-start | bytes 786440 | tf_op jit(solution)/shard_map/ppermute | solution.py:341
  31.7 4.0 %collective-permute-start.3 = (bf16[64,256]{1,0:T(8,128)(2,1)S(1)}, bf16[64,256]{1,0:T(8,128)(2,1)S(1)}, u32[]{:S(2)}, u32[]{:S(2)}) collective-permute-start(bf16[64,256]{1,0:T(8,128)(2,1)S(1)} %self_attention.1), channel_id=1, source_target_pairs={{0,2},{1,3},{2,0},{3,1},{4,6},{5,7},{6,4},{7,5},{8,10},{9,11},{10,... | collective-permute-start | bytes 98312 | tf_op jit(solution)/shard_map/ppermute | solution.py:341
  35.6 6.4 %collective-permute-start.4 = (bf16[128,256]{1,0:T(8,128)(2,1)S(1)}, bf16[128,256]{1,0:T(8,128)(2,1)S(1)}, u32[]{:S(2)}, u32[]{:S(2)}) collective-permute-start(bf16[128,256]{1,0:T(8,128)(2,1)S(1)} %pad_maximum_fusion.2), channel_id=1, source_target_pairs={{0,8},{1,9},{2,10},{3,11},{4,12},{5,13},{6,14},{7,15},{8,0},{9,1},... | collective-permute-start | bytes 196616 | tf_op jit(solution)/shard_map/ppermute | solution.py:341
  41.5 6.1 %collective-permute-start.9 = (bf16[256,1024]{1,0:T(8,128)(2,1)}, bf16[256,1024]{1,0:T(8,128)(2,1)S(1)}, u32[]{:S(2)}, u32[]{:S(2)}) collective-permute-start(bf16[256,1024]{1,0:T(8,128)(2,1)} %collective-permute-done.7.out_1_ref), channel_id=1, source_target_pairs={{0,1},{1,0},{2,3},{3,2},{4,5},{5,4},{6,7},{7,6},{8,9},{9,8},{10,11... | collective-permute-start | bytes 1572872 | tf_op jit(solution)/shard_map/ppermute | solution.py:341
  41.5 6.1 %collective-permute-start.8 = (bf16[256,1024]{1,0:T(8,128)(2,1)S(1)}, bf16[256,1024]{1,0:T(8,128)(2,1)S(1)}, u32[]{:S(2)}, u32[]{:S(2)}) collective-permute-start(bf16[256,1024]{1,0:T(8,128)(2,1)S(1)} %constant_dynamic-update-slice_fusion.2.out_0_ref), channel_id=1, source_target_pairs={{0,1},{1,0},{2,3},{3,2},{4,5},{5,4},{6,7},{7,6},{8,9},{9,8},{10,11... | collective-permute-start | bytes 1572872 | tf_op jit(solution)/shard_map/ppermute | solution.py:341
  42.0 5.5 %collective-permute-start.5 = (bf16[256,256]{1,0:T(8,128)(2,1)S(1)}, bf16[256,256]{1,0:T(8,128)(2,1)S(1)}, u32[]{:S(2)}, u32[]{:S(2)}) collective-permute-start(bf16[256,256]{1,0:T(8,128)(2,1)S(1)} %pad_maximum_fusion.1), channel_id=1, source_target_pairs={{0,4},{1,5},{2,6},{3,7},{4,0},{5,1},{6,2},{7,3},{8,12},{9,13},{10,... | collective-permute-start | bytes 393224 | tf_op jit(solution)/shard_map/ppermute | solution.py:341
  47.5 1.6 %collective-permute-start.6 = (bf16[512,256]{1,0:T(8,128)(2,1)S(1)}, bf16[512,256]{1,0:T(8,128)(2,1)S(1)}, u32[]{:S(2)}, u32[]{:S(2)}) collective-permute-start(bf16[512,256]{1,0:T(8,128)(2,1)S(1)} %pad_maximum_fusion.near_ref), channel_id=1, source_target_pairs={{0,1},{1,0},{2,3},{3,2},{4,5},{5,4},{6,7},{7,6},{8,9},{9,8},{10,11... | collective-permute-start | bytes 786440 | tf_op jit(solution)/shard_map/ppermute | solution.py:341

commit v5 on v4

--- a/solution.py
+++ b/solution.py
@@ -253,21 +253,23 @@
     place_ref, near_ref, far_ref, out_0_ref, out_1_ref, out_2_ref, out_3_ref, own_ref, other_ref,
     gain_cross_ref, w_kv_ref,
     queries_ref, features_ref, w_back_ref, w_embed_ref, gain_head_ref, w_hidden_ref, w_sdf_ref,
-    decoded_ref, sdf_ref, attended, all_decoded, key_pairs, value_rows, crossed,
+    decoded_ref, sdf_ref, all_decoded, key_pairs, value_rows, crossed,
 ):
     me, core = place_ref[0], place_ref[1]
-    order = [EXCHANGES.index(bit) for bit in HEAD_EXCHANGES]
-    for block in range(HEADS):
-        place = sum(1 << to for at, to in enumerate(order) if block >> at & 1)
-        side_ref = near_ref if block < HEADS // 2 else far_ref
-        row = HEAD_DIM * (block % (HEADS // 2))
-        attended[HEAD_DIM * place : HEAD_DIM * place + HEAD_DIM, :] = side_ref[
-            row : row + HEAD_DIM, :
-        ]
-    update = joined_halves(core, own_ref[...], other_ref[...]).astype(jnp.float32)
+    half_width = own_ref.shape[1]
+    for side_ref, place in ((own_ref, core), (other_ref, 1 - core)):
+        low = pl.multiple_of(half_width * place, half_width)
+        all_decoded[:, pl.ds(low, half_width)] = side_ref[...]
+    update = all_decoded[...].astype(jnp.float32)
     quarter = out_0_ref.shape[0]
     for piece, out_ref in enumerate((out_0_ref, out_1_ref, out_2_ref, out_3_ref)):
-        update += dot_tn(attended[quarter * piece : quarter * piece + quarter, :], out_ref[...])
+        side_ref = near_ref if piece < 2 else far_ref
+        low = quarter * (piece % 2)
+        heads = [
+            side_ref[low + HEAD_DIM * block : low + HEAD_DIM * block + HEAD_DIM, :]
+            for block in (0, 2, 1, 3)
+        ]
+        update += dot_tn(jnp.concatenate(heads, axis=0), out_ref[...])
     decoded = update.astype(jnp.bfloat16)
     all_decoded[...] = decoded
     rows = decoded_ref.shape[0]
@@ -323,7 +325,6 @@
             jax.ShapeDtypeStruct((1, points), jnp.float32),
         ),
         scratch_shapes=[
-            pltpu.VMEM((width, keys), jnp.bfloat16),
             pltpu.VMEM((keys, width), jnp.bfloat16),
             pltpu.VMEM((HEADS // 2, 2 * keys, 128), jnp.bfloat16),
             pltpu.VMEM((HEADS, HEAD_DIM + 16, keys), jnp.bfloat16),

time: 64.5 us -> 64.5 us (level)
  no operation moved by 1% of the time
where the time goes in v5:
time: 64.5 us; the launch traced here: 64.2 us
  Pallas kernels  25.8 us (40%)
  starting transfers between devices  18.9 us (29%)
  waiting for transfers between devices  13.5 us (21%)
  local copies, waits for them, and re-layouts  4.42 us (7%)
  between operations  0.91 us (1%)
  other arithmetic  0.68 us (1%)
    pallas_call x1, Pallas kernels, tail(): pl.pallas_call(tail_kernel, in_specs=[pl.BlockSpec(memory_space=pltpu.SME...  15.1 us
    ppermute x10, starting transfers between devices, swap(): return lax.ppermute(values, 'query', [(i, i ^ bit) for i in range(count)])  15 us
    ppermute x10, waiting for transfers between devices, swap(): return lax.ppermute(values, 'query', [(i, i ^ bit) for i in range(count)])  13.5 us
    pallas_call x1, Pallas kernels, point_queries(): pl.pallas_call(point_query_kernel, grid=(points // POINT_BLOCK,), in_spec...  5.55 us
    all_to_all x1, starting transfers between devices, to_all(): lax.all_to_all(blocks, 'query', split_axis=0, concat_axis=0, tiled=True)  3.91 us
    unnamed x28, local copies, waits for them, and re-layouts  2.73 us
    pallas_call x1, Pallas kernels, pack(): pl.pallas_call(pack_kernel, out_shape=jax.ShapeDtypeStruct((HEADS, depth,...  2.02 us
    pallas_call x1, Pallas kernels, point_norms(): pl.pallas_call(point_norm_kernel, out_shape=jax.ShapeDtypeStruct((points,...  1.58 us
  transfers between devices with their start and end apart: 11, of which 6 were waited for; matrix products, arithmetic and copies ran while one was open for 6% of the time, Pallas kernels for 17%

profile of v5, /device:TPU:0, one launch (start us, length us, event | category | flops | bytes accessed | tf_op | source)
XLA Modules:
  0.0 64.2 jit_solution(15115598660365769712)
XLA Ops:
  0.6 0.0 copy-start.10
  0.6 0.0 copy-start.12
  0.7 0.0 copy-start.11
  0.7 0.0 copy-start.6
  0.7 4.1 %collective-permute-start = (bf16[64,1024]{1,0:T(8,128)(2,1)}, bf16[64,1024]{1,0:T(8,128)(2,1)S(1)}, u32[]{:S(2)}, u32[]{:S(2)}) collective-permute-start(bf16[64,1024]{1,0:T(8,128)(2,1)} %param.16), channel_id=1, source_target_pairs={{0,8},{1,9},{2,10},{3,11},{4,12},{5,13},{6,14},{7,15},{8,0},{9,1},... | collective-permute-start | bytes 393224 | tf_op jit(solution)/shard_map/ppermute | solution.py:342
  4.8 2.0 %pack.1 = bf16[16,160,128]{2,1,0:T(8,128)(2,1)} custom-call(bf16[3,64,1024]{2,1,0:T(8,128)(2,1)} %w_ref.1, bf16[16,1024]{1,0:T(8,128)(2,1)} %latents_ref.1), custom_call_target="tpu_custom_call" | custom-call | tf_op jit(solution)/shard_map/pack/pallas_call | solution.py:154
  6.8 3.9 %all-to-all-start = ((bf16[16,160,128]{2,1,0:T(8,128)(2,1)}), bf16[16,160,128]{2,1,0:T(8,128)(2,1)S(1)}, u32[]{:S(2)}, u32[]{:S(2)}) async-start(bf16[16,160,128]{2,1,0:T(8,128)(2,1)} %pack.1), calls=%async_computation | async-start | bytes 1310720 | tf_op jit(solution)/shard_map/all_to_all | solution.py:346
  10.8 0.1 and_select_fusion
  10.9 0.1 mul.47
  11.0 0.0 copy-done.10
  11.0 0.7 %constant_dynamic-update-slice_fusion.4 = (bf16[256,1024]{1,0:T(8,128)(2,1)S(1)}, bf16[128,1024]{1,0:T(8,128)(2,1)}) fusion(bf16[64,1024]{1,0:T(8,128)(2,1)S(1)} %copy-done.10), kind=kLoop, calls=%fused_computation.29 | loop fusion | bytes 393216
  11.7 0.0 collective-permute-done
  11.7 0.7 %constant_dynamic-update-slice_fusion.3 = (bf16[256,1024]{1,0:T(8,128)(2,1)S(1)}, bf16[128,1024]{1,0:T(8,128)(2,1)}) fusion(bf16[256,1024]{1,0:T(8,128)(2,1)S(1)} %get-tuple-element.30, bf16[64,1024]{1,0:T(8,128)(2,1)S(1)} %collective-permute-done, bf16[128,1024]{1,0:T(8,128)(2,1)} %get-tuple-element.31), kind=kLoop, calls=%fused_computation.28 | loop fusion | bytes 393216
  12.3 1.9 %collective-permute-start.1 = (bf16[128,1024]{1,0:T(8,128)(2,1)}, bf16[128,1024]{1,0:T(8,128)(2,1)}, u32[]{:S(2)}, u32[]{:S(2)}) collective-permute-start(bf16[128,1024]{1,0:T(8,128)(2,1)} %get-tuple-element.29), channel_id=1, source_target_pairs={{0,2},{1,3},{2,0},{3,1},{4,6},{5,7},{6,4},{7,5},{8,10},{9,11},{10,... | collective-permute-start | bytes 786440 | tf_op jit(solution)/shard_map/ppermute | solution.py:342
  14.3 0.4 fusion.7
  14.7 0.0 copy-done.12
  14.7 0.0 copy-done.11
  14.7 0.6 pad.13.w_sdf_ref
  15.4 0.1 pad_add_fusion.place_ref
  15.5 0.0 copy-done.6
  15.5 1.6 %point_norms.1.normed_ref = bf16[1024,1024]{1,0:T(8,128)(2,1)S(1)} custom-call(bf16[64,1024]{1,0:T(8,128)(2,1)S(1)} %fusion.4.features_ref, bf16[64,1024]{1,0:T(8,128)(2,1)S(1)} %pad.12.w_embed_ref, f32[1,1024]{1,0:T(1,128)S(1)} %bitcast.17), custom_call_target="tpu_custom_call" | custom-call | flops 1024 | bytes 1024 | tf_op jit(solution)/shard_map/point_norms/pallas_call | solution.py:191
  17.1 0.0 copy-start.1
  17.1 1.3 %copy-done.1 = bf16[1024,1024]{1,0:T(8,128)(2,1)} copy-done((bf16[1024,1024]{1,0:T(8,128)(2,1)}, bf16[1024,1024]{1,0:T(8,128)(2,1)S(1)}, u32[]{:S(2)}) %copy-start.1) | copy-done | bytes 2097176
  18.4 0.0 copy-start.4
  18.4 5.5 %point_queries.1.queries_ref = bf16[1024,1024]{1,0:T(8,128)(2,1)} custom-call(bf16[1024,1024]{1,0:T(8,128)(2,1)} %copy-done.1, bf16[1024,1024]{1,0:T(8,128)(2,1)} %w_query_ref.1), custom_call_target="tpu_custom_call" | custom-call | flops 1024 | bytes 1024 | tf_op jit(solution)/shard_map/point_queries/pallas_call | solution.py:206
  23.9 0.9 %collective-permute-done.1 = bf16[128,1024]{1,0:T(8,128)(2,1)} collective-permute-done((bf16[128,1024]{1,0:T(8,128)(2,1)}, bf16[128,1024]{1,0:T(8,128)(2,1)}, u32[]{:S(2)}, u32[]{:S(2)}) %collective-permute-start.1) | collective-permute-done | bytes 262176 | tf_op jit(solution)/shard_map/ppermute | solution.py:342
  24.8 1.0 %constant_dynamic-update-slice_fusion.2.out_0_ref = bf16[256,1024]{1,0:T(8,128)(2,1)S(1)} fusion(bf16[256,1024]{1,0:T(8,128)(2,1)S(1)} %get-tuple-element.28, bf16[128,1024]{1,0:T(8,128)(2,1)} %collective-permute-done.1), kind=kLoop, calls=%fused_computation.27 | loop fusion | bytes 524288 | tf_op jit(solution)/shard_map/concatenate | solution.py:370
  25.8 0.0 copy-start.7
  25.8 2.5 %collective-permute-start.7 = (bf16[256,1024]{1,0:T(8,128)(2,1)S(1)}, bf16[256,1024]{1,0:T(8,128)(2,1)}, u32[]{:S(2)}, u32[]{:S(2)}) collective-permute-start(bf16[256,1024]{1,0:T(8,128)(2,1)S(1)} %constant_dynamic-update-slice_fusion.2.out_0_ref), channel_id=1, source_target_pairs={{0,4},{1,5},{2,6},{3,7},{4,0},{5,1},{6,2},{7,3},{8,12},{9,13},{10,... | collective-permute-start | bytes 1572872 | tf_op jit(solution)/shard_map/ppermute | solution.py:342
  28.4 0.0 all-to-all-done.received_ref
  28.4 0.0 copy-start.2
  28.4 0.0 copy-start.3
  28.4 0.0 copy-start
  28.4 0.0 copy-start.5
  28.5 0.0 copy-start.8
  28.5 0.0 copy-start.9
  28.5 0.1 collective-permute-start.2
  28.6 1.5 %collective-permute-done.2.other_ref = bf16[256,512]{1,0:T(8,128)(2,1)S(1)} collective-permute-done((bf16[256,512]{1,0:T(8,128)(2,1)S(1)}, bf16[256,512]{1,0:T(8,128)(2,1)S(1)}, u32[]{:S(2)}, u32[]{:S(2)}) %collective-permute-start.2) | collective-permute-done | bytes 262176 | tf_op jit(solution)/shard_map/ppermute | solution.py:342
  30.1 0.0 copy-done.7
  30.1 1.6 %self_attention.1 = bf16[64,256]{1,0:T(8,128)(2,1)S(1)} custom-call(s32[2]{0:T(128)S(1)} %pad_add_fusion.place_ref, bf16[16,160,128]{2,1,0:T(8,128)(2,1)S(1)} %all-to-all-done.received_ref, bf16[256,512]{1,0:T(8,128)(2,1)S(1)} %unpack.1.own_ref, bf16[256,512]{1,0:T(8,128)(2,1)S(1)} %collective-permute-done.2.other_ref, f32[1,1024]{1,0:T(1,128)S(1)} %bitcast.18), custom_call_target="tpu_custom_call" | custom-call | tf_op jit(solution)/shard_map/self_attention/pallas_call | solution.py:243
  31.7 0.6 collective-permute-start.3
  32.3 3.4 %collective-permute-done.3 = bf16[64,256]{1,0:T(8,128)(2,1)S(1)} collective-permute-done((bf16[64,256]{1,0:T(8,128)(2,1)S(1)}, bf16[64,256]{1,0:T(8,128)(2,1)S(1)}, u32[]{:S(2)}, u32[]{:S(2)}) %collective-permute-start.3) | collective-permute-done | bytes 32800 | tf_op jit(solution)/shard_map/ppermute | solution.py:342
  35.6 3.0 %collective-permute-start.4 = (bf16[128,256]{1,0:T(8,128)(2,1)S(1)}, bf16[128,256]{1,0:T(8,128)(2,1)S(1)}, u32[]{:S(2)}, u32[]{:S(2)}) collective-permute-start(bf16[128,256]{1,0:T(8,128)(2,1)S(1)} %pad_maximum_fusion.2), channel_id=1, source_target_pairs={{0,8},{1,9},{2,10},{3,11},{4,12},{5,13},{6,14},{7,15},{8,0},{9,1},... | collective-permute-start | bytes 196616 | tf_op jit(solution)/shard_map/ppermute | solution.py:342
  38.6 2.8 %collective-permute-done.7.out_1_ref = bf16[256,1024]{1,0:T(8,128)(2,1)} collective-permute-done((bf16[256,1024]{1,0:T(8,128)(2,1)S(1)}, bf16[256,1024]{1,0:T(8,128)(2,1)}, u32[]{:S(2)}, u32[]{:S(2)}) %collective-permute-start.7) | collective-permute-done | bytes 524320 | tf_op jit(solution)/shard_map/ppermute | solution.py:342
  41.5 0.0 collective-permute-start.9
  41.5 0.5 collective-permute-start.8
  42.0 0.0 collective-permute-done.4
  42.0 2.2 %collective-permute-start.5 = (bf16[256,256]{1,0:T(8,128)(2,1)S(1)}, bf16[256,256]{1,0:T(8,128)(2,1)S(1)}, u32[]{:S(2)}, u32[]{:S(2)}) collective-permute-start(bf16[256,256]{1,0:T(8,128)(2,1)S(1)} %pad_maximum_fusion.1), channel_id=1, source_target_pairs={{0,4},{1,5},{2,6},{3,7},{4,0},{5,1},{6,2},{7,3},{8,12},{9,13},{10,... | collective-permute-start | bytes 393224 | tf_op jit(solution)/shard_map/ppermute | solution.py:342
  44.2 3.3 %collective-permute-done.5 = bf16[256,256]{1,0:T(8,128)(2,1)S(1)} collective-permute-done((bf16[256,256]{1,0:T(8,128)(2,1)S(1)}, bf16[256,256]{1,0:T(8,128)(2,1)S(1)}, u32[]{:S(2)}, u32[]{:S(2)}) %collective-permute-start.5) | collective-permute-done | bytes 131104 | tf_op jit(solution)/shard_map/ppermute | solution.py:342
  47.5 0.1 collective-permute-start.6
  47.6 0.0 collective-permute-done.9.out_3_ref
  47.6 0.0 collective-permute-done.8.out_2_ref
  47.6 1.5 %collective-permute-done.6.far_ref = bf16[512,256]{1,0:T(8,128)(2,1)S(1)} collective-permute-done((bf16[512,256]{1,0:T(8,128)(2,1)S(1)}, bf16[512,256]{1,0:T(8,128)(2,1)S(1)}, u32[]{:S(2)}, u32[]{:S(2)}) %collective-permute-start.6) | collective-permute-done | bytes 262176 | tf_op jit(solution)/shard_map/ppermute | solution.py:342
  49.1 0.0 copy-done.4
  49.1 0.0 copy-done.2
  49.1 0.0 copy-done.3
  49.1 0.0 copy-done
  49.1 0.0 copy-done.5
  49.1 0.0 copy-done.8
  49.1 0.0 copy-done.9
  49.2 15.1 %tail.1 = (bf16[16,1024]{1,0:T(8,128)(2,1)}, f32[1,1024]{1,0:T(1,128)}) custom-call(s32[2]{0:T(128)S(1)} %pad_add_fusion.place_ref, bf16[512,256]{1,0:T(8,128)(2,1)S(1)} %pad_maximum_fusion.near_ref, bf16[512,256]{1,0:T(8,128)(2,1)S(1)} %collective-permute-done.6.far_ref, bf16[256,1024]{1,0:T(8,128)(2,1)S(1)} %constant_dynamic-update-slice_fusion.2.out_0_ref, ...), custom_call_target="tpu_custom_call" | custom-call | tf_op jit(solution)/shard_map/tail/pallas_call | solution.py:317
  (11 shorter events, 0.2 us)
Async XLA Ops:
  0.6 10.3 %copy-start.10 = (bf16[64,1024]{1,0:T(8,128)(2,1)S(1)}, bf16[64,1024]{1,0:T(8,128)(2,1)}, u32[]{:S(2)}) copy-start(bf16[64,1024]{1,0:T(8,128)(2,1)} %param.16) | copy-start | bytes 393220
  0.6 14.0 %copy-start.12 = (bf16[1024]{0:T(1024)(128)(2,1)S(1)}, bf16[1024]{0:T(1024)(128)(2,1)}, u32[]{:S(2)}) copy-start(bf16[1024]{0:T(1024)(128)(2,1)} %param.25) | copy-start | bytes 6148
  0.7 14.1 %copy-start.11 = (bf16[51,1024]{1,0:T(8,128)(2,1)S(1)}, bf16[51,1024]{1,0:T(8,128)(2,1)}, u32[]{:S(2)}) copy-start(bf16[51,1024]{1,0:T(8,128)(2,1)} %param.19) | copy-start | bytes 313348
  0.7 14.8 %copy-start.6 = (f32[1024]{0:T(1024)S(1)}, f32[1024]{0:T(1024)}, u32[]{:S(2)}) copy-start(f32[1024]{0:T(1024)} %param.20) | copy-start | bytes 12292
  0.7 11.0 %collective-permute-start = (bf16[64,1024]{1,0:T(8,128)(2,1)}, bf16[64,1024]{1,0:T(8,128)(2,1)S(1)}, u32[]{:S(2)}, u32[]{:S(2)}) collective-permute-start(bf16[64,1024]{1,0:T(8,128)(2,1)} %param.16), channel_id=1, source_target_pairs={{0,8},{1,9},{2,10},{3,11},{4,12},{5,13},{6,14},{7,15},{8,0},{9,1},... | collective-permute-start | bytes 393224 | tf_op jit(solution)/shard_map/ppermute | solution.py:342
  6.8 21.6 %all-to-all-start = ((bf16[16,160,128]{2,1,0:T(8,128)(2,1)}), bf16[16,160,128]{2,1,0:T(8,128)(2,1)S(1)}, u32[]{:S(2)}, u32[]{:S(2)}) async-start(bf16[16,160,128]{2,1,0:T(8,128)(2,1)} %pack.1), calls=%async_computation | async-start | bytes 1310720 | tf_op jit(solution)/shard_map/all_to_all | solution.py:346
  12.3 12.5 %collective-permute-start.1 = (bf16[128,1024]{1,0:T(8,128)(2,1)}, bf16[128,1024]{1,0:T(8,128)(2,1)}, u32[]{:S(2)}, u32[]{:S(2)}) collective-permute-start(bf16[128,1024]{1,0:T(8,128)(2,1)} %get-tuple-element.29), channel_id=1, source_target_pairs={{0,2},{1,3},{2,0},{3,1},{4,6},{5,7},{6,4},{7,5},{8,10},{9,11},{10,... | collective-permute-start | bytes 786440 | tf_op jit(solution)/shard_map/ppermute | solution.py:342
  17.1 1.3 %copy-start.1 = (bf16[1024,1024]{1,0:T(8,128)(2,1)}, bf16[1024,1024]{1,0:T(8,128)(2,1)S(1)}, u32[]{:S(2)}) copy-start(bf16[1024,1024]{1,0:T(8,128)(2,1)S(1)} %point_norms.1.normed_ref) | copy-start | bytes 6291460
  18.4 30.7 %copy-start.4 = (bf16[1024,1024]{1,0:T(8,128)(2,1)S(1)}, bf16[1024,1024]{1,0:T(8,128)(2,1)}, u32[]{:S(2)}) copy-start(bf16[1024,1024]{1,0:T(8,128)(2,1)} %w_hidden_ref.1) | copy-start | bytes 6291460
  25.8 4.3 %copy-start.7 = (f32[1024]{0:T(1024)S(1)}, f32[1024]{0:T(1024)}, u32[]{:S(2)}) copy-start(f32[1024]{0:T(1024)} %param.14) | copy-start | bytes 12292
  25.8 15.7 %collective-permute-start.7 = (bf16[256,1024]{1,0:T(8,128)(2,1)S(1)}, bf16[256,1024]{1,0:T(8,128)(2,1)}, u32[]{:S(2)}, u32[]{:S(2)}) collective-permute-start(bf16[256,1024]{1,0:T(8,128)(2,1)S(1)} %constant_dynamic-update-slice_fusion.2.out_0_ref), channel_id=1, source_target_pairs={{0,4},{1,5},{2,6},{3,7},{4,0},{5,1},{6,2},{7,3},{8,12},{9,13},{10,... | collective-permute-start | bytes 1572872 | tf_op jit(solution)/shard_map/ppermute | solution.py:342
  28.4 20.7 %copy-start.2 = (bf16[2,1024,1024]{2,1,0:T(8,128)(2,1)S(1)}, bf16[2,1024,1024]{2,1,0:T(8,128)(2,1)}, u32[]{:S(2)}) copy-start(bf16[2,1024,1024]{2,1,0:T(8,128)(2,1)} %w_kv_ref.1) | copy-start | bytes 12582916
  28.4 20.7 %copy-start.3 = (bf16[1024,1024]{1,0:T(8,128)(2,1)S(1)}, bf16[1024,1024]{1,0:T(8,128)(2,1)}, u32[]{:S(2)}) copy-start(bf16[1024,1024]{1,0:T(8,128)(2,1)} %w_back_ref.1) | copy-start | bytes 6291460
  28.4 20.7 %copy-start = (bf16[1024,1024]{1,0:T(8,128)(2,1)S(1)}, bf16[1024,1024]{1,0:T(8,128)(2,1)}, u32[]{:S(2)}) copy-start(bf16[1024,1024]{1,0:T(8,128)(2,1)} %point_queries.1.queries_ref) | copy-start | bytes 6291460
  28.4 20.7 %copy-start.5 = (bf16[16,1024]{1,0:T(8,128)(2,1)S(1)}, bf16[16,1024]{1,0:T(8,128)(2,1)}, u32[]{:S(2)}) copy-start(bf16[16,1024]{1,0:T(8,128)(2,1)} %pad.13.w_sdf_ref) | copy-start | bytes 98308
  28.5 20.7 %copy-start.8 = (f32[1024]{0:T(1024)S(1)}, f32[1024]{0:T(1024)}, u32[]{:S(2)}) copy-start(f32[1024]{0:T(1024)} %param.17) | copy-start | bytes 12292
  28.5 20.7 %copy-start.9 = (f32[1024]{0:T(1024)S(1)}, f32[1024]{0:T(1024)}, u32[]{:S(2)}) copy-start(f32[1024]{0:T(1024)} %param.23) | copy-start | bytes 12292
  28.5 1.6 %collective-permute-start.2 = (bf16[256,512]{1,0:T(8,128)(2,1)S(1)}, bf16[256,512]{1,0:T(8,128)(2,1)S(1)}, u32[]{:S(2)}, u32[]{:S(2)}) collective-permute-start(bf16[256,512]{1,0:T(8,128)(2,1)S(1)} %unpack.1.own_ref), channel_id=1, source_target_pairs={{0,1},{1,0},{2,3},{3,2},{4,5},{5,4},{6,7},{7,6},{8,9},{9,8},{10,11... | collective-permute-start | bytes 786440 | tf_op jit(solution)/shard_map/ppermute | solution.py:342
  31.7 4.0 %collective-permute-start.3 = (bf16[64,256]{1,0:T(8,128)(2,1)S(1)}, bf16[64,256]{1,0:T(8,128)(2,1)S(1)}, u32[]{:S(2)}, u32[]{:S(2)}) collective-permute-start(bf16[64,256]{1,0:T(8,128)(2,1)S(1)} %self_attention.1), channel_id=1, source_target_pairs={{0,2},{1,3},{2,0},{3,1},{4,6},{5,7},{6,4},{7,5},{8,10},{9,11},{10,... | collective-permute-start | bytes 98312 | tf_op jit(solution)/shard_map/ppermute | solution.py:342
  35.6 6.4 %collective-permute-start.4 = (bf16[128,256]{1,0:T(8,128)(2,1)S(1)}, bf16[128,256]{1,0:T(8,128)(2,1)S(1)}, u32[]{:S(2)}, u32[]{:S(2)}) collective-permute-start(bf16[128,256]{1,0:T(8,128)(2,1)S(1)} %pad_maximum_fusion.2), channel_id=1, source_target_pairs={{0,8},{1,9},{2,10},{3,11},{4,12},{5,13},{6,14},{7,15},{8,0},{9,1},... | collective-permute-start | bytes 196616 | tf_op jit(solution)/shard_map/ppermute | solution.py:342
  41.5 6.1 %collective-permute-start.9 = (bf16[256,1024]{1,0:T(8,128)(2,1)}, bf16[256,1024]{1,0:T(8,128)(2,1)S(1)}, u32[]{:S(2)}, u32[]{:S(2)}) collective-permute-start(bf16[256,1024]{1,0:T(8,128)(2,1)} %collective-permute-done.7.out_1_ref), channel_id=1, source_target_pairs={{0,1},{1,0},{2,3},{3,2},{4,5},{5,4},{6,7},{7,6},{8,9},{9,8},{10,11... | collective-permute-start | bytes 1572872 | tf_op jit(solution)/shard_map/ppermute | solution.py:342
  41.5 6.1 %collective-permute-start.8 = (bf16[256,1024]{1,0:T(8,128)(2,1)S(1)}, bf16[256,1024]{1,0:T(8,128)(2,1)S(1)}, u32[]{:S(2)}, u32[]{:S(2)}) collective-permute-start(bf16[256,1024]{1,0:T(8,128)(2,1)S(1)} %constant_dynamic-update-slice_fusion.2.out_0_ref), channel_id=1, source_target_pairs={{0,1},{1,0},{2,3},{3,2},{4,5},{5,4},{6,7},{7,6},{8,9},{9,8},{10,11... | collective-permute-start | bytes 1572872 | tf_op jit(solution)/shard_map/ppermute | solution.py:342
  42.0 5.5 %collective-permute-start.5 = (bf16[256,256]{1,0:T(8,128)(2,1)S(1)}, bf16[256,256]{1,0:T(8,128)(2,1)S(1)}, u32[]{:S(2)}, u32[]{:S(2)}) collective-permute-start(bf16[256,256]{1,0:T(8,128)(2,1)S(1)} %pad_maximum_fusion.1), channel_id=1, source_target_pairs={{0,4},{1,5},{2,6},{3,7},{4,0},{5,1},{6,2},{7,3},{8,12},{9,13},{10,... | collective-permute-start | bytes 393224 | tf_op jit(solution)/shard_map/ppermute | solution.py:342
  47.5 1.6 %collective-permute-start.6 = (bf16[512,256]{1,0:T(8,128)(2,1)S(1)}, bf16[512,256]{1,0:T(8,128)(2,1)S(1)}, u32[]{:S(2)}, u32[]{:S(2)}) collective-permute-start(bf16[512,256]{1,0:T(8,128)(2,1)S(1)} %pad_maximum_fusion.near_ref), channel_id=1, source_target_pairs={{0,1},{1,0},{2,3},{3,2},{4,5},{5,4},{6,7},{7,6},{8,9},{9,8},{10,11... | collective-permute-start | bytes 786440 | tf_op jit(solution)/shard_map/ppermute | solution.py:342
